TPU v7x, 32 devices: a whole 2x2x4 slice. The times are simulated.
32 devices in a mesh: rows: 8 (over z, x), blk: 4 (over y, core).
Axes of the slice: x: 2, y: 2, z: 4, core: 2. Of those that a mesh axis runs over, the one named last changes fastest.
Arguments:
- inputs: bfloat16 [32, 1152, 768], P('rows', 'blk'), may hold values from -6 to 6
- image_index: int32 [32, 1152], P('rows', 'blk'), may hold values from -1 to 3, as said below
- keep_mask: int32 [32, 2], P('rows'), may hold values 0 or 1
- first_gain: float32 [768], replicated, may hold values from 0.5 to 1.5
- first_shift: float32 [768], replicated, may hold values from -2.5 to 2.5
- input_weight: bfloat16 [768, 2304], replicated, may hold values from -0.21875 to 0.21875
- input_bias: float32 [2, 768], replicated, may hold values from -2.5 to 2.5
- output_weight: bfloat16 [768, 768], replicated, may hold values from -3.5 to 3.5
- output_bias: float32 [768], replicated, may hold values from -2.5 to 2.5
- second_gain: float32 [768], replicated, may hold values from 0.5 to 1.5
- second_shift: float32 [768], replicated, may hold values from -2.5 to 2.5
- up_weight: bfloat16 [768, 3072], replicated, may hold values from -0.21875 to 0.21875
- up_bias: float32 [3072], replicated, may hold values from -2.5 to 2.5
- down_weight: bfloat16 [3072, 768], replicated, may hold values from -0.109375 to 0.109375
- down_bias: float32 [768], replicated, may hold values from -2.5 to 2.5
- cotangent: bfloat16 [32, 1152, 768], P('rows', 'blk'), may hold values from -6 to 6
Outputs:
- result: bfloat16 [32, 1152, 768], P('rows', 'blk')
- inputs_gradient: bfloat16 [32, 1152, 768], P('rows', 'blk')
- first_gain_gradient: float32 [768], replicated
- first_shift_gradient: float32 [768], replicated
- input_weight_gradient: float32 [768, 2304], replicated
- input_bias_gradient: float32 [2, 768], replicated
- output_weight_gradient: float32 [768, 768], replicated
- output_bias_gradient: float32 [768], replicated
- second_gain_gradient: float32 [768], replicated
- second_shift_gradient: float32 [768], replicated
- up_weight_gradient: float32 [768, 3072], replicated
- up_bias_gradient: float32 [3072], replicated
- down_weight_gradient: float32 [3072, 768], replicated
- down_bias_gradient: float32 [768], replicated
Inputs may be any that keep to these rules, and one draw needn't show every extreme that they name: `image_index`: in each row, images 0 to 3 each hold 194 to 282 slots, the rest of the row is padding (-1); every image and the padding of every row have slots on every device of blk.
All inputs are finite; a program needn't handle non-finite values. No bound on the sum of `keep_mask` on one device may be relied on, other than what follows from the above.
Results may differ from a plain program's by a relative error of at most 0.015.
Values may be sent and summed in bfloat16 or wider, within the bound.
No kernel may reach another device: no remote copies, remote signals or barrier semaphores. Data moves between devices by JAX's collectives and lax.ppermute only.
A program may use at most 448 MiB of HBM per device.

v0:
```python
import functools

import jax
import jax.numpy as jnp
from jax import lax
from jax.experimental import pallas as pl
from jax.experimental.pallas import tpu as pltpu
from jax.sharding import PartitionSpec as P

HEADS = 12
HEAD_DIM = 64
PAIR = 2 * HEAD_DIM
PAIRS = HEADS // 2
eps_norm = 1e-06
keep_rate = 0.9
F32 = jnp.float32
BF16 = jnp.bfloat16
NEG = -1e30
VMEM = 62 * 1024 * 1024
QUICK = pl.CostEstimate(flops=1 << 20, bytes_accessed=1 << 16, transcendentals=0)


def dot(a, b):
    return jnp.dot(a, b, preferred_element_type=F32)


def dot_nt(a, b):
    return lax.dot_general(a, b, (((1,), (1,)), ((), ())), preferred_element_type=F32)


def dot_tn(a, b):
    return lax.dot_general(a, b, (((0,), (0,)), ((), ())), preferred_element_type=F32)


def whole(shape):
    return pl.BlockSpec(shape, lambda *g: (0,) * len(shape), pipeline_mode=pl.Buffered(1))


def centre_scale(values):
    centre = values - jnp.mean(values, axis=-1, keepdims=True)
    spread = jnp.mean(centre * centre, axis=-1, keepdims=True)
    inv = lax.rsqrt(spread + eps_norm)
    return centre * inv, inv


def norm_back(grad_hat, hat, inv):
    first = jnp.mean(grad_hat, axis=-1, keepdims=True)
    second = jnp.mean(grad_hat * hat, axis=-1, keepdims=True)
    return (grad_hat - first - hat * second) * inv


def gather_pieces(step, pieces, row):
    @pl.when(step == 0)
    def _():
        span = pieces[0].shape[0]
        for i, piece in enumerate(pieces):
            row[i * span : (i + 1) * span, :] = piece[...]


def sort_tile(rank_row, tile, step, row):
    place = step * tile + lax.broadcasted_iota(jnp.int32, (tile, row.shape[0]), 0)
    return dot((rank_row == place).astype(BF16), row[...])


def qkv_kernel(n, tile, *refs):
    rank, *pieces = refs[: n + 1]
    gain, shift, weight, bias, xs_out, normed_out, qkv_out, row = refs[n + 1 :]
    gather_pieces(pl.program_id(0), pieces, row)
    xs = sort_tile(rank[...], tile, pl.program_id(0), row)
    xs_out[...] = xs.astype(BF16)
    hat, _ = centre_scale(xs)
    normed = (hat * gain[...] + shift[...]).astype(BF16)
    normed_out[...] = normed
    width = normed.shape[1]
    for j in range(3):
        cols = slice(j * width, (j + 1) * width)
        mixed = (dot(normed, weight[:, cols]) + bias[j : j + 1, :]).astype(BF16)
        qkv_out[j] = mixed * BF16(HEAD_DIM**-0.5) if j == 0 else mixed


def qkv_call(rank, pieces, gain, shift, weight, bias, tile=288):
    n = len(pieces)
    span, width = pieces[0].shape
    count = n * span
    return pl.pallas_call(
        functools.partial(qkv_kernel, n, tile),
        grid=(count // tile,),
        in_specs=[whole((1, count))]
        + [whole((span, width))] * n
        + [whole((1, width)), whole((1, width)), whole(weight.shape), whole(bias.shape)],
        out_specs=[
            pl.BlockSpec((tile, width), lambda i: (i, 0)),
            pl.BlockSpec((tile, width), lambda i: (i, 0)),
            pl.BlockSpec((3, tile, width), lambda i: (0, i, 0)),
        ],
        out_shape=[
            jax.ShapeDtypeStruct((count, width), BF16),
            jax.ShapeDtypeStruct((count, width), BF16),
            jax.ShapeDtypeStruct((3, count, width), BF16),
        ],
        scratch_shapes=[pltpu.VMEM((count, width), BF16)],
        compiler_params=pltpu.CompilerParams(vmem_limit_bytes=VMEM),
        cost_estimate=QUICK,
        name="sort_qkv",
    )(rank, *pieces, gain, shift, weight, bias)


SMALL = 304
LARGE = 384


def windows(starts, seg, length):
    first, last = starts[seg], starts[seg + 1]
    aligned = first // 16 * 16
    small = SMALL if seg < 4 else LARGE
    at_small = pl.multiple_of(jnp.minimum(aligned, length - small), 16)
    at_large = pl.multiple_of(jnp.minimum(aligned, length - LARGE), 16)
    return first, last, small, at_small, at_large


def inside(at, size, lanes, first, last):
    place = at + lax.broadcasted_iota(jnp.int32, (size, lanes), 0)
    return (place >= first) & (place < last)


def forward_kernel(starts, qkv, out, stat):
    length = qkv.shape[1]
    for seg in range(5):
        first, last, small, at_q, at_k = windows(starts, seg, length)
        rows_q = pl.ds(at_q, small)
        q = qkv[0, rows_q, :]
        k = qkv[1, pl.ds(at_k, LARGE), :]
        v = qkv[2, pl.ds(at_k, LARGE), :]
        lane = lax.broadcasted_iota(jnp.int32, (LARGE, PAIR), 1)
        lane_q = lax.broadcasted_iota(jnp.int32, (small, PAIR), 1)
        low = lane < HEAD_DIM
        seen = inside(at_k, LARGE, PAIR, first, last)
        zero = jnp.zeros((LARGE, PAIR), BF16)
        one = jnp.ones((LARGE, PAIR), BF16)
        bias = jnp.where((lane == 0) & ~seen, NEG, 0.0).astype(BF16)
        q_ext = jnp.concatenate([q, (lane_q == 0).astype(BF16)], axis=1)
        halves = (low, ~low)
        k_ext = [jnp.concatenate([jnp.where(half, k, zero), bias], axis=1) for half in halves]
        mixes = [
            jnp.concatenate([jnp.where(half, v, zero), jnp.where(half, one, zero)], axis=1) for half in halves
        ]
        pair = dot_nt(q_ext, jnp.concatenate(k_ext, axis=0))
        tops, weights = [], []
        for h in range(2):
            scores = pair[:, h * LARGE : (h + 1) * LARGE]
            top = jnp.max(scores, axis=-1, keepdims=True)
            tops.append(top)
            weights.append(jnp.exp(scores - top).astype(BF16))
        both = dot(jnp.concatenate(weights, axis=1), jnp.concatenate(mixes, axis=0))
        total = both[:, PAIR:]
        peak = jnp.where(lane_q < HEAD_DIM, tops[0], tops[1])
        mine = inside(at_q, small, PAIR, first, last)
        out[rows_q, :] = jnp.where(mine, both[:, :PAIR] / total, out[rows_q, :])
        stat[rows_q, :] = jnp.where(mine, peak + jnp.log(total), stat[rows_q, :])


def forward_call(starts, qkv):
    _, count, wide = qkv.shape
    pairs = wide // PAIR
    return pl.pallas_call(
        forward_kernel,
        grid_spec=pltpu.PrefetchScalarGridSpec(
            num_scalar_prefetch=1,
            grid=(pairs,),
            in_specs=[pl.BlockSpec((3, count, PAIR), lambda p, s: (0, 0, p))],
            out_specs=[
                pl.BlockSpec((count, PAIR), lambda p, s: (0, p)),
                pl.BlockSpec((count, PAIR), lambda p, s: (0, p)),
            ],
        ),
        out_shape=[jax.ShapeDtypeStruct((count, pairs * PAIR), F32)] * 2,
        compiler_params=pltpu.CompilerParams(vmem_limit_bytes=VMEM),
        cost_estimate=QUICK,
        name="attention_forward",
    )(starts, qkv)


def split3(value):
    high = value.astype(BF16)
    rest = value - high.astype(F32)
    mid = rest.astype(BF16)
    return high, mid, (rest - mid.astype(F32)).astype(BF16)


def backward_kernel(starts, qkv, grad, att, stat, *refs):
    out, sums = refs[-2:]
    length = qkv.shape[1]
    third = lax.broadcasted_iota(jnp.int32, (PAIR, PAIR), 0) // HEAD_DIM
    block = (third == lax.broadcasted_iota(jnp.int32, (PAIR, PAIR), 1) // HEAD_DIM).astype(BF16)
    for seg in range(5):
        first, last, small, at_k, at_q = windows(starts, seg, length)
        rows_q, rows_k = pl.ds(at_q, LARGE), pl.ds(at_k, small)
        lane_q = lax.broadcasted_iota(jnp.int32, (LARGE, PAIR), 1)
        lane_k = lax.broadcasted_iota(jnp.int32, (small, PAIR), 1)
        spot_q, spot_k = lane_q % HEAD_DIM, lane_k % HEAD_DIM
        mine_q = inside(at_q, LARGE, PAIR, first, last)
        mine_k = inside(at_k, small, PAIR, first, last)
        zero_q = jnp.zeros((LARGE, PAIR), BF16)
        zero_k = jnp.zeros((small, PAIR), BF16)
        q = qkv[0, rows_q, :]
        k = jnp.where(mine_k, qkv[1, rows_k, :], zero_k)
        v = qkv[2, rows_k, :]
        g = jnp.where(mine_q, grad[rows_q, :], zero_q)
        prod = g.astype(F32) * jnp.where(mine_q, att[rows_q, :], 0.0)
        p_high = prod.astype(BF16)
        p_low = (prod - p_high.astype(F32)).astype(BF16)
        inner = dot(p_high, block) + dot(p_low, block)
        logs = jnp.where(mine_q, stat[rows_q, :], 0.0)

        def spread(value, fifth):
            a, b, c = split3(value)
            return jnp.where(
                spot_q == 0, a, jnp.where(spot_q == 1, b, jnp.where(spot_q == 2, c, fifth))
            )

        query_bias = jnp.where(mine_q, 0.0, NEG).astype(BF16)
        unit = jnp.ones((LARGE, PAIR), BF16)
        q_tail = spread(logs, jnp.where(spot_q == 3, unit, jnp.where(spot_q == 4, query_bias, zero_q)))
        g_tail = spread(inner, zero_q)
        key_bias = jnp.where(mine_k, 0.0, NEG).astype(BF16)
        minus = jnp.where(spot_k < 3, -1.0, 0.0).astype(BF16)
        k_tail = jnp.where(
            spot_k == 3, key_bias, jnp.where(spot_k == 4, jnp.ones((small, PAIR), BF16), minus)
        )
        heads_q = [lane_q // HEAD_DIM == h for h in range(2)]
        qs = [jnp.where(head, q, zero_q) for head in heads_q]
        gs = [jnp.where(head, g, zero_q) for head in heads_q]
        q_both = [jnp.concatenate([x, jnp.where(head, q_tail, zero_q)], axis=1) for x, head in zip(qs, heads_q)]
        g_both = [jnp.concatenate([x, jnp.where(head, g_tail, zero_q)], axis=1) for x, head in zip(gs, heads_q)]
        prob = jnp.exp(dot_nt(jnp.concatenate([k, k_tail], axis=1), jnp.concatenate(q_both, axis=0)))
        prob_grad = dot_nt(jnp.concatenate([v, minus], axis=1), jnp.concatenate(g_both, axis=0))
        score_grad = (prob * prob_grad).astype(BF16)
        value_grad = dot(prob.astype(BF16), jnp.concatenate(gs, axis=0))
        key_grad = dot(score_grad, jnp.concatenate(qs, axis=0))
        stacked = jnp.concatenate([score_grad[:, :LARGE], score_grad[:, LARGE:]], axis=0)
        ks = [jnp.where(lane_k // HEAD_DIM == h, k, zero_k) for h in range(2)]
        query_grad = dot_tn(stacked, jnp.concatenate(ks, axis=0))
        query_grad = (query_grad * HEAD_DIM**-0.5).astype(BF16)
        out[0, rows_q, :] = jnp.where(mine_q, query_grad, out[0, rows_q, :])
        out[1, rows_k, :] = jnp.where(mine_k, key_grad.astype(BF16), out[1, rows_k, :])
        out[2, rows_k, :] = jnp.where(mine_k, value_grad.astype(BF16), out[2, rows_k, :])
    for j in range(3):
        sums[j : j + 1, :] = jnp.sum(out[j].astype(F32), axis=0, keepdims=True)


def backward_call(starts, qkv, grad, att, stat, first_pair, pairs, before=None):
    _, count, width = qkv.shape
    held = [] if before is None else list(before)
    return pl.pallas_call(
        backward_kernel,
        grid_spec=pltpu.PrefetchScalarGridSpec(
            num_scalar_prefetch=1,
            grid=(pairs,),
            in_specs=[pl.BlockSpec((3, count, PAIR), lambda p, s: (0, 0, p + first_pair))]
            + [pl.BlockSpec((count, PAIR), lambda p, s: (0, p + first_pair))] * 3
            + [pl.BlockSpec(memory_space=pl.ANY)] * len(held),
            out_specs=[
                pl.BlockSpec((3, count, PAIR), lambda p, s: (0, 0, p + first_pair)),
                pl.BlockSpec((8, PAIR), lambda p, s: (0, p + first_pair)),
            ],
        ),
        out_shape=[
            jax.ShapeDtypeStruct((3, count, width), BF16),
            jax.ShapeDtypeStruct((8, width), F32),
        ],
        input_output_aliases={5: 0, 6: 1} if held else {},
        compiler_params=pltpu.CompilerParams(vmem_limit_bytes=VMEM),
        cost_estimate=QUICK,
        name="attention_backward",
    )(starts, qkv, grad, att, stat, *held)


ERF = (0.254829592, -0.284496736, 1.421413741, -1.453152027, 1.061405429)


def gelu_pair(u):
    size = jnp.abs(u)
    t = 1.0 / (1.0 + (0.3275911 * 0.5**0.5) * size)
    bell = jnp.exp(u * u * -0.5)
    poly = ERF[4] * t + ERF[3]
    for c in (ERF[2], ERF[1], ERF[0]):
        poly = poly * t + c
    tail = 0.5 * poly * t * bell
    phi = jnp.where(u < 0, tail, 1.0 - tail)
    return u * phi, phi + u * bell * 0.3989422804014327


def middle_kernel(n, tile, *refs):
    keep, rank, *pieces = refs[: n + 2]
    att, xs, out_w, vectors, cot_out, att_low_out, middle_out, normed_out, mlp_out, sums, row = refs[n + 2 :]
    step = pl.program_id(0)
    gather_pieces(step, pieces, row)
    cot = sort_tile(rank[...], tile, step, row)
    cot_out[...] = cot.astype(BF16)
    mlp_grad = (cot * keep[1]).astype(BF16)
    mlp_out[...] = mlp_grad
    att_low = att[...].astype(BF16)
    att_low_out[...] = att_low
    middle = xs[...].astype(F32) + keep[0] * (dot(att_low, out_w[...]) + vectors[0:1, :])
    middle_out[...] = middle
    hat, _ = centre_scale(middle)
    normed_out[...] = (hat * vectors[1:2, :] + vectors[2:3, :]).astype(BF16)

    @pl.when(step == 0)
    def _():
        sums[...] = jnp.zeros_like(sums)

    sums[0:1, :] += jnp.sum(mlp_grad.astype(F32), axis=0, keepdims=True)


def middle_call(keep, rank, pieces, att, xs, out_w, vectors, tile=384):
    n = len(pieces)
    span, width = pieces[0].shape
    count = n * span
    rows = pl.BlockSpec((tile, width), lambda i: (i, 0))
    low, full = jax.ShapeDtypeStruct((count, width), BF16), jax.ShapeDtypeStruct((count, width), F32)
    return pl.pallas_call(
        functools.partial(middle_kernel, n, tile),
        grid=(count // tile,),
        in_specs=[pl.BlockSpec(memory_space=pltpu.SMEM), whole((1, count))]
        + [whole((span, width))] * n
        + [rows, rows, whole(out_w.shape), whole(vectors.shape)],
        out_specs=[rows] * 5 + [pl.BlockSpec((8, width), lambda i: (0, 0))],
        out_shape=[low, low, full, low, low, jax.ShapeDtypeStruct((8, width), F32)],
        scratch_shapes=[pltpu.VMEM((count, width), BF16)],
        compiler_params=pltpu.CompilerParams(vmem_limit_bytes=VMEM),
        cost_estimate=QUICK,
        name="middle",
    )(keep, rank, *pieces, att, xs, out_w, vectors)


def mlp_kernel(parts, core, keep, normed, mlp_grad, middle, cot, att, out_w, vectors, up_w, up_b, down_w, *refs):
    (
        up_send, up_keep, down_send, down_keep, up_sums, result, middle_grad_out, branch_out, att_grad_out, sums,
        lift, back, act_all, hidden_all,
    ) = refs
    step, half = pl.program_id(0), pl.num_programs(0) // 2
    count, width = normed.shape
    cuts = [slice(i * (count // parts), (i + 1) * (count // parts)) for i in range(parts)]

    @pl.when(step == 0)
    def _():
        lift[...] = jnp.zeros_like(lift)
        back[...] = jnp.zeros_like(back)

    @pl.when(step < 2 * half)
    def _():
        total = jnp.zeros(up_sums.shape, F32)
        ready = None
        for rows in cuts + [None]:
            fresh = None
            if rows is not None:
                u = dot(normed[rows, :], up_w[...]) + up_b[...]
                fresh = (rows, u, dot_nt(mlp_grad[rows, :], down_w[...]))
            if ready is not None:
                past, u, act_grad = ready
                act, slope = gelu_pair(u)
                act_all[past, :] = act.astype(BF16)
                hidden = (act_grad * slope).astype(BF16)
                hidden_all[past, :] = hidden
                total = total + jnp.sum(hidden.astype(F32), axis=0, keepdims=True)
            ready = fresh
        lift[...] += dot(act_all[...], down_w[...])
        back[...] += dot_nt(hidden_all[...], up_w[...])
        up_sums[...] = total
        up_part = dot_tn(normed[...], hidden_all[...]).astype(BF16)
        down_part = dot_tn(act_all[...], mlp_grad[...]).astype(BF16)

        @pl.when(step < half)
        def _():
            up_send[...] = up_part
            down_send[...] = down_part

        @pl.when(step >= half)
        def _():
            up_keep[...] = up_part
            down_keep[...] = down_part

    @pl.when(step == 2 * half)
    def _():
        gain, down_b = vectors[1:2, :], vectors[3:4, :]
        sums[...] = jnp.zeros_like(sums)
        for rows in cuts:
            mid, grad = middle[rows, :], back[rows, :]
            hat, inv = centre_scale(mid)
            result[rows, :] = (mid + keep[1] * (lift[rows, :] + down_b)).astype(BF16)
            middle_grad = cot[rows, :].astype(F32) + norm_back(grad * gain, hat, inv)
            middle_grad_out[rows, :] = middle_grad
            branch = (keep[0] * middle_grad).astype(BF16)
            branch_out[rows, :] = branch
            att_grad_out[rows, :] = dot_nt(branch, out_w[...]).astype(BF16)
            sums[0:1, :] += jnp.sum(grad * hat, axis=0, keepdims=True)
            sums[1:2, :] += jnp.sum(grad, axis=0, keepdims=True)
            sums[2:3, :] += jnp.sum(branch.astype(F32), axis=0, keepdims=True)
        for out, c in ((down_send, 1 - core[0]), (down_keep, core[0])):
            cols = pl.ds(pl.multiple_of(c * (width // 2), 128), width // 2)
            out[: width // 2, :] = dot_tn(att[:, cols], branch_out[...]).astype(BF16)
            out[width // 2 :, :] = jnp.zeros((out.shape[0] - width // 2, width), BF16)


def mlp_call(core, keep, normed, mlp_grad, middle, cot, att, out_w, vectors, up_w, up_b, down_w, chunk=512, parts=4):
    count, width = normed.shape
    ff = up_w.shape[1]
    half = ff // 2 // chunk

    def place(i, c):
        i = jnp.minimum(i, 2 * half - 1)
        return jnp.where(i < half, (1 - c[0]) * half + i, c[0] * half + i - half)

    def first(i):
        return jnp.minimum(i, half - 1)

    def second(i):
        return jnp.clip(i - half, 0, half - 1)

    def extra(i, index):
        return jnp.where(i == 2 * half, half, index)

    low, full = jax.ShapeDtypeStruct((count, width), BF16), jax.ShapeDtypeStruct((count, width), F32)
    return pl.pallas_call(
        functools.partial(mlp_kernel, parts),
        grid_spec=pltpu.PrefetchScalarGridSpec(
            num_scalar_prefetch=1,
            grid=(2 * half + 1,),
            in_specs=[pl.BlockSpec(memory_space=pltpu.SMEM)]
            + [whole((count, width))] * 5
            + [
                whole(out_w.shape),
                whole(vectors.shape),
                pl.BlockSpec((width, chunk), lambda i, c: (0, place(i, c))),
                pl.BlockSpec((1, chunk), lambda i, c: (0, place(i, c))),
                pl.BlockSpec((chunk, width), lambda i, c: (place(i, c), 0)),
            ],
            out_specs=[
                pl.BlockSpec((width, chunk), lambda i, c: (0, first(i))),
                pl.BlockSpec((width, chunk), lambda i, c: (0, second(i))),
                pl.BlockSpec((chunk, width), lambda i, c: (extra(i, first(i)), 0)),
                pl.BlockSpec((chunk, width), lambda i, c: (extra(i, second(i)), 0)),
                pl.BlockSpec((1, chunk), lambda i, c: (0, place(i, c))),
            ]
            + [whole((count, width))] * 4
            + [whole((8, width))],
            scratch_shapes=[pltpu.VMEM((count, width), F32)] * 2 + [pltpu.VMEM((count, chunk), BF16)] * 2,
        ),
        out_shape=[jax.ShapeDtypeStruct((width, ff // 2), BF16)] * 2
        + [jax.ShapeDtypeStruct((ff // 2 + chunk, width), BF16)] * 2
        + [jax.ShapeDtypeStruct((1, ff), F32), low, full, low, low, jax.ShapeDtypeStruct((8, width), F32)],
        compiler_params=pltpu.CompilerParams(vmem_limit_bytes=VMEM),
        cost_estimate=QUICK,
        name="mlp",
    )(core, keep, normed, mlp_grad, middle, cot, att, out_w, vectors, up_w, up_b, down_w)


def input_kernel(grads, weight, xs, middle_grad, gain, out, sums):
    span = xs.shape[1]
    back = None
    for j in range(3):
        part = dot_nt(grads[j], weight[:, j * span : (j + 1) * span])
        back = part if back is None else back + part
    hat, inv = centre_scale(xs[...].astype(F32))
    out[...] = (middle_grad[...] + norm_back(back * gain[...], hat, inv)).astype(BF16)

    @pl.when(pl.program_id(0) == 0)
    def _():
        sums[...] = jnp.zeros_like(sums)

    sums[0:1, :] += jnp.sum(back * hat, axis=0, keepdims=True)
    sums[1:2, :] += jnp.sum(back, axis=0, keepdims=True)


def input_call(grads, weight, xs, middle_grad, gain, tile=288):
    count, width = xs.shape
    return pl.pallas_call(
        input_kernel,
        grid=(count // tile,),
        in_specs=[pl.BlockSpec((3, tile, width), lambda i: (0, i, 0))]
        + [
            whole(weight.shape),
            pl.BlockSpec((tile, width), lambda i: (i, 0)),
            pl.BlockSpec((tile, width), lambda i: (i, 0)),
            whole((1, width)),
        ],
        out_specs=[pl.BlockSpec((tile, width), lambda i: (i, 0)), pl.BlockSpec((8, width), lambda i: (0, 0))],
        out_shape=[jax.ShapeDtypeStruct((count, width), BF16), jax.ShapeDtypeStruct((8, width), F32)],
        compiler_params=pltpu.CompilerParams(vmem_limit_bytes=VMEM),
        cost_estimate=QUICK,
        name="input_backward",
    )(grads, weight, xs, middle_grad, gain)


def unsort_kernel(me, rank, source, out):
    count, span = source.shape[0], rank.shape[0]
    place = lax.broadcasted_iota(jnp.int32, (span, count), 1)
    out[0] = dot((rank[...] == place).astype(BF16), source[...]).astype(BF16)


def unsort_call(me, rank_col, n, array):
    count, width = array.shape
    span = count // n
    return pl.pallas_call(
        unsort_kernel,
        grid_spec=pltpu.PrefetchScalarGridSpec(
            num_scalar_prefetch=1,
            grid=(n,),
            in_specs=[pl.BlockSpec((span, 1), lambda i, m: (i, 0)), whole((count, width))],
            out_specs=pl.BlockSpec((1, span, width), lambda i, m: (m[0] ^ i, 0, 0)),
        ),
        out_shape=jax.ShapeDtypeStruct((n, span, width), BF16),
        compiler_params=pltpu.CompilerParams(vmem_limit_bytes=VMEM),
        cost_estimate=QUICK,
        name="unsort",
    )(me, rank_col, array)


VECTORS = 128


def input_weights_kernel(core, normed, grads, first, second, third, up_sums, send, keep):
    mid, width = normed.shape[1], grads.shape[2]
    h = core[0] ^ 1 ^ pl.program_id(0)

    def write(out):
        for j in range(3):
            out[:, j * width : (j + 1) * width] = dot_tn(normed[...], grads[j]).astype(BF16)
        rows = [first[0:3, :], second[0:3, :], third[0:1, :]]
        for i in range(up_sums.shape[1] // width):
            rows.append(up_sums[:, pl.ds(pl.multiple_of(i * width + h * mid, 128), mid)])
        count = sum(row.shape[0] for row in rows)
        rows.append(jnp.zeros((VECTORS - count, mid), F32))
        out[:, 3 * width :] = jnp.concatenate(rows, axis=0).T.astype(BF16)

    pl.when(pl.program_id(0) == 0)(lambda: write(send))
    pl.when(pl.program_id(0) == 1)(lambda: write(keep))


def input_weights_call(core, normed, grads, first, second, third, up_sums):
    count, width = normed.shape
    half = jax.ShapeDtypeStruct((width // 2, 3 * width + VECTORS), BF16)
    rows = pl.BlockSpec((count, width // 2), lambda i, c: (0, c[0] ^ 1 ^ i))
    vector = pl.BlockSpec((8, width // 2), lambda i, c: (0, c[0] ^ 1 ^ i))
    return pl.pallas_call(
        input_weights_kernel,
        grid_spec=pltpu.PrefetchScalarGridSpec(
            num_scalar_prefetch=1,
            grid=(2,),
            in_specs=[rows, whole(grads.shape), vector, vector, vector, whole(up_sums.shape)],
            out_specs=[whole(half.shape)] * 2,
        ),
        out_shape=[half] * 2,
        compiler_params=pltpu.CompilerParams(vmem_limit_bytes=VMEM),
        cost_estimate=QUICK,
        name="input_weights",
    )(core, normed, grads, first, second, third, up_sums)


GROUPS = 4


def final_call(core, turns, blocks, groups, pieces, name, spread, outs):
    size = blocks // groups
    rows = pieces[0].shape[0] // (blocks // 2)
    whole_tile = 1 if rows % 16 == 0 else 2

    def kernel(c, t, *refs):
        h, g = pl.program_id(0), pl.program_id(1)
        active = (h * groups + g) // (groups // 2)
        turn = t[h]
        place = g ^ (turn // size)

        def write(source):
            for j in range(0, size, whole_tile):
                part = source[j * rows : (j + whole_tile) * rows, :].astype(F32)
                for i in range(whole_tile):
                    spread(part[i * rows : (i + 1) * rows], (j + i) ^ (turn % size), place, refs[4:])

        for q in range(4):
            pl.when(active == q)(functools.partial(write, refs[q]))

    def in_spec(q):
        def index(h, g, c, t):
            return jnp.clip(h * groups + g - q * (groups // 2), 0, groups // 2 - 1), 0

        return pl.BlockSpec((size * rows, pieces[q].shape[1]), index)

    def out_spec(block, index):
        return pl.BlockSpec(block, lambda h, g, c, t: index(h ^ c[0], g, lambda n: n ^ (t[h] // size)))

    return pl.pallas_call(
        kernel,
        grid_spec=pltpu.PrefetchScalarGridSpec(
            num_scalar_prefetch=2,
            grid=(2, groups),
            in_specs=[in_spec(q) for q in range(4)],
            out_specs=[out_spec(block, index) for _, block, index in outs],
        ),
        out_shape=[jax.ShapeDtypeStruct(shape, F32) for shape, _, _ in outs],
        compiler_params=pltpu.CompilerParams(vmem_limit_bytes=VMEM),
        cost_estimate=QUICK,
        name=name,
    )(core, turns, *pieces)


def rows_at(ref, place, value):
    rows = value.shape[0]
    ref[pl.ds(pl.multiple_of(place * rows, 8), rows), :] = value


def down_final(core, turns, blocks, pieces, ff):
    rows, width = pieces[0].shape[0] // (blocks // 2), pieces[0].shape[1]
    size = blocks // GROUPS * rows

    def spread(block, j, place, refs):
        @pl.when(place < GROUPS - 1)
        def _():
            rows_at(refs[0], j, block)

        @pl.when((place == GROUPS - 1) & (j * rows < width // 2))
        def _():
            rows_at(refs[1], j, block)

    def down_index(h, g, place):
        at = place(g)
        near = place(jnp.where(g == 0, 1, g - 1))
        return h * (GROUPS - 1) + jnp.where(at == GROUPS - 1, near, at), 0

    outs = [
        ((ff, width), (size, width), down_index),
        ((width, width), (width // 2, width), lambda h, g, place: (h, 0)),
    ]
    return final_call(core, turns, blocks, GROUPS, pieces, "down_final", spread, outs)


def up_final(core, turns, blocks, pieces):
    rows, cols = pieces[0].shape[0] * 2, pieces[0].shape[1]

    def spread(block, j, place, refs):
        rows_at(refs[0], j, block)

    outs = [((rows, 2 * cols), (rows // 2, cols), lambda h, g, place: (place(g), h))]
    return final_call(core, turns, blocks, 2, pieces, "up_final", spread, outs)[0]


def input_final(core, turns, blocks, pieces):
    width, cols = pieces[0].shape[0] * 4, pieces[0].shape[1]

    def spread(block, j, place, refs):
        rows_at(refs[0], j, block[:, : 3 * width])
        rows_at(refs[1], j, block[:, 3 * width :])

    outs = [
        ((width, n), (width // 4, n), lambda h, g, place: (h * 2 + place(g), 0))
        for n in (3 * width, cols - 3 * width)
    ]
    return final_call(core, turns, blocks, 2, pieces, "input_final", spread, outs)


def copy_kernel(source, out):
    out[...] = source[...]


def copy_call(array):
    spec = pl.BlockSpec((1, *array.shape[1:]), lambda i: (i, 0, 0))
    return pl.pallas_call(
        copy_kernel,
        grid=(array.shape[0],),
        in_specs=[spec],
        out_specs=spec,
        out_shape=jax.ShapeDtypeStruct(array.shape, array.dtype),
        compiler_params=pltpu.CompilerParams(vmem_limit_bytes=VMEM),
        cost_estimate=QUICK,
        name="copy",
    )(array)


MICRO = 2


def from_behind(value, axis, steps):
    count = lax.axis_size(axis)
    pairs = [(source, (source + steps) % count) for source in range(count)]
    return lax.ppermute(value, axis, pairs)


def norm_rows(values, gain, shift):
    centre = values - jnp.mean(values, axis=-1, keepdims=True)
    spread = jnp.mean(centre * centre, axis=-1, keepdims=True)
    return centre * lax.rsqrt(spread + eps_norm) * gain + shift


def gelu_exact(values):
    return jax.nn.gelu(values, approximate=False)


def split_heads(block):
    return block.reshape(block.shape[0], block.shape[1], HEADS, HEAD_DIM)


def take_rows(array, first_row, count_rows):
    return lax.slice_in_dim(array, first_row, first_row + count_rows, axis=0)


def masked_scores(query, keys, ids_query, ids_keys):
    scores = jnp.einsum(
        "rqhd,rkhd->rhqk", split_heads(query), split_heads(keys), preferred_element_type=jnp.float32
    ) * HEAD_DIM ** (-0.5)
    same = ids_query[:, None, :, None] == ids_keys[:, None, None, :]
    return jnp.where(same, scores, -jnp.inf)


def attend_piece(carry, query, ids_query, piece):
    keys, values, ids_keys = piece
    peak, total, accum = carry
    scores = masked_scores(query, keys, ids_query, ids_keys)
    top = jnp.maximum(peak, jnp.max(scores, axis=-1))
    weights = jnp.exp(scores - top[..., None])
    total = jnp.sum(weights, axis=-1)
    update = jnp.einsum(
        "rhqk,rkhd->rqhd",
        weights.astype(jnp.bfloat16),
        split_heads(values),
        preferred_element_type=jnp.float32,
    )
    return (top, total, update.reshape(accum.shape))


def attention_forward(query, keys, values, ids_query):
    rows_here, slots, width = query.shape
    start_state = (
        jnp.full((rows_here, HEADS, slots), -1e30, jnp.float32),
        jnp.zeros((rows_here, HEADS, slots), jnp.float32),
        jnp.zeros((rows_here, slots, width), jnp.float32),
    )
    carry = attend_piece(
        start_state,
        query,
        ids_query,
        (
            lax.all_gather(keys, "blk", axis=1, tiled=True),
            lax.all_gather(values, "blk", axis=1, tiled=True),
            lax.all_gather(ids_query, "blk", axis=1, tiled=True),
        ),
    )
    return (carry[0], carry[1], carry[2], None)


def attention_back(query, out_grad, ids_query, log_total, inner, piece):
    keys, values, ids_keys = piece
    scale = HEAD_DIM ** (-0.5)
    scores = masked_scores(query, keys, ids_query, ids_keys)
    probs = jnp.exp(scores - log_total[..., None])
    prob_grad = jnp.einsum(
        "rqhd,rkhd->rhqk",
        split_heads(out_grad),
        split_heads(values),
        preferred_element_type=jnp.float32,
    )
    score_grad = (probs * (prob_grad - inner[..., None])).astype(jnp.bfloat16)
    value_grad = jnp.einsum(
        "rhqk,rqhd->rkhd",
        probs.astype(jnp.bfloat16),
        split_heads(out_grad),
        preferred_element_type=jnp.float32,
    )
    key_grad = (
        jnp.einsum(
            "rhqk,rqhd->rkhd", score_grad, split_heads(query), preferred_element_type=jnp.float32
        )
        * scale
    )
    query_grad = (
        jnp.einsum(
            "rhqk,rkhd->rqhd", score_grad, split_heads(keys), preferred_element_type=jnp.float32
        )
        * scale
    )
    return (
        query_grad.reshape(query.shape),
        key_grad.reshape(keys.shape),
        value_grad.reshape(values.shape),
    )


def local(
    inputs,
    image_index,
    keep_mask,
    first_gain,
    first_shift,
    input_weight,
    input_bias,
    output_weight,
    output_bias,
    second_gain,
    second_shift,
    up_weight,
    up_bias,
    down_weight,
    down_bias,
    cotangent,
):
    rows_local, slots, width = inputs.shape
    rows_micro = rows_local // MICRO
    count = rows_micro * slots
    blocks = lax.axis_size("blk")
    params = (
        first_gain,
        first_shift,
        input_weight,
        input_bias,
        output_weight,
        output_bias,
        second_gain,
        second_shift,
        up_weight,
        up_bias,
        down_weight,
        down_bias,
    )
    sums = [jnp.zeros(item.shape, jnp.float32) for item in params]
    results = []
    input_grads = []
    for micro in range(MICRO):
        first_row = micro * rows_micro
        rows_in = take_rows(inputs, first_row, rows_micro).astype(jnp.float32).reshape(count, width)
        out_cot = (
            take_rows(cotangent, first_row, rows_micro).astype(jnp.float32).reshape(count, width)
        )
        ids_query = take_rows(image_index, first_row, rows_micro).astype(jnp.bfloat16)
        keep = take_rows(keep_mask, first_row, rows_micro).astype(jnp.float32) / keep_rate
        keep_attn = jnp.broadcast_to(keep[:, None, 0:1], (rows_micro, slots, 1)).reshape(count, 1)
        keep_mlp = jnp.broadcast_to(keep[:, None, 1:2], (rows_micro, slots, 1)).reshape(count, 1)
        normed = norm_rows(rows_in, first_gain, first_shift).astype(jnp.bfloat16)
        mixed = jnp.dot(normed, input_weight, preferred_element_type=jnp.float32)
        query = (
            (mixed[:, :width] + input_bias[0])
            .astype(jnp.bfloat16)
            .reshape(rows_micro, slots, width)
        )
        keys = mixed[:, width : 2 * width].astype(jnp.bfloat16).reshape(rows_micro, slots, width)
        values = (
            (mixed[:, 2 * width :] + input_bias[1])
            .astype(jnp.bfloat16)
            .reshape(rows_micro, slots, width)
        )
        top, total, accum, whole = attention_forward(query, keys, values, ids_query)
        attended = (split_heads(accum) / jnp.transpose(total, (0, 2, 1))[..., None]).reshape(
            count, width
        )
        log_total = top + jnp.log(total)
        attended_low = attended.astype(jnp.bfloat16)
        branch = (
            jnp.dot(attended_low, output_weight, preferred_element_type=jnp.float32) + output_bias
        )
        middle = rows_in + keep_attn * branch
        normed_second = norm_rows(middle, second_gain, second_shift).astype(jnp.bfloat16)
        hidden = jnp.dot(normed_second, up_weight, preferred_element_type=jnp.float32) + up_bias
        active = gelu_exact(hidden).astype(jnp.bfloat16)
        branch_second = jnp.dot(active, down_weight, preferred_element_type=jnp.float32) + down_bias
        results.append(
            (middle + keep_mlp * branch_second)
            .astype(jnp.bfloat16)
            .reshape(rows_micro, slots, width)
        )
        mlp_grad = (out_cot * keep_mlp).astype(jnp.bfloat16)
        sums[10] = sums[10] + jnp.dot(active.T, mlp_grad, preferred_element_type=jnp.float32)
        sums[11] = sums[11] + jnp.sum(mlp_grad.astype(jnp.float32), axis=0)
        active_grad = jnp.dot(mlp_grad, down_weight.T, preferred_element_type=jnp.float32)
        hidden_grad = jax.vjp(gelu_exact, hidden)[1](active_grad)[0].astype(jnp.bfloat16)
        sums[8] = sums[8] + jnp.dot(
            normed_second.T, hidden_grad, preferred_element_type=jnp.float32
        )
        sums[9] = sums[9] + jnp.sum(hidden_grad.astype(jnp.float32), axis=0)
        second_in_grad = jnp.dot(hidden_grad, up_weight.T, preferred_element_type=jnp.float32)
        middle_part, second_gain_part, second_shift_part = jax.vjp(
            norm_rows, middle, second_gain, second_shift
        )[1](second_in_grad)
        sums[6] = sums[6] + second_gain_part
        sums[7] = sums[7] + second_shift_part
        middle_grad = middle_part + out_cot
        branch_grad = (middle_grad * keep_attn).astype(jnp.bfloat16)
        sums[4] = sums[4] + jnp.dot(attended_low.T, branch_grad, preferred_element_type=jnp.float32)
        sums[5] = sums[5] + jnp.sum(branch_grad.astype(jnp.float32), axis=0)
        attended_grad = jnp.dot(
            branch_grad, output_weight.T, preferred_element_type=jnp.float32
        ).astype(jnp.bfloat16)
        out_grad = attended_grad.reshape(rows_micro, slots, width)
        inner = jnp.transpose(
            jnp.sum(
                split_heads(
                    (attended_grad.astype(jnp.float32) * attended).reshape(rows_micro, slots, width)
                ),
                axis=-1,
            ),
            (0, 2, 1),
        )
        query_grad = jnp.zeros((rows_micro, slots, width), jnp.float32)
        visiting = (keys, values, ids_query)
        key_grad = jnp.zeros((rows_micro, slots, width), jnp.float32)
        value_grad = jnp.zeros((rows_micro, slots, width), jnp.float32)
        for step in range(blocks):
            query_part, key_part, value_part = attention_back(
                query, out_grad, ids_query, log_total, inner, visiting
            )
            query_grad = query_grad + query_part
            key_grad, value_grad = (
                from_behind((key_grad + key_part).astype(jnp.bfloat16), "blk", 1).astype(
                    jnp.float32
                ),
                from_behind((value_grad + value_part).astype(jnp.bfloat16), "blk", 1).astype(
                    jnp.float32
                ),
            )
            if step + 1 < blocks:
                visiting = from_behind((visiting[0], visiting[1], visiting[2]), "blk", 1)
        joined_grad = (
            jnp.concatenate([query_grad, key_grad, value_grad], axis=-1)
            .astype(jnp.bfloat16)
            .reshape(count, 3 * width)
        )
        sums[2] = sums[2] + jnp.dot(normed.T, joined_grad, preferred_element_type=jnp.float32)
        joined_sums = jnp.sum(joined_grad.astype(jnp.float32), axis=0)
        sums[3] = sums[3] + jnp.stack([joined_sums[:width], joined_sums[2 * width :]])
        first_in_grad = jnp.dot(joined_grad, input_weight.T, preferred_element_type=jnp.float32)
        rows_part, first_gain_part, first_shift_part = jax.vjp(
            norm_rows, rows_in, first_gain, first_shift
        )[1](first_in_grad)
        sums[0] = sums[0] + first_gain_part
        sums[1] = sums[1] + first_shift_part
        input_grads.append(
            (rows_part + middle_grad).astype(jnp.bfloat16).reshape(rows_micro, slots, width)
        )
    totals = lax.psum(
        (
            sums[0],
            sums[1],
            sums[2],
            sums[3],
            sums[4],
            sums[5],
            sums[6],
            sums[7],
            sums[8],
            sums[9],
            sums[10],
            sums[11],
        ),
        ("rows", "blk"),
    )
    return (
        jnp.concatenate(results, axis=0),
        jnp.concatenate(input_grads, axis=0),
        totals[0],
        totals[1],
        totals[2],
        totals[3],
        totals[4],
        totals[5],
        totals[6],
        totals[7],
        totals[8],
        totals[9],
        totals[10],
        totals[11],
    )


def swap(value, axis, bit):
    return lax.ppermute(value, axis, [(i, i ^ bit) for i in range(lax.axis_size(axis))])


def side(axis, bit):
    return (lax.axis_index(axis) // bit) % 2


def after(value, *others):
    return lax.optimization_barrier((value, *others))[0]


def axis_bits(axis):
    bits, bit = [], 1
    while bit < lax.axis_size(axis):
        bits.append((axis, bit))
        bit *= 2
    return bits


def add_low(a, b):
    return (a.astype(F32) + b.astype(F32)).astype(BF16)


def swap_two(value, step):
    rows, blocks = lax.axis_size("rows"), lax.axis_size("blk")
    pairs = []
    for r in range(rows):
        for b in range(blocks):
            axis, bit = step[b % 2]
            other = (r ^ bit, b) if axis == "rows" else (r, b ^ bit)
            pairs.append((r * blocks + b, other[0] * blocks + other[1]))
    return lax.ppermute(value, ("rows", "blk"), pairs)


def side_two(step):
    return jnp.where(side("blk", 1) == 0, side(*step[0]), side(*step[1]))


class Order:
    def __init__(self):
        self.last = ()

    def hold(self, value):
        return after(value, *self.last) if self.last else value

    def advance(self, *parts):
        parts = [part for part in parts if part.result is None]
        if parts:
            held = lax.optimization_barrier(([part.recv for part in parts], self.last))[0]
            self.done(*[value for part, recv in zip(parts, held) for value in part.step(recv)])

    def done(self, *values):
        self.last = values
        return values[0] if len(values) == 1 else values


class Chain:
    def __init__(self, steps, send, keep):
        self.steps, self.at = steps, -1
        self.recv, self.keep, self.result = send, keep, None

    def step(self, recv):
        keep, n = self.keep, len(self.steps)
        if self.at < 0:
            send, self.recv = recv, swap(recv, "blk", 1)
        elif self.at < n:
            step = self.steps[self.at]
            half = keep.shape[0] // 2
            own = side_two(step)

            def part(which):
                return add_low(
                    lax.dynamic_slice_in_dim(keep, which * half, half, 0),
                    lax.dynamic_slice_in_dim(recv, which * half, half, 0),
                )

            send, self.keep = part(1 - own), part(own)
            self.recv = swap_two(send, step)
        elif self.at < 2 * n:
            send = add_low(keep, recv) if self.at == n else jnp.concatenate([keep, recv], axis=0)
            send = self.keep = lax.optimization_barrier(send)
            self.recv = swap_two(send, self.steps[2 * n - 1 - self.at])
        elif self.at == 2 * n:
            self.at, self.keep, self.recv = self.at + 1, (keep, recv), [swap(piece, "blk", 1) for piece in (keep, recv)]
            return keep, recv
        else:
            self.result, self.recv = (*keep, *recv), None
            return ()
        self.at += 1
        return send, self.keep


class Small:
    def __init__(self, value):
        count = lax.axis_size("rows") * lax.axis_size("blk")
        self.recv, self.result, self.sent = jnp.broadcast_to(value[None], (count, *value.shape)), None, False

    def step(self, recv):
        if not self.sent:
            self.recv, self.sent = lax.all_to_all(recv, ("rows", "blk"), 0, 0), True
            return (recv,)
        self.result, self.recv = jnp.sum(recv, axis=0), None
        return (self.result,)


class Home:
    def __init__(self, pieces):
        self.recv, self.result, self.sent = pieces, None, False

    def step(self, recv):
        if not self.sent:
            self.recv, self.sent = lax.all_to_all(recv, "blk", 0, 0), True
        else:
            self.result, self.recv = recv, None
        return (recv,)


def block_turns(steps):
    core = side("blk", 1)
    turns = []
    for c in range(2):
        turn = 0
        for step in steps:
            turn = turn * 2 + side(*step[c])
        turns.append(turn)
    first, second = jnp.where(core == 0, turns[0], turns[1]), jnp.where(core == 0, turns[1], turns[0])
    return core.astype(jnp.int32).reshape(1), jnp.stack([first, second]).astype(jnp.int32), 1 << len(steps)


def local_rows(
    inputs,
    image_index,
    keep_mask,
    first_gain,
    first_shift,
    input_weight,
    input_bias,
    output_weight,
    output_bias,
    second_gain,
    second_shift,
    up_weight,
    up_bias,
    down_weight,
    down_bias,
    cotangent,
):
    blocks, span, width = inputs.shape
    ff = up_weight.shape[1]
    me = lax.axis_index("blk")

    def row_piece(array, s):
        return lax.dynamic_index_in_dim(array, me ^ s, 0, keepdims=False)

    xs_send = [row_piece(inputs, s) for s in range(blocks)]
    xs_in = xs_send[:1] + [swap(xs_send[s], "blk", s) for s in range(1, blocks)]
    ids = [row_piece(image_index, 0)] + [
        swap(row_piece(after(image_index, *xs_send), s), "blk", s) for s in range(1, blocks)
    ]
    cots = [row_piece(cotangent, 0)] + [
        swap(after(row_piece(cotangent, s), *xs_in), "blk", s) for s in range(1, blocks)
    ]
    ids = jnp.concatenate(ids)
    image = jnp.where(ids < 0, 4, ids)
    order_key = image * ids.shape[0] + jnp.arange(ids.shape[0], dtype=jnp.int32)
    less = (order_key[None, :] < order_key[:, None]).astype(jnp.int32)
    rank = jnp.sum(less, axis=1)
    starts = jnp.sum((image[None, :] < jnp.arange(6, dtype=jnp.int32)[:, None]).astype(jnp.int32), axis=1)
    keep = lax.dynamic_index_in_dim(keep_mask, me, 0, keepdims=False).astype(F32) / keep_rate
    rank_row, rank_col = rank[None, :], rank[:, None]

    bias = jnp.stack([input_bias[0], jnp.zeros_like(input_bias[0]), input_bias[1]])
    xs, normed, qkv = qkv_call(rank_row, xs_in, first_gain[None], first_shift[None], input_weight, bias)
    attended, stat = forward_call(starts, qkv)
    vectors = jnp.stack([output_bias, second_gain, second_shift, down_bias])
    core = side("blk", 1).astype(jnp.int32).reshape(1)
    cot, att_low, middle, normed2, mlp_grad, sums_mid = middle_call(
        keep, rank_row, cots, attended, xs, output_weight, vectors
    )
    (up_send, up_keep, down_send, down_keep, up_sums, result, middle_grad, branch, att_grad, sums2) = mlp_call(
        core, keep, normed2, mlp_grad, middle, cot, att_low, output_weight, vectors, up_weight, up_bias[None], down_weight
    )

    y, x, z = axis_bits("blk")[1], axis_bits("rows")[0], axis_bits("rows")[1:]
    far = [(d, d) for d in z[1:]]
    xy = [(x, y), (y, x), (z[0], z[0])] + far
    zx = [(z[0], z[0]), (x, y), (y, x)] + far
    order = Order()
    order.done(att_grad)
    up_chain, down_chain = Chain(zx, up_send, up_keep), Chain(xy, down_send, down_keep)

    order.advance(down_chain, up_chain)
    result_home = Home(order.done(unsort_call(me.reshape(1), rank_col, blocks, order.hold(result))))
    order.advance(down_chain, up_chain, result_home)
    grads, bias_sums = backward_call(starts, qkv, order.hold(att_grad), attended, stat, 0, PAIRS)
    order.done(grads)
    order.advance(down_chain, up_chain, result_home)
    input_chain = Chain(
        xy, *order.done(*input_weights_call(core, order.hold(normed), grads, bias_sums, sums2, sums_mid, up_sums))
    )
    order.advance(down_chain, up_chain, input_chain)
    inputs_grad, sums1 = order.done(*input_call(grads, input_weight, xs, order.hold(middle_grad), first_gain[None]))
    small = Small(sums1[:2])
    order.advance(down_chain, up_chain, input_chain, small)
    home = Home(order.done(unsort_call(me.reshape(1), rank_col, blocks, order.hold(inputs_grad))))
    order.advance(down_chain, up_chain, input_chain, small, home)
    order.advance(down_chain, up_chain, input_chain)
    order.advance(down_chain, up_chain, input_chain, home)
    while down_chain.at < 2 * len(xy):
        order.advance(down_chain, up_chain, input_chain)
    result_out = order.done(copy_call(order.hold(result_home.result)))
    inputs_out = order.done(copy_call(order.hold(home.result)))
    order.advance(down_chain, up_chain, input_chain)
    order.advance(down_chain, up_chain, input_chain)
    up_total = order.done(up_final(*block_turns(zx), (order.hold(up_chain.result[0]), *up_chain.result[1:])))
    order.advance(input_chain)
    down_total, out_total = order.done(
        *down_final(*block_turns(xy), (order.hold(down_chain.result[0]), *down_chain.result[1:]), ff)
    )
    while input_chain.result is None:
        order.advance(input_chain)
    input_total, sums = input_final(*block_turns(xy), input_chain.result)
    sums = jnp.concatenate([small.result, sums[:, :16].T])

    return (
        result_out,
        inputs_out,
        sums[0],
        sums[1],
        input_total,
        jnp.stack([sums[2], sums[4]]),
        out_total,
        sums[7],
        sums[5],
        sums[6],
        up_total,
        sums[9:13].reshape(ff),
        down_total,
        sums[8],
    )


def solution(mesh):
    blocks, groups = mesh.shape["blk"], mesh.shape["rows"]

    def run(*args):
        whole_rows = args[0].shape[0] // groups == blocks == 4 and groups in (4, 8, 16)
        return jax.shard_map(
            local_rows if whole_rows else local,
            mesh=mesh,
            in_specs=(P("rows", "blk", None), P("rows", "blk"), P("rows", None)) + (P(),) * 12 + (P("rows", "blk", None),),
            out_specs=(P("rows", "blk", None),) * 2 + (P(),) * 12,
            check_vma=False,
        )(*args)

    return run
```

profile of v0, /device:TPU:0, one launch (start us, length us, event | category | flops | bytes accessed | tf_op | source)
XLA Modules:
  0.0 393.0 jit_solution(13010130142562248731)
XLA Ops:
  12.9 13.6 %collective-permute-done.1 = s32[288]{0:T(512)S(1)} collective-permute-done((s32[288]{0:T(512)S(1)}, s32[288]{0:T(512)S(1)}, u32[]{:S(2)}, u32[]{:S(2)}) %collective-permute-start.1) | collective-permute-done | bytes 1184 | tf_op jit(solution)/shard_map/ppermute | solution.py:973
  30.5 13.1 %sort_qkv.1 = (bf16[1152,768]{1,0:T(8,128)(2,1)}, bf16[1152,768]{1,0:T(8,128)(2,1)}, bf16[3,1152,768]{2,1,0:T(8,128)(2,1)}) custom-call(s32[1,1152]{1,0:T(1,128)} %broadcast_in_dim.31.refs_0_.refs_1_, bf16[288,768]{1,0:T(8,128)(2,1)} %get-tuple-element.239.refs_1_, bf16[288,768]{1,0:T(8,128)(2,1)} %copy-done.17, bf16[288,768]{1,0:T(8,128)(2,1)} %copy-done.18, ...), custom_call_target="tpu_custom_call" | custom-call | flops 1048576 | bytes 65536 | tf_op jit(solution)/shard_map/sort_qkv/pallas_call | solution.py:85
  43.6 15.5 %attention_forward.1 = (f32[1152,768]{1,0:T(8,128)}, f32[1152,768]{1,0:T(8,128)}) custom-call(s32[6]{0:T(128)} %convert_reduce_fusion.1.starts, bf16[3,1152,768]{2,1,0:T(8,128)(2,1)} %get-tuple-element.103.qkv), custom_call_target="tpu_custom_call" | custom-call | flops 1048576 | bytes 65536 | tf_op jit(solution)/shard_map/attention_forward/pallas_call | solution.py:165
  59.2 10.5 %middle.1 = (bf16[1152,768]{1,0:T(8,128)(2,1)}, bf16[1152,768]{1,0:T(8,128)(2,1)}, f32[1152,768]{1,0:T(8,128)}, bf16[1152,768]{1,0:T(8,128)(2,1)}, bf16[1152,768]{1,0:T(8,128)(2,1)}, /*index=5*/f32[8,768]{1,0:T(8,128)}) custom-call(f32[2]{0:T(128)} %fusion.6.refs_0_.keep, s32[1,1152]{1,0:T(1,128)} %broadcast_in_dim.31.refs_0_.refs_1_, ...), custom_call_target="tpu_custom_call" | custom-call | flops 1048576 | bytes 65536 | tf_op jit(solution)/shard_map/middle/pallas_call | solution.py:322
  69.7 59.7 %mlp.1 = (bf16[768,1536]{1,0:T(8,128)(2,1)}, bf16[768,1536]{1,0:T(8,128)(2,1)}, bf16[2048,768]{1,0:T(8,128)(2,1)}, bf16[2048,768]{1,0:T(8,128)(2,1)}, f32[1,3072...) custom-call(s32[1]{0:T(128)} %bitcast.core.c, ...), custom_call_target="tpu_custom_call" | custom-call | flops 1048576 | bytes 65536 | tf_op jit(solution)/shard_map/mlp/pallas_call | solution.py:425
  131.4 6.0 %unsort.2 = bf16[4,288,768]{2,1,0:T(8,128)(2,1)} custom-call(s32[1]{0:T(128)} %bitcast.10.me, s32[1152,1]{1,0:T(8,128)} %broadcast_in_dim.37.rank, bf16[1152,768]{1,0:T(8,128)(2,1)} %get-tuple-element.119.source), custom_call_target="tpu_custom_call" | custom-call | flops 1048576 | bytes 65536 | tf_op jit(solution)/shard_map/unsort/pallas_call | solution.py:505
  139.3 5.3 %add_convert_fusion = (bf16[1024,768]{1,0:T(8,128)(2,1)}, bf16[1024,768]{1,0:T(8,128)(2,1)}) fusion(bf16[2048,768]{1,0:T(8,128)(2,1)} %collective-permute-done.9, s32[]{:T(128)S(6)} %select_n.383, bf16[2048,768]{1,0:T(8,128)(2,1)} %get-tuple-element.111, s32[]{:T(128)S(6)} %select_n.379), kind=kLoop, calls=%fused_computation.1 | loop fusion | flops 6291456 | bytes 9437192 | tf_op jit(solution)/shard_map/convert_element_type | solution.py:993
  146.2 3.6 all-to-all-start
  149.8 4.3 %add_convert_fusion.2 = (bf16[384,1536]{1,0:T(8,128)(2,1)}, bf16[384,1536]{1,0:T(8,128)(2,1)}) fusion(bf16[768,1536]{1,0:T(8,128)(2,1)} %collective-permute-done.10, s32[]{:T(128)S(6)} %select_n.384, bf16[768,1536]{1,0:T(8,128)(2,1)} %get-tuple-element.118, s32[]{:T(128)S(6)} %select_n.382), kind=kLoop, calls=%fused_computation.3 | loop fusion | flops 4718592 | bytes 7077896 | tf_op jit(solution)/shard_map/convert_element_type | solution.py:993
  155.6 31.9 %attention_backward.1 = (bf16[3,1152,768]{2,1,0:T(8,128)(2,1)}, f32[8,768]{1,0:T(8,128)}) custom-call(s32[6]{0:T(128)} %convert_reduce_fusion.1.starts, bf16[3,1152,768]{2,1,0:T(8,128)(2,1)} %get-tuple-element.103.qkv, bf16[1152,768]{1,0:T(8,128)(2,1)} %get-tuple-element.123.grad, f32[1152,768]{1,0:T(8,128)} %get-tuple-element.104.refs_6_.att, ...), custom_call_target="tpu_custom_call" | custom-call | flops 1048576 | bytes 65536 | tf_op jit(solution)/shard_map/attention_backward/pallas_call | solution.py:254
  187.6 4.0 %add_convert_fusion.7 = (bf16[512,768]{1,0:T(8,128)(2,1)}, bf16[512,768]{1,0:T(8,128)(2,1)}) fusion(bf16[1024,768]{1,0:T(8,128)(2,1)} %collective-permute-done.11, s32[]{:T(128)S(6)} %select_n.386, bf16[1024,768]{1,0:T(8,128)(2,1)} %get-tuple-element.221, s32[]{:T(128)S(6)} %select_n.388), kind=kLoop, calls=%fused_computation.9 | loop fusion | flops 3145728 | bytes 4718600 | tf_op jit(solution)/shard_map/convert_element_type | solution.py:993
  197.0 9.8 %input_weights.1 = (bf16[384,2432]{1,0:T(8,128)(2,1)}, bf16[384,2432]{1,0:T(8,128)(2,1)}) custom-call(s32[1]{0:T(128)} %bitcast.core.c, bf16[1152,768]{1,0:T(8,128)(2,1)} %get-tuple-element.130.normed, bf16[3,1152,768]{2,1,0:T(8,128)(2,1)} %get-tuple-element.125.grads, f32[8,768]{1,0:T(8,128)} %get-tuple-element.131.first, ...), custom_call_target="tpu_custom_call" | custom-call | flops 1048576 | bytes 65536 | tf_op jit(solution)/shard_map/input_weights/pallas_call | solution.py:546
  206.8 2.9 collective-permute-done.14
  215.4 10.6 %input_backward.1 = (bf16[1152,768]{1,0:T(8,128)(2,1)}, f32[8,768]{1,0:T(8,128)}) custom-call(bf16[3,1152,768]{2,1,0:T(8,128)(2,1)} %get-tuple-element.125.grads, bf16[768,2304]{1,0:T(8,128)(2,1)} %weight.1, bf16[1152,768]{1,0:T(8,128)(2,1)} %get-tuple-element.105.refs_7_.xs, f32[1152,768]{1,0:T(8,128)} %get-tuple-element.141.middle_grad, ...), custom_call_target="tpu_custom_call" | custom-call | flops 1048576 | bytes 65536 | tf_op jit(solution)/shard_map/input_backward/pallas_call | solution.py:478
  227.5 3.4 add_convert_fusion.4
  235.5 3.3 all-to-all-start.1
  238.9 2.7 collective-permute-start.19
  241.6 5.9 %unsort.3 = bf16[4,288,768]{2,1,0:T(8,128)(2,1)} custom-call(s32[1]{0:T(128)} %bitcast.10.me, s32[1152,1]{1,0:T(8,128)} %broadcast_in_dim.37.rank, bf16[1152,768]{1,0:T(8,128)(2,1)} %get-tuple-element.148.source), custom_call_target="tpu_custom_call" | custom-call | flops 1048576 | bytes 65536 | tf_op jit(solution)/shard_map/unsort/pallas_call | solution.py:505
  247.6 8.1 %collective-permute-done.19 = bf16[48,1536]{1,0:T(8,128)(2,1)S(1)} collective-permute-done((bf16[48,1536]{1,0:T(8,128)(2,1)S(1)}, bf16[48,1536]{1,0:T(8,128)(2,1)S(1)}, u32[]{:S(2)}, u32[]{:S(2)}) %collective-permute-start.19) | collective-permute-done | bytes 147488 | tf_op jit(solution)/shard_map/ppermute | solution.py:1004
  260.0 3.6 all-to-all-start.2
  263.6 2.9 collective-permute-start.22
  267.1 10.8 %collective-permute-done.22 = bf16[48,1536]{1,0:T(8,128)(2,1)S(1)} collective-permute-done((bf16[48,1536]{1,0:T(8,128)(2,1)S(1)}, bf16[48,1536]{1,0:T(8,128)(2,1)S(1)}, u32[]{:S(2)}, u32[]{:S(2)}) %collective-permute-start.22) | collective-permute-done | bytes 147488 | tf_op jit(solution)/shard_map/ppermute | solution.py:1004
  282.2 11.2 %collective-permute-done.26 = bf16[48,2432]{1,0:T(8,128)(2,1)S(1)} collective-permute-done((bf16[48,2432]{1,0:T(8,128)(2,1)S(1)}, bf16[48,2432]{1,0:T(8,128)(2,1)S(1)}, u32[]{:S(2)}, u32[]{:S(2)}) %collective-permute-start.26) | collective-permute-done | bytes 233504 | tf_op jit(solution)/shard_map/ppermute | solution.py:1004
  301.0 5.4 %collective-permute-done.29 = bf16[24,2432]{1,0:T(8,128)(2,1)S(1)} collective-permute-done((bf16[24,2432]{1,0:T(8,128)(2,1)S(1)}, bf16[24,2432]{1,0:T(8,128)(2,1)S(1)}, u32[]{:S(2)}, u32[]{:S(2)}) %collective-permute-start.29) | collective-permute-done | bytes 116768 | tf_op jit(solution)/shard_map/ppermute | solution.py:1004
  306.4 6.1 %collective-permute-done.28 = bf16[192,1536]{1,0:T(8,128)(2,1)} collective-permute-done((bf16[192,1536]{1,0:T(8,128)(2,1)S(1)}, bf16[192,1536]{1,0:T(8,128)(2,1)}, u32[]{:S(2)}, u32[]{:S(2)}) %collective-permute-start.28) | collective-permute-done | bytes 589856 | tf_op jit(solution)/shard_map/ppermute | solution.py:1004
  321.7 3.6 copy.47
  325.4 3.6 copy.48
  329.0 15.9 %collective-permute-done.32 = bf16[24,2432]{1,0:T(8,128)(2,1)S(1)} collective-permute-done((bf16[24,2432]{1,0:T(8,128)(2,1)S(1)}, bf16[24,2432]{1,0:T(8,128)(2,1)S(1)}, u32[]{:S(2)}, u32[]{:S(2)}) %collective-permute-start.32) | collective-permute-done | bytes 116768 | tf_op jit(solution)/shard_map/ppermute | solution.py:1004
  351.8 3.8 collective-permute-done.37
  358.6 7.0 %up_final.1 = f32[768,3072]{1,0:T(8,128)} custom-call(s32[1]{0:T(128)} %bitcast.core.c, s32[2]{0:T(128)} %pad_add_fusion.1.t, bf16[384,1536]{1,0:T(8,128)(2,1)} %pad_maximum_fusion.1.refs_0_, bf16[384,1536]{1,0:T(8,128)(2,1)} %collective-permute-done.31.refs_1_, bf16[384,1536]{1,0:T(8,128)(2,1)} %copy-done.10, bf16[384,1536]{1,0:T(8,128)(2,1)} %copy-done.11), custom_call_target="tpu_custom_call" | custom-call | flops 1048576 | bytes 65536 | tf_op jit(solution)/shard_map/up_final/pallas_call | solution.py:593
  368.2 10.6 %down_final.1 = (f32[3072,768]{1,0:T(8,128)}, f32[768,768]{1,0:T(8,128)}) custom-call(s32[1]{0:T(128)} %bitcast.core.c, s32[2]{0:T(128)} %pad_add_fusion.t, bf16[1024,768]{1,0:T(8,128)(2,1)} %copy-done.2, bf16[1024,768]{1,0:T(8,128)(2,1)} %collective-permute-done.30.refs_1_, bf16[1024,768]{1,0:T(8,128)(2,1)} %collective-permute-done.33.refs_2_, ...), custom_call_target="tpu_custom_call" | custom-call | flops 1048576 | bytes 65536 | tf_op jit(solution)/shard_map/down_final/pallas_call | solution.py:593
  381.9 6.1 %input_final.1 = (f32[768,2304]{1,0:T(8,128)}, f32[768,128]{1,0:T(8,128)}) custom-call(s32[1]{0:T(128)} %bitcast.core.c, s32[2]{0:T(128)} %pad_add_fusion.t, bf16[192,2432]{1,0:T(8,128)(2,1)} %copy-done.4, bf16[192,2432]{1,0:T(8,128)(2,1)} %copy-done.14, bf16[192,2432]{1,0:T(8,128)(2,1)} %collective-permute-done.40.refs_2_, ...), custom_call_target="tpu_custom_call" | custom-call | flops 1048576 | bytes 65536 | tf_op jit(solution)/shard_map/input_final/pallas_call | solution.py:593
  (207 shorter events, 86.3 us)
Async XLA Ops:
  3.1 23.4 %collective-permute-start.3 = (bf16[288,768]{1,0:T(8,128)(2,1)S(1)}, bf16[288,768]{1,0:T(8,128)(2,1)S(1)}, u32[]{:S(2)}, u32[]{:S(2)}) collective-permute-start(bf16[288,768]{1,0:T(8,128)(2,1)S(1)} %get-tuple-element.238), channel_id=1, source_target_pairs={{0,1},{1,0},{2,3},{3,2},{4,5},{5,4},{6,7},{7,6},{8,9},{9,8},{10,11... | collective-permute-start | bytes 1327112 | tf_op jit(solution)/shard_map/ppermute | solution.py:973
  3.6 23.0 %collective-permute-start.4 = (bf16[288,768]{1,0:T(8,128)(2,1)S(1)}, bf16[288,768]{1,0:T(8,128)(2,1)S(1)}, u32[]{:S(2)}, u32[]{:S(2)}) collective-permute-start(bf16[288,768]{1,0:T(8,128)(2,1)S(1)} %get-tuple-element.240), channel_id=1, source_target_pairs={{0,2},{1,3},{2,0},{3,1},{4,6},{5,7},{6,4},{7,5},{8,10},{9,11},{10,... | collective-permute-start | bytes 1327112 | tf_op jit(solution)/shard_map/ppermute | solution.py:973
  6.1 20.5 %collective-permute-start.5 = (bf16[288,768]{1,0:T(8,128)(2,1)S(1)}, bf16[288,768]{1,0:T(8,128)(2,1)S(1)}, u32[]{:S(2)}, u32[]{:S(2)}) collective-permute-start(bf16[288,768]{1,0:T(8,128)(2,1)S(1)} %get-tuple-element.237), channel_id=1, source_target_pairs={{0,3},{1,2},{2,1},{3,0},{4,7},{5,6},{6,5},{7,4},{8,11},{9,10},{10,... | collective-permute-start | bytes 1327112 | tf_op jit(solution)/shard_map/ppermute | solution.py:973
  6.4 20.1 %collective-permute-start.1 = (s32[288]{0:T(512)S(1)}, s32[288]{0:T(512)S(1)}, u32[]{:S(2)}, u32[]{:S(2)}) collective-permute-start(s32[288]{0:T(512)S(1)} %get-tuple-element.219), channel_id=1, source_target_pairs={{0,2},{1,3},{2,0},{3,1},{4,6},{5,7},{6,4},{7,5},{8,10},{9,11},{10,... | collective-permute-start | bytes 3464 | tf_op jit(solution)/shard_map/ppermute | solution.py:973
  10.3 16.2 %collective-permute-start.2 = (s32[288]{0:T(512)S(1)}, s32[288]{0:T(512)S(1)}, u32[]{:S(2)}, u32[]{:S(2)}) collective-permute-start(s32[288]{0:T(512)S(1)} %get-tuple-element.218), channel_id=1, source_target_pairs={{0,3},{1,2},{2,1},{3,0},{4,7},{5,6},{6,5},{7,4},{8,11},{9,10},{10,... | collective-permute-start | bytes 3464 | tf_op jit(solution)/shard_map/ppermute | solution.py:973
  26.6 32.6 %collective-permute-start.8 = (bf16[288,768]{1,0:T(8,128)(2,1)}, bf16[288,768]{1,0:T(8,128)(2,1)}, u32[]{:S(2)}, u32[]{:S(2)}) collective-permute-start(bf16[288,768]{1,0:T(8,128)(2,1)} %get-tuple-element.102), channel_id=1, source_target_pairs={{0,3},{1,2},{2,1},{3,0},{4,7},{5,6},{6,5},{7,4},{8,11},{9,10},{10,... | collective-permute-start | bytes 1327112 | tf_op jit(solution)/shard_map/ppermute | solution.py:973
  28.1 31.0 %collective-permute-start.7 = (bf16[288,768]{1,0:T(8,128)(2,1)}, bf16[288,768]{1,0:T(8,128)(2,1)}, u32[]{:S(2)}, u32[]{:S(2)}) collective-permute-start(bf16[288,768]{1,0:T(8,128)(2,1)} %get-tuple-element.101), channel_id=1, source_target_pairs={{0,2},{1,3},{2,0},{3,1},{4,6},{5,7},{6,4},{7,5},{8,10},{9,11},{10,... | collective-permute-start | bytes 1327112 | tf_op jit(solution)/shard_map/ppermute | solution.py:973
  28.5 30.7 %collective-permute-start.6 = (bf16[288,768]{1,0:T(8,128)(2,1)S(1)}, bf16[288,768]{1,0:T(8,128)(2,1)}, u32[]{:S(2)}, u32[]{:S(2)}) collective-permute-start(bf16[288,768]{1,0:T(8,128)(2,1)S(1)} %get-tuple-element.100), channel_id=1, source_target_pairs={{0,1},{1,0},{2,3},{3,2},{4,5},{5,4},{6,7},{7,6},{8,9},{9,8},{10,11... | collective-permute-start | bytes 1327112 | tf_op jit(solution)/shard_map/ppermute | solution.py:973
  144.6 43.0 %collective-permute-start.11 = (bf16[1024,768]{1,0:T(8,128)(2,1)}, bf16[1024,768]{1,0:T(8,128)(2,1)}, u32[]{:S(2)}, u32[]{:S(2)}) collective-permute-start(bf16[1024,768]{1,0:T(8,128)(2,1)} %get-tuple-element.222), channel_id=1, source_target_pairs={{0,4},{1,3},{2,6},{3,1},{4,0},{5,7},{6,2},{7,5},{8,12},{9,11},{10,... | collective-permute-start | bytes 4718600 | tf_op jit(solution)/shard_map/ppermute | solution.py:1004
  146.2 41.3 %all-to-all-start = ((bf16[4,288,768]{2,1,0:T(8,128)(2,1)}), bf16[4,288,768]{2,1,0:T(8,128)(2,1)S(1)}, u32[]{:S(2)}, u32[]{:S(2)}) async-start(bf16[4,288,768]{2,1,0:T(8,128)(2,1)} %unsort.2), calls=%async_computation | async-start | bytes 3538944 | tf_op jit(solution)/shard_map/all_to_all | solution.py:1084
  154.1 33.4 %collective-permute-start.12 = (bf16[384,1536]{1,0:T(8,128)(2,1)}, bf16[384,1536]{1,0:T(8,128)(2,1)}, u32[]{:S(2)}, u32[]{:S(2)}) collective-permute-start(bf16[384,1536]{1,0:T(8,128)(2,1)} %get-tuple-element.224), channel_id=1, source_target_pairs={{0,8},{1,9},{2,10},{3,11},{4,12},{5,13},{6,14},{7,15},{8,0},{9,1},... | collective-permute-start | bytes 3538952 | tf_op jit(solution)/shard_map/ppermute | solution.py:1004
  191.6 18.4 %collective-permute-start.13 = (bf16[512,768]{1,0:T(8,128)(2,1)}, bf16[512,768]{1,0:T(8,128)(2,1)}, u32[]{:S(2)}, u32[]{:S(2)}) collective-permute-start(bf16[512,768]{1,0:T(8,128)(2,1)} %get-tuple-element.228), channel_id=1, source_target_pairs={{0,2},{1,5},{2,0},{3,7},{4,6},{5,1},{6,4},{7,3},{8,10},{9,13},{10,... | collective-permute-start | bytes 2359304 | tf_op jit(solution)/shard_map/ppermute | solution.py:1004
  210.0 16.7 %collective-permute-start.17 = (bf16[384,2432]{1,0:T(8,128)(2,1)}, bf16[384,2432]{1,0:T(8,128)(2,1)}, u32[]{:S(2)}, u32[]{:S(2)}) collective-permute-start(bf16[384,2432]{1,0:T(8,128)(2,1)} %get-tuple-element.139), channel_id=1, source_target_pairs={{0,1},{1,0},{2,3},{3,2},{4,5},{5,4},{6,7},{7,6},{8,9},{9,8},{10,11... | collective-permute-start | bytes 5603336 | tf_op jit(solution)/shard_map/ppermute | solution.py:973
  212.7 14.1 %collective-permute-start.15 = (bf16[256,768]{1,0:T(8,128)(2,1)}, bf16[256,768]{1,0:T(8,128)(2,1)}, u32[]{:S(2)}, u32[]{:S(2)}) collective-permute-start(bf16[256,768]{1,0:T(8,128)(2,1)} %get-tuple-element.242), channel_id=1, source_target_pairs={{0,8},{1,9},{2,10},{3,11},{4,12},{5,13},{6,14},{7,15},{8,0},{9,1},... | collective-permute-start | bytes 1179656 | tf_op jit(solution)/shard_map/ppermute | solution.py:1004
  213.2 13.5 %collective-permute-start.16 = (bf16[96,1536]{1,0:T(8,128)(2,1)S(1)}, bf16[96,1536]{1,0:T(8,128)(2,1)S(1)}, u32[]{:S(2)}, u32[]{:S(2)}) collective-permute-start(bf16[96,1536]{1,0:T(8,128)(2,1)S(1)} %get-tuple-element.244), channel_id=1, source_target_pairs={{0,2},{1,5},{2,0},{3,7},{4,6},{5,1},{6,4},{7,3},{8,10},{9,13},{10,... | collective-permute-start | bytes 884744 | tf_op jit(solution)/shard_map/ppermute | solution.py:1004
  230.9 25.4 %collective-permute-start.20 = (bf16[192,2432]{1,0:T(8,128)(2,1)}, bf16[192,2432]{1,0:T(8,128)(2,1)}, u32[]{:S(2)}, u32[]{:S(2)}) collective-permute-start(bf16[192,2432]{1,0:T(8,128)(2,1)} %get-tuple-element.226), channel_id=1, source_target_pairs={{0,4},{1,3},{2,6},{3,1},{4,0},{5,7},{6,2},{7,5},{8,12},{9,11},{10,... | collective-permute-start | bytes 2801672 | tf_op jit(solution)/shard_map/ppermute | solution.py:1004
  232.8 22.8 %collective-permute-start.18 = (bf16[128,768]{1,0:T(8,128)(2,1)}, bf16[128,768]{1,0:T(8,128)(2,1)}, u32[]{:S(2)}, u32[]{:S(2)}) collective-permute-start(bf16[128,768]{1,0:T(8,128)(2,1)} %get-tuple-element.248), channel_id=1, source_target_pairs={{0,16},{1,17},{2,18},{3,19},{4,20},{5,21},{6,22},{7,23},{8,24},{9,... | collective-permute-start | bytes 589832 | tf_op jit(solution)/shard_map/ppermute | solution.py:1004
  235.5 20.2 %all-to-all-start.1 = ((f32[32,2,768]{2,1,0:T(2,128)}), f32[32,2,768]{2,1,0:T(2,128)S(1)}, u32[]{:S(2)}, u32[]{:S(2)}) async-start(f32[32,2,768]{2,1,0:T(2,128)} %broadcast_in_dim.36), calls=%async_computation.1 | async-start | bytes 393216 | tf_op jit(solution)/shard_map/all_to_all | solution.py:1072
  238.9 16.8 %collective-permute-start.19 = (bf16[48,1536]{1,0:T(8,128)(2,1)S(1)}, bf16[48,1536]{1,0:T(8,128)(2,1)S(1)}, u32[]{:S(2)}, u32[]{:S(2)}) collective-permute-start(bf16[48,1536]{1,0:T(8,128)(2,1)S(1)} %get-tuple-element.250), channel_id=1, source_target_pairs={{0,16},{1,17},{2,18},{3,19},{4,20},{5,21},{6,22},{7,23},{8,24},{9,... | collective-permute-start | bytes 442376 | tf_op jit(solution)/shard_map/ppermute | solution.py:1004
  258.5 19.5 %collective-permute-start.23 = (bf16[96,2432]{1,0:T(8,128)(2,1)}, bf16[96,2432]{1,0:T(8,128)(2,1)}, u32[]{:S(2)}, u32[]{:S(2)}) collective-permute-start(bf16[96,2432]{1,0:T(8,128)(2,1)} %get-tuple-element.232), channel_id=1, source_target_pairs={{0,2},{1,5},{2,0},{3,7},{4,6},{5,1},{6,4},{7,3},{8,10},{9,13},{10,... | collective-permute-start | bytes 1400840 | tf_op jit(solution)/shard_map/ppermute | solution.py:1004
  259.8 18.2 %collective-permute-start.21 = (bf16[128,768]{1,0:T(8,128)(2,1)S(1)}, bf16[128,768]{1,0:T(8,128)(2,1)S(1)}, u32[]{:S(2)}, u32[]{:S(2)}) collective-permute-start(bf16[128,768]{1,0:T(8,128)(2,1)S(1)} %add_convert_fusion.18), channel_id=1, source_target_pairs={{0,16},{1,17},{2,18},{3,19},{4,20},{5,21},{6,22},{7,23},{8,24},{9,... | collective-permute-start | bytes 589832 | tf_op jit(solution)/shard_map/ppermute | solution.py:1004
  260.0 34.2 %all-to-all-start.2 = ((bf16[4,288,768]{2,1,0:T(8,128)(2,1)}), bf16[4,288,768]{2,1,0:T(8,128)(2,1)S(1)}, u32[]{:S(2)}, u32[]{:S(2)}) async-start(bf16[4,288,768]{2,1,0:T(8,128)(2,1)} %unsort.3), calls=%async_computation.2 | async-start | bytes 3538944 | tf_op jit(solution)/shard_map/all_to_all | solution.py:1084
  263.6 14.4 %collective-permute-start.22 = (bf16[48,1536]{1,0:T(8,128)(2,1)S(1)}, bf16[48,1536]{1,0:T(8,128)(2,1)S(1)}, u32[]{:S(2)}, u32[]{:S(2)}) collective-permute-start(bf16[48,1536]{1,0:T(8,128)(2,1)S(1)} %add_convert_fusion.21), channel_id=1, source_target_pairs={{0,16},{1,17},{2,18},{3,19},{4,20},{5,21},{6,22},{7,23},{8,24},{9,... | collective-permute-start | bytes 442376 | tf_op jit(solution)/shard_map/ppermute | solution.py:1004
  278.0 15.4 %collective-permute-start.25 = (bf16[96,1536]{1,0:T(8,128)(2,1)S(1)}, bf16[96,1536]{1,0:T(8,128)(2,1)S(1)}, u32[]{:S(2)}, u32[]{:S(2)}) collective-permute-start(bf16[96,1536]{1,0:T(8,128)(2,1)S(1)} %pad_maximum_fusion.7), channel_id=1, source_target_pairs={{0,2},{1,5},{2,0},{3,7},{4,6},{5,1},{6,4},{7,3},{8,10},{9,13},{10,... | collective-permute-start | bytes 884744 | tf_op jit(solution)/shard_map/ppermute | solution.py:1004
  278.9 15.2 %collective-permute-start.24 = (bf16[256,768]{1,0:T(8,128)(2,1)S(1)}, bf16[256,768]{1,0:T(8,128)(2,1)S(1)}, u32[]{:S(2)}, u32[]{:S(2)}) collective-permute-start(bf16[256,768]{1,0:T(8,128)(2,1)S(1)} %pad_maximum_fusion.6), channel_id=1, source_target_pairs={{0,8},{1,9},{2,10},{3,11},{4,12},{5,13},{6,14},{7,15},{8,0},{9,1},... | collective-permute-start | bytes 1179656 | tf_op jit(solution)/shard_map/ppermute | solution.py:1004
  296.3 17.8 %collective-permute-start.27 = (bf16[512,768]{1,0:T(8,128)(2,1)S(1)}, bf16[512,768]{1,0:T(8,128)(2,1)}, u32[]{:S(2)}, u32[]{:S(2)}) collective-permute-start(bf16[512,768]{1,0:T(8,128)(2,1)S(1)} %pad_maximum_fusion.3), channel_id=1, source_target_pairs={{0,2},{1,5},{2,0},{3,7},{4,6},{5,1},{6,4},{7,3},{8,10},{9,13},{10,... | collective-permute-start | bytes 2359304 | tf_op jit(solution)/shard_map/ppermute | solution.py:1004
  296.7 15.7 %collective-permute-start.28 = (bf16[192,1536]{1,0:T(8,128)(2,1)S(1)}, bf16[192,1536]{1,0:T(8,128)(2,1)}, u32[]{:S(2)}, u32[]{:S(2)}) collective-permute-start(bf16[192,1536]{1,0:T(8,128)(2,1)S(1)} %pad_maximum_fusion.4), channel_id=1, source_target_pairs={{0,4},{1,3},{2,6},{3,1},{4,0},{5,7},{6,2},{7,5},{8,12},{9,11},{10,... | collective-permute-start | bytes 1769480 | tf_op jit(solution)/shard_map/ppermute | solution.py:1004
  315.6 31.2 %collective-permute-start.30 = (bf16[1024,768]{1,0:T(8,128)(2,1)S(1)}, bf16[1024,768]{1,0:T(8,128)(2,1)}, u32[]{:S(2)}, u32[]{:S(2)}) collective-permute-start(bf16[1024,768]{1,0:T(8,128)(2,1)S(1)} %pad_maximum_fusion.refs_0_), channel_id=1, source_target_pairs={{0,4},{1,3},{2,6},{3,1},{4,0},{5,7},{6,2},{7,5},{8,12},{9,11},{10,... | collective-permute-start | bytes 4718600 | tf_op jit(solution)/shard_map/ppermute | solution.py:1004
  318.5 28.4 %collective-permute-start.31 = (bf16[384,1536]{1,0:T(8,128)(2,1)}, bf16[384,1536]{1,0:T(8,128)(2,1)}, u32[]{:S(2)}, u32[]{:S(2)}) collective-permute-start(bf16[384,1536]{1,0:T(8,128)(2,1)} %pad_maximum_fusion.1.refs_0_), channel_id=1, source_target_pairs={{0,8},{1,9},{2,10},{3,11},{4,12},{5,13},{6,14},{7,15},{8,0},{9,1},... | collective-permute-start | bytes 3538952 | tf_op jit(solution)/shard_map/ppermute | solution.py:1004
  319.1 25.8 %collective-permute-start.32 = (bf16[24,2432]{1,0:T(8,128)(2,1)S(1)}, bf16[24,2432]{1,0:T(8,128)(2,1)S(1)}, u32[]{:S(2)}, u32[]{:S(2)}) collective-permute-start(bf16[24,2432]{1,0:T(8,128)(2,1)S(1)} %add_convert_fusion.24), channel_id=1, source_target_pairs={{0,16},{1,17},{2,18},{3,19},{4,20},{5,21},{6,22},{7,23},{8,24},{9,... | collective-permute-start | bytes 350216 | tf_op jit(solution)/shard_map/ppermute | solution.py:1004
  321.7 30.1 %collective-permute-start.33 = (bf16[1024,768]{1,0:T(8,128)(2,1)S(1)}, bf16[1024,768]{1,0:T(8,128)(2,1)}, u32[]{:S(2)}, u32[]{:S(2)}) collective-permute-start(bf16[1024,768]{1,0:T(8,128)(2,1)S(1)} %pad_maximum_fusion.refs_0_), channel_id=1, source_target_pairs={{0,1},{1,0},{2,3},{3,2},{4,5},{5,4},{6,7},{7,6},{8,9},{9,8},{10,11... | collective-permute-start | bytes 4718600 | tf_op jit(solution)/shard_map/ppermute | solution.py:973
  365.7 13.6 %collective-permute-start.39 = (bf16[192,2432]{1,0:T(8,128)(2,1)S(1)}, bf16[192,2432]{1,0:T(8,128)(2,1)S(1)}, u32[]{:S(2)}, u32[]{:S(2)}) collective-permute-start(bf16[192,2432]{1,0:T(8,128)(2,1)S(1)} %pad_maximum_fusion.2.refs_0_), channel_id=1, source_target_pairs={{0,4},{1,3},{2,6},{3,1},{4,0},{5,7},{6,2},{7,5},{8,12},{9,11},{10,... | collective-permute-start | bytes 2801672 | tf_op jit(solution)/shard_map/ppermute | solution.py:1004
  (51 other events, 318.5 us)
where the time goes:
time: 401 us; the launch traced here: 393 us
  Pallas kernels  194 us (48%)
  waiting for transfers between devices  88.5 us (22%)
  starting transfers between devices  52.2 us (13%)
  other arithmetic  40 us (10%)
  local copies, waits for them, and re-layouts  16.5 us (4%)
    ppermute x24, waiting for transfers between devices, swap_two(): return lax.ppermute(value, ('rows', 'blk'), pairs)  68.6 us
    pallas_call x1, Pallas kernels, mlp_call(): pl.pallas_call(functools.partial(mlp_kernel, parts), grid_spec=pltpu.Pref...  59.7 us
    ppermute x24, starting transfers between devices, swap_two(): return lax.ppermute(value, ('rows', 'blk'), pairs)  32.9 us
    pallas_call x1, Pallas kernels, backward_call(): pl.pallas_call(backward_kernel, grid_spec=pltpu.PrefetchScalarGridSpec(nu...  31.9 us
    convert_element_type x15, other arithmetic, add_low(): return (a.astype(F32) + b.astype(F32)).astype(BF16)  29 us
    pallas_call x3, Pallas kernels, final_call(): pl.pallas_call(kernel, grid_spec=pltpu.PrefetchScalarGridSpec(num_scalar_...  23.7 us
    ppermute x18, waiting for transfers between devices, swap(): lax.ppermute(value, axis, [(i, i ^ bit) for i in range(lax.axis_size(axis...  19.9 us
    pallas_call x1, Pallas kernels, forward_call(): pl.pallas_call(forward_kernel, grid_spec=pltpu.PrefetchScalarGridSpec(num...  15.5 us
  transfers between devices with their start and end apart: 45, of which 16 were waited for; matrix products, arithmetic and copies ran while one was open for 7% of the time, Pallas kernels for 30%

commit v1 on v0

--- a/solution.py
+++ b/solution.py
@@ -123,7 +123,7 @@
     return (place >= first) & (place < last)
 
 
-def forward_kernel(starts, qkv, out, stat):
+def forward_kernel(starts, qkv, out, stat, low_out):
     length = qkv.shape[1]
     for seg in range(5):
         first, last, small, at_q, at_k = windows(starts, seg, length)
@@ -157,6 +157,7 @@
         mine = inside(at_q, small, PAIR, first, last)
         out[rows_q, :] = jnp.where(mine, both[:, :PAIR] / total, out[rows_q, :])
         stat[rows_q, :] = jnp.where(mine, peak + jnp.log(total), stat[rows_q, :])
+    low_out[...] = out[...].astype(BF16)
 
 
 def forward_call(starts, qkv):
@@ -168,12 +169,9 @@
             num_scalar_prefetch=1,
             grid=(pairs,),
             in_specs=[pl.BlockSpec((3, count, PAIR), lambda p, s: (0, 0, p))],
-            out_specs=[
-                pl.BlockSpec((count, PAIR), lambda p, s: (0, p)),
-                pl.BlockSpec((count, PAIR), lambda p, s: (0, p)),
-            ],
+            out_specs=[pl.BlockSpec((count, PAIR), lambda p, s: (0, p))] * 3,
         ),
-        out_shape=[jax.ShapeDtypeStruct((count, pairs * PAIR), F32)] * 2,
+        out_shape=[jax.ShapeDtypeStruct((count, pairs * PAIR), dtype) for dtype in (F32, F32, BF16)],
         compiler_params=pltpu.CompilerParams(vmem_limit_bytes=VMEM),
         cost_estimate=QUICK,
         name="attention_forward",
@@ -275,33 +273,32 @@
     )(starts, qkv, grad, att, stat, *held)
 
 
-ERF = (0.254829592, -0.284496736, 1.421413741, -1.453152027, 1.061405429)
+HALF_ERF = tuple(0.5 * c for c in (0.254829592, -0.284496736, 1.421413741, -1.453152027, 1.061405429))
+LOG2_E = 1.4426950408889634
 
 
 def gelu_pair(u):
     size = jnp.abs(u)
     t = 1.0 / (1.0 + (0.3275911 * 0.5**0.5) * size)
-    bell = jnp.exp(u * u * -0.5)
-    poly = ERF[4] * t + ERF[3]
-    for c in (ERF[2], ERF[1], ERF[0]):
+    bell = jnp.exp2(u * u * (-0.5 * LOG2_E))
+    poly = HALF_ERF[4] * t + HALF_ERF[3]
+    for c in (HALF_ERF[2], HALF_ERF[1], HALF_ERF[0]):
         poly = poly * t + c
-    tail = 0.5 * poly * t * bell
+    tail = poly * t * bell
     phi = jnp.where(u < 0, tail, 1.0 - tail)
     return u * phi, phi + u * bell * 0.3989422804014327
 
 
 def middle_kernel(n, tile, *refs):
     keep, rank, *pieces = refs[: n + 2]
-    att, xs, out_w, vectors, cot_out, att_low_out, middle_out, normed_out, mlp_out, sums, row = refs[n + 2 :]
+    att, xs, out_w, vectors, cot_out, middle_out, normed_out, mlp_out, sums, row = refs[n + 2 :]
     step = pl.program_id(0)
     gather_pieces(step, pieces, row)
     cot = sort_tile(rank[...], tile, step, row)
     cot_out[...] = cot.astype(BF16)
     mlp_grad = (cot * keep[1]).astype(BF16)
     mlp_out[...] = mlp_grad
-    att_low = att[...].astype(BF16)
-    att_low_out[...] = att_low
-    middle = xs[...].astype(F32) + keep[0] * (dot(att_low, out_w[...]) + vectors[0:1, :])
+    middle = xs[...].astype(F32) + keep[0] * (dot(att[...], out_w[...]) + vectors[0:1, :])
     middle_out[...] = middle
     hat, _ = centre_scale(middle)
     normed_out[...] = (hat * vectors[1:2, :] + vectors[2:3, :]).astype(BF16)
@@ -325,8 +322,8 @@
         in_specs=[pl.BlockSpec(memory_space=pltpu.SMEM), whole((1, count))]
         + [whole((span, width))] * n
         + [rows, rows, whole(out_w.shape), whole(vectors.shape)],
-        out_specs=[rows] * 5 + [pl.BlockSpec((8, width), lambda i: (0, 0))],
-        out_shape=[low, low, full, low, low, jax.ShapeDtypeStruct((8, width), F32)],
+        out_specs=[rows] * 4 + [pl.BlockSpec((8, width), lambda i: (0, 0))],
+        out_shape=[low, full, low, low, jax.ShapeDtypeStruct((8, width), F32)],
         scratch_shapes=[pltpu.VMEM((count, width), BF16)],
         compiler_params=pltpu.CompilerParams(vmem_limit_bytes=VMEM),
         cost_estimate=QUICK,
@@ -1130,7 +1127,7 @@
         swap(row_piece(after(image_index, *xs_send), s), "blk", s) for s in range(1, blocks)
     ]
     cots = [row_piece(cotangent, 0)] + [
-        swap(after(row_piece(cotangent, s), *xs_in), "blk", s) for s in range(1, blocks)
+        swap(after(row_piece(cotangent, s), *xs_send), "blk", s) for s in range(1, blocks)
     ]
     ids = jnp.concatenate(ids)
     image = jnp.where(ids < 0, 4, ids)
@@ -1143,11 +1140,11 @@
 
     bias = jnp.stack([input_bias[0], jnp.zeros_like(input_bias[0]), input_bias[1]])
     xs, normed, qkv = qkv_call(rank_row, xs_in, first_gain[None], first_shift[None], input_weight, bias)
-    attended, stat = forward_call(starts, qkv)
+    attended, stat, att_low = forward_call(starts, qkv)
     vectors = jnp.stack([output_bias, second_gain, second_shift, down_bias])
     core = side("blk", 1).astype(jnp.int32).reshape(1)
-    cot, att_low, middle, normed2, mlp_grad, sums_mid = middle_call(
-        keep, rank_row, cots, attended, xs, output_weight, vectors
+    cot, middle, normed2, mlp_grad, sums_mid = middle_call(
+        keep, rank_row, cots, att_low, xs, output_weight, vectors
     )
     (up_send, up_keep, down_send, down_keep, up_sums, result, middle_grad, branch, att_grad, sums2) = mlp_call(
         core, keep, normed2, mlp_grad, middle, cot, att_low, output_weight, vectors, up_weight, up_bias[None], down_weight

time: 401 us -> 398 us (level)
    ppermute x18, waiting for transfers between devices: 19.9 us -> 13.2 us  [swap(): lax.ppermute(value, axis, [(i, i ^ bit) for i in range(lax.axis_size(axis...]
  transfers between devices with their start and end apart: 45 -> 45, of which waited for: 16 -> 17; matrix products, arithmetic and copies ran while one was open for 7% -> 7% of each run, Pallas kernels for 30% -> 30%
where the time goes in v1:
time: 398 us; the launch traced here: 391 us
  Pallas kernels  193 us (48%)
  waiting for transfers between devices  85.3 us (21%)
  starting transfers between devices  52.6 us (13%)
  other arithmetic  40 us (10%)
  local copies, waits for them, and re-layouts  18.2 us (5%)
    ppermute x24, waiting for transfers between devices, swap_two(): return lax.ppermute(value, ('rows', 'blk'), pairs)  72 us
    pallas_call x1, Pallas kernels, mlp_call(): pl.pallas_call(functools.partial(mlp_kernel, parts), grid_spec=pltpu.Pref...  58.8 us
    ppermute x24, starting transfers between devices, swap_two(): return lax.ppermute(value, ('rows', 'blk'), pairs)  33.5 us
    pallas_call x1, Pallas kernels, backward_call(): pl.pallas_call(backward_kernel, grid_spec=pltpu.PrefetchScalarGridSpec(nu...  32.3 us
    convert_element_type x15, other arithmetic, add_low(): return (a.astype(F32) + b.astype(F32)).astype(BF16)  29 us
    pallas_call x3, Pallas kernels, final_call(): pl.pallas_call(kernel, grid_spec=pltpu.PrefetchScalarGridSpec(num_scalar_...  23.7 us
    pallas_call x1, Pallas kernels, forward_call(): pl.pallas_call(forward_kernel, grid_spec=pltpu.PrefetchScalarGridSpec(num...  16.1 us
    ppermute x18, waiting for transfers between devices, swap(): lax.ppermute(value, axis, [(i, i ^ bit) for i in range(lax.axis_size(axis...  13.2 us
  transfers between devices with their start and end apart: 45, of which 17 were waited for; matrix products, arithmetic and copies ran while one was open for 7% of the time, Pallas kernels for 30%

profile of v1, /device:TPU:0, one launch (start us, length us, event | category | flops | bytes accessed | tf_op | source)
XLA Modules:
  0.0 391.0 jit_solution(761577425774525882)
XLA Ops:
  13.4 4.2 %collective-permute-done.1 = s32[288]{0:T(512)S(1)} collective-permute-done((s32[288]{0:T(512)S(1)}, s32[288]{0:T(512)S(1)}, u32[]{:S(2)}, u32[]{:S(2)}) %collective-permute-start.1) | collective-permute-done | bytes 1184 | tf_op jit(solution)/shard_map/ppermute | solution.py:970
  22.3 4.4 %collective-permute-done.8.refs_4_ = bf16[288,768]{1,0:T(8,128)(2,1)S(1)} collective-permute-done((bf16[288,768]{1,0:T(8,128)(2,1)S(1)}, bf16[288,768]{1,0:T(8,128)(2,1)S(1)}, u32[]{:S(2)}, u32[]{:S(2)}) %collective-permute-start.8) | collective-permute-done | bytes 442400 | tf_op jit(solution)/shard_map/ppermute | solution.py:970
  27.5 13.1 %sort_qkv.1 = (bf16[1152,768]{1,0:T(8,128)(2,1)}, bf16[1152,768]{1,0:T(8,128)(2,1)}, bf16[3,1152,768]{2,1,0:T(8,128)(2,1)}) custom-call(s32[1,1152]{1,0:T(1,128)} %broadcast_in_dim.31.refs_0_.refs_1_, bf16[288,768]{1,0:T(8,128)(2,1)} %get-tuple-element.239.refs_1_, bf16[288,768]{1,0:T(8,128)(2,1)} %copy-done.17, bf16[288,768]{1,0:T(8,128)(2,1)} %copy-done.18, ...), custom_call_target="tpu_custom_call" | custom-call | flops 1048576 | bytes 65536 | tf_op jit(solution)/shard_map/sort_qkv/pallas_call | solution.py:85
  40.6 16.1 %attention_forward.1 = (f32[1152,768]{1,0:T(8,128)}, f32[1152,768]{1,0:T(8,128)}, bf16[1152,768]{1,0:T(8,128)(2,1)}) custom-call(s32[6]{0:T(128)} %convert_reduce_fusion.1.starts, bf16[3,1152,768]{2,1,0:T(8,128)(2,1)} %get-tuple-element.103.qkv), custom_call_target="tpu_custom_call" | custom-call | flops 1048576 | bytes 65536 | tf_op jit(solution)/shard_map/attention_forward/pallas_call | solution.py:166
  56.7 9.7 %middle.1 = (bf16[1152,768]{1,0:T(8,128)(2,1)}, f32[1152,768]{1,0:T(8,128)}, bf16[1152,768]{1,0:T(8,128)(2,1)}, bf16[1152,768]{1,0:T(8,128)(2,1)}, f32[8,768]{1,0:T(8,128)}) custom-call(f32[2]{0:T(128)} %fusion.6.refs_0_.keep, s32[1,1152]{1,0:T(1,128)} %broadcast_in_dim.31.refs_0_.refs_1_, bf16[288,768]{1,0:T(8,128)(2,1)} %get-tuple-element.235.refs_2_, ...), custom_call_target="tpu_custom_call" | custom-call | flops 1048576 | bytes 65536 | tf_op jit(solution)/shard_map/middle/pallas_call | solution.py:319
  66.4 58.8 %mlp.1 = (bf16[768,1536]{1,0:T(8,128)(2,1)}, bf16[768,1536]{1,0:T(8,128)(2,1)}, bf16[2048,768]{1,0:T(8,128)(2,1)}, bf16[2048,768]{1,0:T(8,128)(2,1)}, f32[1,3072...) custom-call(s32[1]{0:T(128)} %bitcast.core.c, ...), custom_call_target="tpu_custom_call" | custom-call | flops 1048576 | bytes 65536 | tf_op jit(solution)/shard_map/mlp/pallas_call | solution.py:422
  127.1 6.0 %unsort.2 = bf16[4,288,768]{2,1,0:T(8,128)(2,1)} custom-call(s32[1]{0:T(128)} %bitcast.10.me, s32[1152,1]{1,0:T(8,128)} %broadcast_in_dim.37.rank, bf16[1152,768]{1,0:T(8,128)(2,1)} %get-tuple-element.118.source), custom_call_target="tpu_custom_call" | custom-call | flops 1048576 | bytes 65536 | tf_op jit(solution)/shard_map/unsort/pallas_call | solution.py:502
  134.9 5.3 %add_convert_fusion = (bf16[1024,768]{1,0:T(8,128)(2,1)}, bf16[1024,768]{1,0:T(8,128)(2,1)}) fusion(bf16[2048,768]{1,0:T(8,128)(2,1)} %collective-permute-done.9, s32[]{:T(128)S(6)} %select_n.383, bf16[2048,768]{1,0:T(8,128)(2,1)} %get-tuple-element.110, s32[]{:T(128)S(6)} %select_n.379), kind=kLoop, calls=%fused_computation.1 | loop fusion | flops 6291456 | bytes 9437192 | tf_op jit(solution)/shard_map/convert_element_type | solution.py:990
  142.0 3.6 all-to-all-start
  145.6 4.3 %add_convert_fusion.2 = (bf16[384,1536]{1,0:T(8,128)(2,1)}, bf16[384,1536]{1,0:T(8,128)(2,1)}) fusion(bf16[768,1536]{1,0:T(8,128)(2,1)} %collective-permute-done.10, s32[]{:T(128)S(6)} %select_n.384, bf16[768,1536]{1,0:T(8,128)(2,1)} %get-tuple-element.117, s32[]{:T(128)S(6)} %select_n.382), kind=kLoop, calls=%fused_computation.3 | loop fusion | flops 4718592 | bytes 7077896 | tf_op jit(solution)/shard_map/convert_element_type | solution.py:990
  151.3 32.3 %attention_backward.1 = (bf16[3,1152,768]{2,1,0:T(8,128)(2,1)}, f32[8,768]{1,0:T(8,128)}) custom-call(s32[6]{0:T(128)} %convert_reduce_fusion.1.starts, bf16[3,1152,768]{2,1,0:T(8,128)(2,1)} %get-tuple-element.103.qkv, bf16[1152,768]{1,0:T(8,128)(2,1)} %get-tuple-element.122.grad, f32[1152,768]{1,0:T(8,128)} %get-tuple-element.123.att, ...), custom_call_target="tpu_custom_call" | custom-call | flops 1048576 | bytes 65536 | tf_op jit(solution)/shard_map/attention_backward/pallas_call | solution.py:252
  183.7 4.0 %add_convert_fusion.7 = (bf16[512,768]{1,0:T(8,128)(2,1)}, bf16[512,768]{1,0:T(8,128)(2,1)}) fusion(bf16[1024,768]{1,0:T(8,128)(2,1)} %collective-permute-done.11, s32[]{:T(128)S(6)} %select_n.386, bf16[1024,768]{1,0:T(8,128)(2,1)} %get-tuple-element.221, s32[]{:T(128)S(6)} %select_n.388), kind=kLoop, calls=%fused_computation.9 | loop fusion | flops 3145728 | bytes 4718600 | tf_op jit(solution)/shard_map/convert_element_type | solution.py:990
  192.7 9.8 %input_weights.1 = (bf16[384,2432]{1,0:T(8,128)(2,1)}, bf16[384,2432]{1,0:T(8,128)(2,1)}) custom-call(s32[1]{0:T(128)} %bitcast.core.c, bf16[1152,768]{1,0:T(8,128)(2,1)} %get-tuple-element.130.normed, bf16[3,1152,768]{2,1,0:T(8,128)(2,1)} %get-tuple-element.125.grads, f32[8,768]{1,0:T(8,128)} %get-tuple-element.131.first, ...), custom_call_target="tpu_custom_call" | custom-call | flops 1048576 | bytes 65536 | tf_op jit(solution)/shard_map/input_weights/pallas_call | solution.py:543
  202.5 3.0 collective-permute-done.14
  211.0 10.6 %input_backward.1 = (bf16[1152,768]{1,0:T(8,128)(2,1)}, f32[8,768]{1,0:T(8,128)}) custom-call(bf16[3,1152,768]{2,1,0:T(8,128)(2,1)} %get-tuple-element.125.grads, bf16[768,2304]{1,0:T(8,128)(2,1)} %weight.1, bf16[1152,768]{1,0:T(8,128)(2,1)} %get-tuple-element.105.refs_7_.xs, f32[1152,768]{1,0:T(8,128)} %get-tuple-element.141.middle_grad, ...), custom_call_target="tpu_custom_call" | custom-call | flops 1048576 | bytes 65536 | tf_op jit(solution)/shard_map/input_backward/pallas_call | solution.py:475
  223.1 3.4 add_convert_fusion.4
  237.3 5.9 %unsort.3 = bf16[4,288,768]{2,1,0:T(8,128)(2,1)} custom-call(s32[1]{0:T(128)} %bitcast.10.me, s32[1152,1]{1,0:T(8,128)} %broadcast_in_dim.37.rank, bf16[1152,768]{1,0:T(8,128)(2,1)} %get-tuple-element.148.source), custom_call_target="tpu_custom_call" | custom-call | flops 1048576 | bytes 65536 | tf_op jit(solution)/shard_map/unsort/pallas_call | solution.py:502
  243.2 8.6 %collective-permute-done.19 = bf16[48,1536]{1,0:T(8,128)(2,1)S(1)} collective-permute-done((bf16[48,1536]{1,0:T(8,128)(2,1)S(1)}, bf16[48,1536]{1,0:T(8,128)(2,1)S(1)}, u32[]{:S(2)}, u32[]{:S(2)}) %collective-permute-start.19) | collective-permute-done | bytes 147488 | tf_op jit(solution)/shard_map/ppermute | solution.py:1001
  256.0 3.6 all-to-all-start.2
  263.3 10.3 %collective-permute-done.22 = bf16[48,1536]{1,0:T(8,128)(2,1)S(1)} collective-permute-done((bf16[48,1536]{1,0:T(8,128)(2,1)S(1)}, bf16[48,1536]{1,0:T(8,128)(2,1)S(1)}, u32[]{:S(2)}, u32[]{:S(2)}) %collective-permute-start.22) | collective-permute-done | bytes 147488 | tf_op jit(solution)/shard_map/ppermute | solution.py:1001
  278.0 12.2 %collective-permute-done.26 = bf16[48,2432]{1,0:T(8,128)(2,1)S(1)} collective-permute-done((bf16[48,2432]{1,0:T(8,128)(2,1)S(1)}, bf16[48,2432]{1,0:T(8,128)(2,1)S(1)}, u32[]{:S(2)}, u32[]{:S(2)}) %collective-permute-start.26) | collective-permute-done | bytes 233504 | tf_op jit(solution)/shard_map/ppermute | solution.py:1001
  296.6 5.4 %collective-permute-done.29 = bf16[24,2432]{1,0:T(8,128)(2,1)S(1)} collective-permute-done((bf16[24,2432]{1,0:T(8,128)(2,1)S(1)}, bf16[24,2432]{1,0:T(8,128)(2,1)S(1)}, u32[]{:S(2)}, u32[]{:S(2)}) %collective-permute-start.29) | collective-permute-done | bytes 116768 | tf_op jit(solution)/shard_map/ppermute | solution.py:1001
  302.0 7.0 %collective-permute-done.28 = bf16[192,1536]{1,0:T(8,128)(2,1)} collective-permute-done((bf16[192,1536]{1,0:T(8,128)(2,1)S(1)}, bf16[192,1536]{1,0:T(8,128)(2,1)}, u32[]{:S(2)}, u32[]{:S(2)}) %collective-permute-start.28) | collective-permute-done | bytes 589856 | tf_op jit(solution)/shard_map/ppermute | solution.py:1001
  315.4 3.3 collective-permute-start.32
  318.7 3.6 copy.47
  322.3 3.6 copy.48
  326.0 15.6 %collective-permute-done.32 = bf16[24,2432]{1,0:T(8,128)(2,1)S(1)} collective-permute-done((bf16[24,2432]{1,0:T(8,128)(2,1)S(1)}, bf16[24,2432]{1,0:T(8,128)(2,1)S(1)}, u32[]{:S(2)}, u32[]{:S(2)}) %collective-permute-start.32) | collective-permute-done | bytes 116768 | tf_op jit(solution)/shard_map/ppermute | solution.py:1001
  343.8 3.6 collective-permute-start.37
  348.2 5.5 %collective-permute-done.37 = bf16[48,2432]{1,0:T(8,128)(2,1)S(1)} collective-permute-done((bf16[48,2432]{1,0:T(8,128)(2,1)S(1)}, bf16[48,2432]{1,0:T(8,128)(2,1)S(1)}, u32[]{:S(2)}, u32[]{:S(2)}) %collective-permute-start.37) | collective-permute-done | bytes 233504 | tf_op jit(solution)/shard_map/ppermute | solution.py:1001
  356.7 7.0 %up_final.1 = f32[768,3072]{1,0:T(8,128)} custom-call(s32[1]{0:T(128)} %bitcast.core.c, s32[2]{0:T(128)} %pad_add_fusion.1.t, bf16[384,1536]{1,0:T(8,128)(2,1)} %pad_maximum_fusion.1.refs_0_, bf16[384,1536]{1,0:T(8,128)(2,1)} %collective-permute-done.31.refs_1_, bf16[384,1536]{1,0:T(8,128)(2,1)} %copy-done.10, bf16[384,1536]{1,0:T(8,128)(2,1)} %copy-done.11), custom_call_target="tpu_custom_call" | custom-call | flops 1048576 | bytes 65536 | tf_op jit(solution)/shard_map/up_final/pallas_call | solution.py:590
  364.7 10.6 %down_final.1 = (f32[3072,768]{1,0:T(8,128)}, f32[768,768]{1,0:T(8,128)}) custom-call(s32[1]{0:T(128)} %bitcast.core.c, s32[2]{0:T(128)} %pad_add_fusion.t, bf16[1024,768]{1,0:T(8,128)(2,1)} %copy-done.2, bf16[1024,768]{1,0:T(8,128)(2,1)} %collective-permute-done.30.refs_1_, bf16[1024,768]{1,0:T(8,128)(2,1)} %collective-permute-done.33.refs_2_, ...), custom_call_target="tpu_custom_call" | custom-call | flops 1048576 | bytes 65536 | tf_op jit(solution)/shard_map/down_final/pallas_call | solution.py:590
  380.0 6.1 %input_final.1 = (f32[768,2304]{1,0:T(8,128)}, f32[768,128]{1,0:T(8,128)}) custom-call(s32[1]{0:T(128)} %bitcast.core.c, s32[2]{0:T(128)} %pad_add_fusion.t, bf16[192,2432]{1,0:T(8,128)(2,1)} %copy-done.4, bf16[192,2432]{1,0:T(8,128)(2,1)} %copy-done.14, bf16[192,2432]{1,0:T(8,128)(2,1)} %collective-permute-done.40.refs_2_, ...), custom_call_target="tpu_custom_call" | custom-call | flops 1048576 | bytes 65536 | tf_op jit(solution)/shard_map/input_final/pallas_call | solution.py:590
  (207 shorter events, 88.8 us)
Async XLA Ops:
  3.3 16.9 %collective-permute-start.6 = (bf16[288,768]{1,0:T(8,128)(2,1)}, bf16[288,768]{1,0:T(8,128)(2,1)S(1)}, u32[]{:S(2)}, u32[]{:S(2)}) collective-permute-start(bf16[288,768]{1,0:T(8,128)(2,1)} %get-tuple-element.238), channel_id=1, source_target_pairs={{0,1},{1,0},{2,3},{3,2},{4,5},{5,4},{6,7},{7,6},{8,9},{9,8},{10,11... | collective-permute-start | bytes 1327112 | tf_op jit(solution)/shard_map/ppermute | solution.py:970
  3.8 18.6 %collective-permute-start.7 = (bf16[288,768]{1,0:T(8,128)(2,1)}, bf16[288,768]{1,0:T(8,128)(2,1)S(1)}, u32[]{:S(2)}, u32[]{:S(2)}) collective-permute-start(bf16[288,768]{1,0:T(8,128)(2,1)} %get-tuple-element.240), channel_id=1, source_target_pairs={{0,2},{1,3},{2,0},{3,1},{4,6},{5,7},{6,4},{7,5},{8,10},{9,11},{10,... | collective-permute-start | bytes 1327112 | tf_op jit(solution)/shard_map/ppermute | solution.py:970
  12.9 13.8 %collective-permute-start.8 = (bf16[288,768]{1,0:T(8,128)(2,1)S(1)}, bf16[288,768]{1,0:T(8,128)(2,1)S(1)}, u32[]{:S(2)}, u32[]{:S(2)}) collective-permute-start(bf16[288,768]{1,0:T(8,128)(2,1)S(1)} %get-tuple-element.237), channel_id=1, source_target_pairs={{0,3},{1,2},{2,1},{3,0},{4,7},{5,6},{6,5},{7,4},{8,11},{9,10},{10,... | collective-permute-start | bytes 1327112 | tf_op jit(solution)/shard_map/ppermute | solution.py:970
  17.6 39.2 %collective-permute-start.5 = (bf16[288,768]{1,0:T(8,128)(2,1)}, bf16[288,768]{1,0:T(8,128)(2,1)}, u32[]{:S(2)}, u32[]{:S(2)}) collective-permute-start(bf16[288,768]{1,0:T(8,128)(2,1)} %get-tuple-element.102), channel_id=1, source_target_pairs={{0,3},{1,2},{2,1},{3,0},{4,7},{5,6},{6,5},{7,4},{8,11},{9,10},{10,... | collective-permute-start | bytes 1327112 | tf_op jit(solution)/shard_map/ppermute | solution.py:970
  18.5 38.3 %collective-permute-start.4 = (bf16[288,768]{1,0:T(8,128)(2,1)}, bf16[288,768]{1,0:T(8,128)(2,1)}, u32[]{:S(2)}, u32[]{:S(2)}) collective-permute-start(bf16[288,768]{1,0:T(8,128)(2,1)} %get-tuple-element.101), channel_id=1, source_target_pairs={{0,2},{1,3},{2,0},{3,1},{4,6},{5,7},{6,4},{7,5},{8,10},{9,11},{10,... | collective-permute-start | bytes 1327112 | tf_op jit(solution)/shard_map/ppermute | solution.py:970
  20.3 36.5 %collective-permute-start.3 = (bf16[288,768]{1,0:T(8,128)(2,1)}, bf16[288,768]{1,0:T(8,128)(2,1)}, u32[]{:S(2)}, u32[]{:S(2)}) collective-permute-start(bf16[288,768]{1,0:T(8,128)(2,1)} %get-tuple-element.100), channel_id=1, source_target_pairs={{0,1},{1,0},{2,3},{3,2},{4,5},{5,4},{6,7},{7,6},{8,9},{9,8},{10,11... | collective-permute-start | bytes 1327112 | tf_op jit(solution)/shard_map/ppermute | solution.py:970
  140.2 43.4 %collective-permute-start.11 = (bf16[1024,768]{1,0:T(8,128)(2,1)}, bf16[1024,768]{1,0:T(8,128)(2,1)}, u32[]{:S(2)}, u32[]{:S(2)}) collective-permute-start(bf16[1024,768]{1,0:T(8,128)(2,1)} %get-tuple-element.222), channel_id=1, source_target_pairs={{0,4},{1,3},{2,6},{3,1},{4,0},{5,7},{6,2},{7,5},{8,12},{9,11},{10,... | collective-permute-start | bytes 4718600 | tf_op jit(solution)/shard_map/ppermute | solution.py:1001
  142.0 41.7 %all-to-all-start = ((bf16[4,288,768]{2,1,0:T(8,128)(2,1)}), bf16[4,288,768]{2,1,0:T(8,128)(2,1)S(1)}, u32[]{:S(2)}, u32[]{:S(2)}) async-start(bf16[4,288,768]{2,1,0:T(8,128)(2,1)} %unsort.2), calls=%async_computation | async-start | bytes 3538944 | tf_op jit(solution)/shard_map/all_to_all | solution.py:1081
  149.9 33.7 %collective-permute-start.12 = (bf16[384,1536]{1,0:T(8,128)(2,1)}, bf16[384,1536]{1,0:T(8,128)(2,1)}, u32[]{:S(2)}, u32[]{:S(2)}) collective-permute-start(bf16[384,1536]{1,0:T(8,128)(2,1)} %get-tuple-element.224), channel_id=1, source_target_pairs={{0,8},{1,9},{2,10},{3,11},{4,12},{5,13},{6,14},{7,15},{8,0},{9,1},... | collective-permute-start | bytes 3538952 | tf_op jit(solution)/shard_map/ppermute | solution.py:1001
  187.7 18.1 %collective-permute-start.13 = (bf16[512,768]{1,0:T(8,128)(2,1)}, bf16[512,768]{1,0:T(8,128)(2,1)}, u32[]{:S(2)}, u32[]{:S(2)}) collective-permute-start(bf16[512,768]{1,0:T(8,128)(2,1)} %get-tuple-element.228), channel_id=1, source_target_pairs={{0,2},{1,5},{2,0},{3,7},{4,6},{5,1},{6,4},{7,3},{8,10},{9,13},{10,... | collective-permute-start | bytes 2359304 | tf_op jit(solution)/shard_map/ppermute | solution.py:1001
  192.0 13.6 %collective-permute-start.14 = (bf16[192,1536]{1,0:T(8,128)(2,1)}, bf16[192,1536]{1,0:T(8,128)(2,1)S(1)}, u32[]{:S(2)}, u32[]{:S(2)}) collective-permute-start(bf16[192,1536]{1,0:T(8,128)(2,1)} %get-tuple-element.230), channel_id=1, source_target_pairs={{0,4},{1,3},{2,6},{3,1},{4,0},{5,7},{6,2},{7,5},{8,12},{9,11},{10,... | collective-permute-start | bytes 1769480 | tf_op jit(solution)/shard_map/ppermute | solution.py:1001
  205.8 16.6 %collective-permute-start.17 = (bf16[384,2432]{1,0:T(8,128)(2,1)}, bf16[384,2432]{1,0:T(8,128)(2,1)}, u32[]{:S(2)}, u32[]{:S(2)}) collective-permute-start(bf16[384,2432]{1,0:T(8,128)(2,1)} %get-tuple-element.139), channel_id=1, source_target_pairs={{0,1},{1,0},{2,3},{3,2},{4,5},{5,4},{6,7},{7,6},{8,9},{9,8},{10,11... | collective-permute-start | bytes 5603336 | tf_op jit(solution)/shard_map/ppermute | solution.py:970
  208.5 13.9 %collective-permute-start.15 = (bf16[256,768]{1,0:T(8,128)(2,1)}, bf16[256,768]{1,0:T(8,128)(2,1)}, u32[]{:S(2)}, u32[]{:S(2)}) collective-permute-start(bf16[256,768]{1,0:T(8,128)(2,1)} %get-tuple-element.242), channel_id=1, source_target_pairs={{0,8},{1,9},{2,10},{3,11},{4,12},{5,13},{6,14},{7,15},{8,0},{9,1},... | collective-permute-start | bytes 1179656 | tf_op jit(solution)/shard_map/ppermute | solution.py:1001
  226.5 25.9 %collective-permute-start.20 = (bf16[192,2432]{1,0:T(8,128)(2,1)}, bf16[192,2432]{1,0:T(8,128)(2,1)}, u32[]{:S(2)}, u32[]{:S(2)}) collective-permute-start(bf16[192,2432]{1,0:T(8,128)(2,1)} %get-tuple-element.226), channel_id=1, source_target_pairs={{0,4},{1,3},{2,6},{3,1},{4,0},{5,7},{6,2},{7,5},{8,12},{9,11},{10,... | collective-permute-start | bytes 2801672 | tf_op jit(solution)/shard_map/ppermute | solution.py:1001
  228.7 23.1 %collective-permute-start.18 = (bf16[128,768]{1,0:T(8,128)(2,1)}, bf16[128,768]{1,0:T(8,128)(2,1)}, u32[]{:S(2)}, u32[]{:S(2)}) collective-permute-start(bf16[128,768]{1,0:T(8,128)(2,1)} %get-tuple-element.248), channel_id=1, source_target_pairs={{0,16},{1,17},{2,18},{3,19},{4,20},{5,21},{6,22},{7,23},{8,24},{9,... | collective-permute-start | bytes 589832 | tf_op jit(solution)/shard_map/ppermute | solution.py:1001
  231.6 20.3 %all-to-all-start.1 = ((f32[32,2,768]{2,1,0:T(2,128)}), f32[32,2,768]{2,1,0:T(2,128)S(1)}, u32[]{:S(2)}, u32[]{:S(2)}) async-start(f32[32,2,768]{2,1,0:T(2,128)} %broadcast_in_dim.36), calls=%async_computation.1 | async-start | bytes 393216 | tf_op jit(solution)/shard_map/all_to_all | solution.py:1069
  234.6 17.2 %collective-permute-start.19 = (bf16[48,1536]{1,0:T(8,128)(2,1)S(1)}, bf16[48,1536]{1,0:T(8,128)(2,1)S(1)}, u32[]{:S(2)}, u32[]{:S(2)}) collective-permute-start(bf16[48,1536]{1,0:T(8,128)(2,1)S(1)} %get-tuple-element.250), channel_id=1, source_target_pairs={{0,16},{1,17},{2,18},{3,19},{4,20},{5,21},{6,22},{7,23},{8,24},{9,... | collective-permute-start | bytes 442376 | tf_op jit(solution)/shard_map/ppermute | solution.py:1001
  254.7 19.0 %collective-permute-start.23 = (bf16[96,2432]{1,0:T(8,128)(2,1)}, bf16[96,2432]{1,0:T(8,128)(2,1)}, u32[]{:S(2)}, u32[]{:S(2)}) collective-permute-start(bf16[96,2432]{1,0:T(8,128)(2,1)} %get-tuple-element.232), channel_id=1, source_target_pairs={{0,2},{1,5},{2,0},{3,7},{4,6},{5,1},{6,4},{7,3},{8,10},{9,13},{10,... | collective-permute-start | bytes 1400840 | tf_op jit(solution)/shard_map/ppermute | solution.py:1001
  255.9 17.7 %collective-permute-start.21 = (bf16[128,768]{1,0:T(8,128)(2,1)S(1)}, bf16[128,768]{1,0:T(8,128)(2,1)S(1)}, u32[]{:S(2)}, u32[]{:S(2)}) collective-permute-start(bf16[128,768]{1,0:T(8,128)(2,1)S(1)} %add_convert_fusion.18), channel_id=1, source_target_pairs={{0,16},{1,17},{2,18},{3,19},{4,20},{5,21},{6,22},{7,23},{8,24},{9,... | collective-permute-start | bytes 589832 | tf_op jit(solution)/shard_map/ppermute | solution.py:1001
  256.0 34.9 %all-to-all-start.2 = ((bf16[4,288,768]{2,1,0:T(8,128)(2,1)}), bf16[4,288,768]{2,1,0:T(8,128)(2,1)S(1)}, u32[]{:S(2)}, u32[]{:S(2)}) async-start(bf16[4,288,768]{2,1,0:T(8,128)(2,1)} %unsort.3), calls=%async_computation.2 | async-start | bytes 3538944 | tf_op jit(solution)/shard_map/all_to_all | solution.py:1081
  259.7 13.9 %collective-permute-start.22 = (bf16[48,1536]{1,0:T(8,128)(2,1)S(1)}, bf16[48,1536]{1,0:T(8,128)(2,1)S(1)}, u32[]{:S(2)}, u32[]{:S(2)}) collective-permute-start(bf16[48,1536]{1,0:T(8,128)(2,1)S(1)} %add_convert_fusion.21), channel_id=1, source_target_pairs={{0,16},{1,17},{2,18},{3,19},{4,20},{5,21},{6,22},{7,23},{8,24},{9,... | collective-permute-start | bytes 442376 | tf_op jit(solution)/shard_map/ppermute | solution.py:1001
  273.7 16.5 %collective-permute-start.25 = (bf16[96,1536]{1,0:T(8,128)(2,1)S(1)}, bf16[96,1536]{1,0:T(8,128)(2,1)S(1)}, u32[]{:S(2)}, u32[]{:S(2)}) collective-permute-start(bf16[96,1536]{1,0:T(8,128)(2,1)S(1)} %pad_maximum_fusion.7), channel_id=1, source_target_pairs={{0,2},{1,5},{2,0},{3,7},{4,6},{5,1},{6,4},{7,3},{8,10},{9,13},{10,... | collective-permute-start | bytes 884744 | tf_op jit(solution)/shard_map/ppermute | solution.py:1001
  274.7 16.2 %collective-permute-start.24 = (bf16[256,768]{1,0:T(8,128)(2,1)S(1)}, bf16[256,768]{1,0:T(8,128)(2,1)S(1)}, u32[]{:S(2)}, u32[]{:S(2)}) collective-permute-start(bf16[256,768]{1,0:T(8,128)(2,1)S(1)} %pad_maximum_fusion.6), channel_id=1, source_target_pairs={{0,8},{1,9},{2,10},{3,11},{4,12},{5,13},{6,14},{7,15},{8,0},{9,1},... | collective-permute-start | bytes 1179656 | tf_op jit(solution)/shard_map/ppermute | solution.py:1001
  275.9 14.2 %collective-permute-start.26 = (bf16[48,2432]{1,0:T(8,128)(2,1)S(1)}, bf16[48,2432]{1,0:T(8,128)(2,1)S(1)}, u32[]{:S(2)}, u32[]{:S(2)}) collective-permute-start(bf16[48,2432]{1,0:T(8,128)(2,1)S(1)} %get-tuple-element.246), channel_id=1, source_target_pairs={{0,8},{1,9},{2,10},{3,11},{4,12},{5,13},{6,14},{7,15},{8,0},{9,1},... | collective-permute-start | bytes 700424 | tf_op jit(solution)/shard_map/ppermute | solution.py:1001
  293.1 16.4 %collective-permute-start.27 = (bf16[512,768]{1,0:T(8,128)(2,1)S(1)}, bf16[512,768]{1,0:T(8,128)(2,1)}, u32[]{:S(2)}, u32[]{:S(2)}) collective-permute-start(bf16[512,768]{1,0:T(8,128)(2,1)S(1)} %pad_maximum_fusion.3), channel_id=1, source_target_pairs={{0,2},{1,5},{2,0},{3,7},{4,6},{5,1},{6,4},{7,3},{8,10},{9,13},{10,... | collective-permute-start | bytes 2359304 | tf_op jit(solution)/shard_map/ppermute | solution.py:1001
  293.5 15.6 %collective-permute-start.28 = (bf16[192,1536]{1,0:T(8,128)(2,1)S(1)}, bf16[192,1536]{1,0:T(8,128)(2,1)}, u32[]{:S(2)}, u32[]{:S(2)}) collective-permute-start(bf16[192,1536]{1,0:T(8,128)(2,1)S(1)} %pad_maximum_fusion.4), channel_id=1, source_target_pairs={{0,4},{1,3},{2,6},{3,1},{4,0},{5,7},{6,2},{7,5},{8,12},{9,11},{10,... | collective-permute-start | bytes 1769480 | tf_op jit(solution)/shard_map/ppermute | solution.py:1001
  311.1 32.2 %collective-permute-start.30 = (bf16[1024,768]{1,0:T(8,128)(2,1)S(1)}, bf16[1024,768]{1,0:T(8,128)(2,1)}, u32[]{:S(2)}, u32[]{:S(2)}) collective-permute-start(bf16[1024,768]{1,0:T(8,128)(2,1)S(1)} %pad_maximum_fusion.refs_0_), channel_id=1, source_target_pairs={{0,4},{1,3},{2,6},{3,1},{4,0},{5,7},{6,2},{7,5},{8,12},{9,11},{10,... | collective-permute-start | bytes 4718600 | tf_op jit(solution)/shard_map/ppermute | solution.py:1001
  314.7 28.5 %collective-permute-start.31 = (bf16[384,1536]{1,0:T(8,128)(2,1)}, bf16[384,1536]{1,0:T(8,128)(2,1)}, u32[]{:S(2)}, u32[]{:S(2)}) collective-permute-start(bf16[384,1536]{1,0:T(8,128)(2,1)} %pad_maximum_fusion.1.refs_0_), channel_id=1, source_target_pairs={{0,8},{1,9},{2,10},{3,11},{4,12},{5,13},{6,14},{7,15},{8,0},{9,1},... | collective-permute-start | bytes 3538952 | tf_op jit(solution)/shard_map/ppermute | solution.py:1001
  315.4 26.2 %collective-permute-start.32 = (bf16[24,2432]{1,0:T(8,128)(2,1)S(1)}, bf16[24,2432]{1,0:T(8,128)(2,1)S(1)}, u32[]{:S(2)}, u32[]{:S(2)}) collective-permute-start(bf16[24,2432]{1,0:T(8,128)(2,1)S(1)} %add_convert_fusion.24), channel_id=1, source_target_pairs={{0,16},{1,17},{2,18},{3,19},{4,20},{5,21},{6,22},{7,23},{8,24},{9,... | collective-permute-start | bytes 350216 | tf_op jit(solution)/shard_map/ppermute | solution.py:1001
  318.7 29.5 %collective-permute-start.33 = (bf16[1024,768]{1,0:T(8,128)(2,1)S(1)}, bf16[1024,768]{1,0:T(8,128)(2,1)}, u32[]{:S(2)}, u32[]{:S(2)}) collective-permute-start(bf16[1024,768]{1,0:T(8,128)(2,1)S(1)} %pad_maximum_fusion.refs_0_), channel_id=1, source_target_pairs={{0,1},{1,0},{2,3},{3,2},{4,5},{5,4},{6,7},{7,6},{8,9},{9,8},{10,11... | collective-permute-start | bytes 4718600 | tf_op jit(solution)/shard_map/ppermute | solution.py:970
  363.7 13.6 %collective-permute-start.39 = (bf16[192,2432]{1,0:T(8,128)(2,1)S(1)}, bf16[192,2432]{1,0:T(8,128)(2,1)S(1)}, u32[]{:S(2)}, u32[]{:S(2)}) collective-permute-start(bf16[192,2432]{1,0:T(8,128)(2,1)S(1)} %pad_maximum_fusion.2.refs_0_), channel_id=1, source_target_pairs={{0,4},{1,3},{2,6},{3,1},{4,0},{5,7},{6,2},{7,5},{8,12},{9,11},{10,... | collective-permute-start | bytes 2801672 | tf_op jit(solution)/shard_map/ppermute | solution.py:1001
  364.7 13.4 %collective-permute-start.40 = (bf16[192,2432]{1,0:T(8,128)(2,1)S(1)}, bf16[192,2432]{1,0:T(8,128)(2,1)}, u32[]{:S(2)}, u32[]{:S(2)}) collective-permute-start(bf16[192,2432]{1,0:T(8,128)(2,1)S(1)} %pad_maximum_fusion.2.refs_0_), channel_id=1, source_target_pairs={{0,1},{1,0},{2,3},{3,2},{4,5},{5,4},{6,7},{7,6},{8,9},{9,8},{10,11... | collective-permute-start | bytes 2801672 | tf_op jit(solution)/shard_map/ppermute | solution.py:970
  (51 other events, 320.6 us)

commit v2 on v1

--- a/solution.py
+++ b/solution.py
@@ -558,7 +558,7 @@
 GROUPS = 4
 
 
-def final_call(core, turns, blocks, groups, pieces, name, spread, outs):
+def final_call(core, turns, blocks, groups, pieces, name, spread, outs, scratch=(), finish=None):
     size = blocks // groups
     rows = pieces[0].shape[0] // (blocks // 2)
     whole_tile = 1 if rows % 16 == 0 else 2
@@ -577,6 +577,8 @@
 
         for q in range(4):
             pl.when(active == q)(functools.partial(write, refs[q]))
+        if finish is not None:
+            pl.when(g == groups - 1)(lambda: finish(refs[4:]))
 
     def in_spec(q):
         def index(h, g, c, t):
@@ -594,6 +596,7 @@
             grid=(2, groups),
             in_specs=[in_spec(q) for q in range(4)],
             out_specs=[out_spec(block, index) for _, block, index in outs],
+            scratch_shapes=list(scratch),
         ),
         out_shape=[jax.ShapeDtypeStruct(shape, F32) for shape, _, _ in outs],
         compiler_params=pltpu.CompilerParams(vmem_limit_bytes=VMEM),
@@ -644,16 +647,21 @@
 
 def input_final(core, turns, blocks, pieces):
     width, cols = pieces[0].shape[0] * 4, pieces[0].shape[1]
+    n, half = cols - 3 * width, width // 2
 
     def spread(block, j, place, refs):
         rows_at(refs[0], j, block[:, : 3 * width])
-        rows_at(refs[1], j, block[:, 3 * width :])
+        rows_at(refs[2], place * (blocks // 2) + j, block[:, 3 * width :])
+
+    def finish(refs):
+        refs[1][...] = refs[2][...].T
 
     outs = [
-        ((width, n), (width // 4, n), lambda h, g, place: (h * 2 + place(g), 0))
-        for n in (3 * width, cols - 3 * width)
+        ((width, 3 * width), (half // 2, 3 * width), lambda h, g, place: (h * 2 + place(g), 0)),
+        ((n, width), (n, half), lambda h, g, place: (0, h)),
     ]
-    return final_call(core, turns, blocks, 2, pieces, "input_final", spread, outs)
+    scratch = [pltpu.VMEM((half, n), F32)]
+    return final_call(core, turns, blocks, 2, pieces, "input_final", spread, outs, scratch, finish)
 
 
 def copy_kernel(source, out):
@@ -1121,8 +1129,8 @@
     def row_piece(array, s):
         return lax.dynamic_index_in_dim(array, me ^ s, 0, keepdims=False)
 
-    xs_send = [row_piece(inputs, s) for s in range(blocks)]
-    xs_in = xs_send[:1] + [swap(xs_send[s], "blk", s) for s in range(1, blocks)]
+    xs_send = [row_piece(inputs, s) for s in range(1, blocks)]
+    xs_in = [row_piece(after(inputs, *xs_send), 0)] + [swap(x, "blk", s + 1) for s, x in enumerate(xs_send)]
     ids = [row_piece(image_index, 0)] + [
         swap(row_piece(after(image_index, *xs_send), s), "blk", s) for s in range(1, blocks)
     ]
@@ -1158,29 +1166,29 @@
     order.done(att_grad)
     up_chain, down_chain = Chain(zx, up_send, up_keep), Chain(xy, down_send, down_keep)
 
-    order.advance(down_chain, up_chain)
+    order.advance(up_chain, down_chain)
     result_home = Home(order.done(unsort_call(me.reshape(1), rank_col, blocks, order.hold(result))))
-    order.advance(down_chain, up_chain, result_home)
+    order.advance(up_chain, down_chain, result_home)
     grads, bias_sums = backward_call(starts, qkv, order.hold(att_grad), attended, stat, 0, PAIRS)
     order.done(grads)
-    order.advance(down_chain, up_chain, result_home)
+    order.advance(up_chain, down_chain, result_home)
     input_chain = Chain(
         xy, *order.done(*input_weights_call(core, order.hold(normed), grads, bias_sums, sums2, sums_mid, up_sums))
     )
-    order.advance(down_chain, up_chain, input_chain)
+    order.advance(input_chain, up_chain, down_chain)
     inputs_grad, sums1 = order.done(*input_call(grads, input_weight, xs, order.hold(middle_grad), first_gain[None]))
     small = Small(sums1[:2])
-    order.advance(down_chain, up_chain, input_chain, small)
+    order.advance(input_chain, up_chain, down_chain, small)
     home = Home(order.done(unsort_call(me.reshape(1), rank_col, blocks, order.hold(inputs_grad))))
-    order.advance(down_chain, up_chain, input_chain, small, home)
-    order.advance(down_chain, up_chain, input_chain)
-    order.advance(down_chain, up_chain, input_chain, home)
+    order.advance(input_chain, up_chain, down_chain, small, home)
+    order.advance(input_chain, up_chain, down_chain)
+    order.advance(input_chain, up_chain, down_chain, home)
     while down_chain.at < 2 * len(xy):
-        order.advance(down_chain, up_chain, input_chain)
+        order.advance(input_chain, up_chain, down_chain)
     result_out = order.done(copy_call(order.hold(result_home.result)))
     inputs_out = order.done(copy_call(order.hold(home.result)))
-    order.advance(down_chain, up_chain, input_chain)
-    order.advance(down_chain, up_chain, input_chain)
+    order.advance(input_chain, up_chain, down_chain)
+    order.advance(input_chain, up_chain, down_chain)
     up_total = order.done(up_final(*block_turns(zx), (order.hold(up_chain.result[0]), *up_chain.result[1:])))
     order.advance(input_chain)
     down_total, out_total = order.done(
@@ -1189,7 +1197,7 @@
     while input_chain.result is None:
         order.advance(input_chain)
     input_total, sums = input_final(*block_turns(xy), input_chain.result)
-    sums = jnp.concatenate([small.result, sums[:, :16].T])
+    sums = jnp.concatenate([small.result, sums[:16]])
 
     return (
         result_out,

time: 398 us -> 395 us (level)
  waiting for transfers between devices: 85.3 us -> 79.9 us
  transfers between devices with their start and end apart: 45 -> 45, of which waited for: 17 -> 19; matrix products, arithmetic and copies ran while one was open for 7% -> 8% of each run, Pallas kernels for 30% -> 30%
where the time goes in v2:
time: 395 us; the launch traced here: 388 us
  Pallas kernels  193 us (49%)
  waiting for transfers between devices  79.9 us (20%)
  starting transfers between devices  55.2 us (14%)
  other arithmetic  41.7 us (11%)
  local copies, waits for them, and re-layouts  16.9 us (4%)
    ppermute x24, waiting for transfers between devices, swap_two(): return lax.ppermute(value, ('rows', 'blk'), pairs)  68.3 us
    pallas_call x1, Pallas kernels, mlp_call(): pl.pallas_call(functools.partial(mlp_kernel, parts), grid_spec=pltpu.Pref...  58.8 us
    ppermute x24, starting transfers between devices, swap_two(): return lax.ppermute(value, ('rows', 'blk'), pairs)  35 us
    pallas_call x1, Pallas kernels, backward_call(): pl.pallas_call(backward_kernel, grid_spec=pltpu.PrefetchScalarGridSpec(nu...  32.2 us
    convert_element_type x15, other arithmetic, add_low(): return (a.astype(F32) + b.astype(F32)).astype(BF16)  29.7 us
    pallas_call x3, Pallas kernels, final_call(): pl.pallas_call(kernel, grid_spec=pltpu.PrefetchScalarGridSpec(num_scalar_...  23.7 us
    pallas_call x1, Pallas kernels, forward_call(): pl.pallas_call(forward_kernel, grid_spec=pltpu.PrefetchScalarGridSpec(num...  16 us
    pallas_call x1, Pallas kernels, qkv_call(): pl.pallas_call(functools.partial(qkv_kernel, n, tile), grid=(count // til...  13.1 us
  transfers between devices with their start and end apart: 45, of which 19 were waited for; matrix products, arithmetic and copies ran while one was open for 8% of the time, Pallas kernels for 30%

profile of v2, /device:TPU:0, one launch (start us, length us, event | category | flops | bytes accessed | tf_op | source)
XLA Modules:
  0.0 388.4 jit_solution(3304828089218421847)
XLA Ops:
  22.2 4.3 %collective-permute-done.8.refs_4_ = bf16[288,768]{1,0:T(8,128)(2,1)S(1)} collective-permute-done((bf16[288,768]{1,0:T(8,128)(2,1)}, bf16[288,768]{1,0:T(8,128)(2,1)S(1)}, u32[]{:S(2)}, u32[]{:S(2)}) %collective-permute-start.8) | collective-permute-done | bytes 442400 | tf_op jit(solution)/shard_map/ppermute | solution.py:978
  27.3 13.1 %sort_qkv.1 = (bf16[1152,768]{1,0:T(8,128)(2,1)}, bf16[1152,768]{1,0:T(8,128)(2,1)}, bf16[3,1152,768]{2,1,0:T(8,128)(2,1)}) custom-call(s32[1,1152]{1,0:T(1,128)} %broadcast_in_dim.31.refs_0_.refs_1_, bf16[288,768]{1,0:T(8,128)(2,1)} %dynamic-slice_bitcast_fusion.refs_1_, bf16[288,768]{1,0:T(8,128)(2,1)} %copy-done.19, bf16[288,768]{1,0:T(8,128)(2,1)} %copy-done.20, ...), custom_call_target="tpu_custom_call" | custom-call | flops 1048576 | bytes 65536 | tf_op jit(solution)/shard_map/sort_qkv/pallas_call | solution.py:85
  40.4 16.0 %attention_forward.1 = (f32[1152,768]{1,0:T(8,128)}, f32[1152,768]{1,0:T(8,128)}, bf16[1152,768]{1,0:T(8,128)(2,1)}) custom-call(s32[6]{0:T(128)} %convert_reduce_fusion.1.starts, bf16[3,1152,768]{2,1,0:T(8,128)(2,1)} %get-tuple-element.105.qkv), custom_call_target="tpu_custom_call" | custom-call | flops 1048576 | bytes 65536 | tf_op jit(solution)/shard_map/attention_forward/pallas_call | solution.py:166
  56.4 9.7 %middle.1 = (bf16[1152,768]{1,0:T(8,128)(2,1)}, f32[1152,768]{1,0:T(8,128)}, bf16[1152,768]{1,0:T(8,128)(2,1)}, bf16[1152,768]{1,0:T(8,128)(2,1)}, f32[8,768]{1,0:T(8,128)}) custom-call(f32[2]{0:T(128)} %fusion.6.refs_0_.keep, s32[1,1152]{1,0:T(1,128)} %broadcast_in_dim.31.refs_0_.refs_1_, bf16[288,768]{1,0:T(8,128)(2,1)} %get-tuple-element.209.refs_2_, ...), custom_call_target="tpu_custom_call" | custom-call | flops 1048576 | bytes 65536 | tf_op jit(solution)/shard_map/middle/pallas_call | solution.py:319
  66.1 58.8 %mlp.1 = (bf16[768,1536]{1,0:T(8,128)(2,1)}, bf16[768,1536]{1,0:T(8,128)(2,1)}, bf16[2048,768]{1,0:T(8,128)(2,1)}, bf16[2048,768]{1,0:T(8,128)(2,1)}, f32[1,3072...) custom-call(s32[1]{0:T(128)} %bitcast.core.c, ...), custom_call_target="tpu_custom_call" | custom-call | flops 1048576 | bytes 65536 | tf_op jit(solution)/shard_map/mlp/pallas_call | solution.py:422
  127.7 6.0 %unsort.2 = bf16[4,288,768]{2,1,0:T(8,128)(2,1)} custom-call(s32[1]{0:T(128)} %bitcast.10.me, s32[1152,1]{1,0:T(8,128)} %broadcast_in_dim.37.rank, bf16[1152,768]{1,0:T(8,128)(2,1)} %get-tuple-element.120.source), custom_call_target="tpu_custom_call" | custom-call | flops 1048576 | bytes 65536 | tf_op jit(solution)/shard_map/unsort/pallas_call | solution.py:502
  135.6 5.3 %add_convert_fusion = (bf16[1024,768]{1,0:T(8,128)(2,1)}, bf16[1024,768]{1,0:T(8,128)(2,1)}) fusion(bf16[2048,768]{1,0:T(8,128)(2,1)} %collective-permute-done.10, s32[]{:T(128)S(6)} %select_n.384, bf16[2048,768]{1,0:T(8,128)(2,1)} %get-tuple-element.119, s32[]{:T(128)S(6)} %select_n.382), kind=kLoop, calls=%fused_computation.1 | loop fusion | flops 6291456 | bytes 9437192 | tf_op jit(solution)/shard_map/convert_element_type | solution.py:998
  142.3 3.6 all-to-all-start
  145.8 4.3 %add_convert_fusion.2 = (bf16[384,1536]{1,0:T(8,128)(2,1)}, bf16[384,1536]{1,0:T(8,128)(2,1)}) fusion(bf16[768,1536]{1,0:T(8,128)(2,1)} %collective-permute-done.9, s32[]{:T(128)S(6)} %select_n.383, bf16[768,1536]{1,0:T(8,128)(2,1)} %get-tuple-element.112, s32[]{:T(128)S(6)} %select_n.377), kind=kLoop, calls=%fused_computation.3 | loop fusion | flops 4718592 | bytes 7077896 | tf_op jit(solution)/shard_map/convert_element_type | solution.py:998
  151.8 32.2 %attention_backward.1 = (bf16[3,1152,768]{2,1,0:T(8,128)(2,1)}, f32[8,768]{1,0:T(8,128)}) custom-call(s32[6]{0:T(128)} %convert_reduce_fusion.1.starts, bf16[3,1152,768]{2,1,0:T(8,128)(2,1)} %get-tuple-element.105.qkv, bf16[1152,768]{1,0:T(8,128)(2,1)} %get-tuple-element.124.grad, f32[1152,768]{1,0:T(8,128)} %get-tuple-element.125.att, ...), custom_call_target="tpu_custom_call" | custom-call | flops 1048576 | bytes 65536 | tf_op jit(solution)/shard_map/attention_backward/pallas_call | solution.py:252
  184.0 4.0 %add_convert_fusion.6 = (bf16[512,768]{1,0:T(8,128)(2,1)}, bf16[512,768]{1,0:T(8,128)(2,1)}) fusion(bf16[1024,768]{1,0:T(8,128)(2,1)} %collective-permute-done.12, s32[]{:T(128)S(6)} %select_n.389, bf16[1024,768]{1,0:T(8,128)(2,1)} %get-tuple-element.195, s32[]{:T(128)S(6)} %select_n.388), kind=kLoop, calls=%fused_computation.8 | loop fusion | flops 3145728 | bytes 4718600 | tf_op jit(solution)/shard_map/convert_element_type | solution.py:998
  192.6 9.8 %input_weights.1 = (bf16[384,2432]{1,0:T(8,128)(2,1)}, bf16[384,2432]{1,0:T(8,128)(2,1)}) custom-call(s32[1]{0:T(128)} %bitcast.core.c, bf16[1152,768]{1,0:T(8,128)(2,1)} %get-tuple-element.132.normed, bf16[3,1152,768]{2,1,0:T(8,128)(2,1)} %get-tuple-element.127.grads, f32[8,768]{1,0:T(8,128)} %get-tuple-element.133.first, ...), custom_call_target="tpu_custom_call" | custom-call | flops 1048576 | bytes 65536 | tf_op jit(solution)/shard_map/input_weights/pallas_call | solution.py:543
  202.4 3.5 collective-permute-done.13
  211.5 10.6 %input_backward.1 = (bf16[1152,768]{1,0:T(8,128)(2,1)}, f32[8,768]{1,0:T(8,128)}) custom-call(bf16[3,1152,768]{2,1,0:T(8,128)(2,1)} %get-tuple-element.127.grads, bf16[768,2304]{1,0:T(8,128)(2,1)} %weight.1, bf16[1152,768]{1,0:T(8,128)(2,1)} %get-tuple-element.107.refs_7_.xs, f32[1152,768]{1,0:T(8,128)} %get-tuple-element.143.middle_grad, ...), custom_call_target="tpu_custom_call" | custom-call | flops 1048576 | bytes 65536 | tf_op jit(solution)/shard_map/input_backward/pallas_call | solution.py:475
  223.6 3.4 add_convert_fusion.5
  238.1 6.0 %unsort.3 = bf16[4,288,768]{2,1,0:T(8,128)(2,1)} custom-call(s32[1]{0:T(128)} %bitcast.10.me, s32[1152,1]{1,0:T(8,128)} %broadcast_in_dim.37.rank, bf16[1152,768]{1,0:T(8,128)(2,1)} %get-tuple-element.150.source), custom_call_target="tpu_custom_call" | custom-call | flops 1048576 | bytes 65536 | tf_op jit(solution)/shard_map/unsort/pallas_call | solution.py:502
  244.1 8.0 %collective-permute-done.19 = bf16[48,1536]{1,0:T(8,128)(2,1)S(1)} collective-permute-done((bf16[48,1536]{1,0:T(8,128)(2,1)S(1)}, bf16[48,1536]{1,0:T(8,128)(2,1)S(1)}, u32[]{:S(2)}, u32[]{:S(2)}) %collective-permute-start.19) | collective-permute-done | bytes 147488 | tf_op jit(solution)/shard_map/ppermute | solution.py:1009
  256.4 3.6 all-to-all-start.2
  263.7 7.8 %collective-permute-done.22 = bf16[48,1536]{1,0:T(8,128)(2,1)S(1)} collective-permute-done((bf16[48,1536]{1,0:T(8,128)(2,1)S(1)}, bf16[48,1536]{1,0:T(8,128)(2,1)S(1)}, u32[]{:S(2)}, u32[]{:S(2)}) %collective-permute-start.22) | collective-permute-done | bytes 147488 | tf_op jit(solution)/shard_map/ppermute | solution.py:1009
  275.9 10.7 %collective-permute-done.24 = bf16[48,2432]{1,0:T(8,128)(2,1)S(1)} collective-permute-done((bf16[48,2432]{1,0:T(8,128)(2,1)S(1)}, bf16[48,2432]{1,0:T(8,128)(2,1)S(1)}, u32[]{:S(2)}, u32[]{:S(2)}) %collective-permute-start.24) | collective-permute-done | bytes 233504 | tf_op jit(solution)/shard_map/ppermute | solution.py:1009
  293.0 3.1 collective-permute-start.27
  296.1 3.3 collective-permute-done.27
  299.4 6.5 %collective-permute-done.28 = bf16[192,1536]{1,0:T(8,128)(2,1)} collective-permute-done((bf16[192,1536]{1,0:T(8,128)(2,1)S(1)}, bf16[192,1536]{1,0:T(8,128)(2,1)}, u32[]{:S(2)}, u32[]{:S(2)}) %collective-permute-start.28) | collective-permute-done | bytes 589856 | tf_op jit(solution)/shard_map/ppermute | solution.py:1009
  312.8 3.5 collective-permute-start.30
  316.3 3.6 copy.36
  320.0 3.6 copy.37
  323.6 15.3 %collective-permute-done.30 = bf16[24,2432]{1,0:T(8,128)(2,1)S(1)} collective-permute-done((bf16[24,2432]{1,0:T(8,128)(2,1)S(1)}, bf16[24,2432]{1,0:T(8,128)(2,1)S(1)}, u32[]{:S(2)}, u32[]{:S(2)}) %collective-permute-start.30) | collective-permute-done | bytes 116768 | tf_op jit(solution)/shard_map/ppermute | solution.py:1009
  341.7 4.0 %collective-permute-start.33 = (bf16[48,2432]{1,0:T(8,128)(2,1)S(1)}, bf16[48,2432]{1,0:T(8,128)(2,1)S(1)}, u32[]{:S(2)}, u32[]{:S(2)}) collective-permute-start(bf16[48,2432]{1,0:T(8,128)(2,1)S(1)} %pad_maximum_fusion.8), channel_id=1, source_target_pairs={{0,8},{1,9},{2,10},{3,11},{4,12},{5,13},{6,14},{7,15},{8,0},{9,1},... | collective-permute-start | bytes 700424 | tf_op jit(solution)/shard_map/ppermute | solution.py:1009
  346.2 5.9 %collective-permute-done.33 = bf16[48,2432]{1,0:T(8,128)(2,1)S(1)} collective-permute-done((bf16[48,2432]{1,0:T(8,128)(2,1)S(1)}, bf16[48,2432]{1,0:T(8,128)(2,1)S(1)}, u32[]{:S(2)}, u32[]{:S(2)}) %collective-permute-start.33) | collective-permute-done | bytes 233504 | tf_op jit(solution)/shard_map/ppermute | solution.py:1009
  354.5 7.0 %up_final.1 = f32[768,3072]{1,0:T(8,128)} custom-call(s32[1]{0:T(128)} %bitcast.core.c, s32[2]{0:T(128)} %pad_add_fusion.1.t, bf16[384,1536]{1,0:T(8,128)(2,1)} %pad_maximum_fusion.1.refs_0_, bf16[384,1536]{1,0:T(8,128)(2,1)} %collective-permute-done.31.refs_1_, bf16[384,1536]{1,0:T(8,128)(2,1)} %copy-done.10, bf16[384,1536]{1,0:T(8,128)(2,1)} %copy-done.11), custom_call_target="tpu_custom_call" | custom-call | flops 1048576 | bytes 65536 | tf_op jit(solution)/shard_map/up_final/pallas_call | solution.py:592
  362.8 10.5 %down_final.1 = (f32[3072,768]{1,0:T(8,128)}, f32[768,768]{1,0:T(8,128)}) custom-call(s32[1]{0:T(128)} %bitcast.core.c, s32[2]{0:T(128)} %pad_add_fusion.t, bf16[1024,768]{1,0:T(8,128)(2,1)} %copy-done.2, bf16[1024,768]{1,0:T(8,128)(2,1)} %collective-permute-done.32.refs_1_, bf16[1024,768]{1,0:T(8,128)(2,1)} %collective-permute-done.36.refs_2_, ...), custom_call_target="tpu_custom_call" | custom-call | flops 1048576 | bytes 65536 | tf_op jit(solution)/shard_map/down_final/pallas_call | solution.py:592
  378.1 6.3 %input_final.1 = (f32[768,2304]{1,0:T(8,128)}, f32[128,768]{1,0:T(8,128)}) custom-call(s32[1]{0:T(128)} %bitcast.core.c, s32[2]{0:T(128)} %pad_add_fusion.t, bf16[192,2432]{1,0:T(8,128)(2,1)} %copy-done.4, bf16[192,2432]{1,0:T(8,128)(2,1)} %copy-done.14, bf16[192,2432]{1,0:T(8,128)(2,1)} %collective-permute-done.40.refs_2_, ...), custom_call_target="tpu_custom_call" | custom-call | flops 1048576 | bytes 65536 | tf_op jit(solution)/shard_map/input_final/pallas_call | solution.py:592
  (207 shorter events, 93.7 us)
Async XLA Ops:
  3.2 16.9 %collective-permute-start.6 = (bf16[288,768]{1,0:T(8,128)(2,1)}, bf16[288,768]{1,0:T(8,128)(2,1)S(1)}, u32[]{:S(2)}, u32[]{:S(2)}) collective-permute-start(bf16[288,768]{1,0:T(8,128)(2,1)} %get-tuple-element.213), channel_id=1, source_target_pairs={{0,1},{1,0},{2,3},{3,2},{4,5},{5,4},{6,7},{7,6},{8,9},{9,8},{10,11... | collective-permute-start | bytes 1327112 | tf_op jit(solution)/shard_map/ppermute | solution.py:978
  3.6 18.6 %collective-permute-start.7 = (bf16[288,768]{1,0:T(8,128)(2,1)}, bf16[288,768]{1,0:T(8,128)(2,1)S(1)}, u32[]{:S(2)}, u32[]{:S(2)}) collective-permute-start(bf16[288,768]{1,0:T(8,128)(2,1)} %get-tuple-element.212), channel_id=1, source_target_pairs={{0,2},{1,3},{2,0},{3,1},{4,6},{5,7},{6,4},{7,5},{8,10},{9,11},{10,... | collective-permute-start | bytes 1327112 | tf_op jit(solution)/shard_map/ppermute | solution.py:978
  14.4 12.1 %collective-permute-start.8 = (bf16[288,768]{1,0:T(8,128)(2,1)}, bf16[288,768]{1,0:T(8,128)(2,1)S(1)}, u32[]{:S(2)}, u32[]{:S(2)}) collective-permute-start(bf16[288,768]{1,0:T(8,128)(2,1)} %get-tuple-element.211), channel_id=1, source_target_pairs={{0,3},{1,2},{2,1},{3,0},{4,7},{5,6},{6,5},{7,4},{8,11},{9,10},{10,... | collective-permute-start | bytes 1327112 | tf_op jit(solution)/shard_map/ppermute | solution.py:978
  17.3 39.1 %collective-permute-start.5 = (bf16[288,768]{1,0:T(8,128)(2,1)}, bf16[288,768]{1,0:T(8,128)(2,1)}, u32[]{:S(2)}, u32[]{:S(2)}) collective-permute-start(bf16[288,768]{1,0:T(8,128)(2,1)} %get-tuple-element.103), channel_id=1, source_target_pairs={{0,3},{1,2},{2,1},{3,0},{4,7},{5,6},{6,5},{7,4},{8,11},{9,10},{10,... | collective-permute-start | bytes 1327112 | tf_op jit(solution)/shard_map/ppermute | solution.py:978
  18.3 38.1 %collective-permute-start.4 = (bf16[288,768]{1,0:T(8,128)(2,1)}, bf16[288,768]{1,0:T(8,128)(2,1)}, u32[]{:S(2)}, u32[]{:S(2)}) collective-permute-start(bf16[288,768]{1,0:T(8,128)(2,1)} %get-tuple-element.102), channel_id=1, source_target_pairs={{0,2},{1,3},{2,0},{3,1},{4,6},{5,7},{6,4},{7,5},{8,10},{9,11},{10,... | collective-permute-start | bytes 1327112 | tf_op jit(solution)/shard_map/ppermute | solution.py:978
  20.1 36.3 %collective-permute-start.3 = (bf16[288,768]{1,0:T(8,128)(2,1)S(1)}, bf16[288,768]{1,0:T(8,128)(2,1)}, u32[]{:S(2)}, u32[]{:S(2)}) collective-permute-start(bf16[288,768]{1,0:T(8,128)(2,1)S(1)} %get-tuple-element.101), channel_id=1, source_target_pairs={{0,1},{1,0},{2,3},{3,2},{4,5},{5,4},{6,7},{7,6},{8,9},{9,8},{10,11... | collective-permute-start | bytes 1327112 | tf_op jit(solution)/shard_map/ppermute | solution.py:978
  140.9 43.1 %collective-permute-start.12 = (bf16[1024,768]{1,0:T(8,128)(2,1)}, bf16[1024,768]{1,0:T(8,128)(2,1)}, u32[]{:S(2)}, u32[]{:S(2)}) collective-permute-start(bf16[1024,768]{1,0:T(8,128)(2,1)} %get-tuple-element.196), channel_id=1, source_target_pairs={{0,4},{1,3},{2,6},{3,1},{4,0},{5,7},{6,2},{7,5},{8,12},{9,11},{10,... | collective-permute-start | bytes 4718600 | tf_op jit(solution)/shard_map/ppermute | solution.py:1009
  142.3 41.7 %all-to-all-start = ((bf16[4,288,768]{2,1,0:T(8,128)(2,1)}), bf16[4,288,768]{2,1,0:T(8,128)(2,1)S(1)}, u32[]{:S(2)}, u32[]{:S(2)}) async-start(bf16[4,288,768]{2,1,0:T(8,128)(2,1)} %unsort.2), calls=%async_computation | async-start | bytes 3538944 | tf_op jit(solution)/shard_map/all_to_all | solution.py:1089
  150.2 33.8 %collective-permute-start.11 = (bf16[384,1536]{1,0:T(8,128)(2,1)}, bf16[384,1536]{1,0:T(8,128)(2,1)}, u32[]{:S(2)}, u32[]{:S(2)}) collective-permute-start(bf16[384,1536]{1,0:T(8,128)(2,1)} %get-tuple-element.198), channel_id=1, source_target_pairs={{0,8},{1,9},{2,10},{3,11},{4,12},{5,13},{6,14},{7,15},{8,0},{9,1},... | collective-permute-start | bytes 3538952 | tf_op jit(solution)/shard_map/ppermute | solution.py:1009
  188.0 18.6 %collective-permute-start.14 = (bf16[512,768]{1,0:T(8,128)(2,1)}, bf16[512,768]{1,0:T(8,128)(2,1)}, u32[]{:S(2)}, u32[]{:S(2)}) collective-permute-start(bf16[512,768]{1,0:T(8,128)(2,1)} %get-tuple-element.202), channel_id=1, source_target_pairs={{0,2},{1,5},{2,0},{3,7},{4,6},{5,1},{6,4},{7,3},{8,10},{9,13},{10,... | collective-permute-start | bytes 2359304 | tf_op jit(solution)/shard_map/ppermute | solution.py:1009
  192.4 13.5 %collective-permute-start.13 = (bf16[192,1536]{1,0:T(8,128)(2,1)}, bf16[192,1536]{1,0:T(8,128)(2,1)S(1)}, u32[]{:S(2)}, u32[]{:S(2)}) collective-permute-start(bf16[192,1536]{1,0:T(8,128)(2,1)} %get-tuple-element.204), channel_id=1, source_target_pairs={{0,4},{1,3},{2,6},{3,1},{4,0},{5,7},{6,2},{7,5},{8,12},{9,11},{10,... | collective-permute-start | bytes 1769480 | tf_op jit(solution)/shard_map/ppermute | solution.py:1009
  206.6 16.2 %collective-permute-start.15 = (bf16[384,2432]{1,0:T(8,128)(2,1)}, bf16[384,2432]{1,0:T(8,128)(2,1)}, u32[]{:S(2)}, u32[]{:S(2)}) collective-permute-start(bf16[384,2432]{1,0:T(8,128)(2,1)} %get-tuple-element.139), channel_id=1, source_target_pairs={{0,1},{1,0},{2,3},{3,2},{4,5},{5,4},{6,7},{7,6},{8,9},{9,8},{10,11... | collective-permute-start | bytes 5603336 | tf_op jit(solution)/shard_map/ppermute | solution.py:978
  208.9 13.9 %collective-permute-start.17 = (bf16[256,768]{1,0:T(8,128)(2,1)}, bf16[256,768]{1,0:T(8,128)(2,1)}, u32[]{:S(2)}, u32[]{:S(2)}) collective-permute-start(bf16[256,768]{1,0:T(8,128)(2,1)} %get-tuple-element.215), channel_id=1, source_target_pairs={{0,8},{1,9},{2,10},{3,11},{4,12},{5,13},{6,14},{7,15},{8,0},{9,1},... | collective-permute-start | bytes 1179656 | tf_op jit(solution)/shard_map/ppermute | solution.py:1009
  209.5 13.3 %collective-permute-start.16 = (bf16[96,1536]{1,0:T(8,128)(2,1)S(1)}, bf16[96,1536]{1,0:T(8,128)(2,1)S(1)}, u32[]{:S(2)}, u32[]{:S(2)}) collective-permute-start(bf16[96,1536]{1,0:T(8,128)(2,1)S(1)} %get-tuple-element.217), channel_id=1, source_target_pairs={{0,2},{1,5},{2,0},{3,7},{4,6},{5,1},{6,4},{7,3},{8,10},{9,13},{10,... | collective-permute-start | bytes 884744 | tf_op jit(solution)/shard_map/ppermute | solution.py:1009
  226.9 25.8 %collective-permute-start.18 = (bf16[192,2432]{1,0:T(8,128)(2,1)}, bf16[192,2432]{1,0:T(8,128)(2,1)}, u32[]{:S(2)}, u32[]{:S(2)}) collective-permute-start(bf16[192,2432]{1,0:T(8,128)(2,1)} %get-tuple-element.200), channel_id=1, source_target_pairs={{0,4},{1,3},{2,6},{3,1},{4,0},{5,7},{6,2},{7,5},{8,12},{9,11},{10,... | collective-permute-start | bytes 2801672 | tf_op jit(solution)/shard_map/ppermute | solution.py:1009
  229.2 22.9 %collective-permute-start.20 = (bf16[128,768]{1,0:T(8,128)(2,1)}, bf16[128,768]{1,0:T(8,128)(2,1)S(1)}, u32[]{:S(2)}, u32[]{:S(2)}) collective-permute-start(bf16[128,768]{1,0:T(8,128)(2,1)} %get-tuple-element.221), channel_id=1, source_target_pairs={{0,16},{1,17},{2,18},{3,19},{4,20},{5,21},{6,22},{7,23},{8,24},{9,... | collective-permute-start | bytes 589832 | tf_op jit(solution)/shard_map/ppermute | solution.py:1009
  231.8 20.3 %all-to-all-start.1 = ((f32[32,2,768]{2,1,0:T(2,128)}), f32[32,2,768]{2,1,0:T(2,128)S(1)}, u32[]{:S(2)}, u32[]{:S(2)}) async-start(f32[32,2,768]{2,1,0:T(2,128)} %broadcast_in_dim.36), calls=%async_computation.1 | async-start | bytes 393216 | tf_op jit(solution)/shard_map/all_to_all | solution.py:1077
  235.5 16.6 %collective-permute-start.19 = (bf16[48,1536]{1,0:T(8,128)(2,1)S(1)}, bf16[48,1536]{1,0:T(8,128)(2,1)S(1)}, u32[]{:S(2)}, u32[]{:S(2)}) collective-permute-start(bf16[48,1536]{1,0:T(8,128)(2,1)S(1)} %get-tuple-element.223), channel_id=1, source_target_pairs={{0,16},{1,17},{2,18},{3,19},{4,20},{5,21},{6,22},{7,23},{8,24},{9,... | collective-permute-start | bytes 442376 | tf_op jit(solution)/shard_map/ppermute | solution.py:1009
  253.8 17.7 %collective-permute-start.23 = (bf16[128,768]{1,0:T(8,128)(2,1)S(1)}, bf16[128,768]{1,0:T(8,128)(2,1)}, u32[]{:S(2)}, u32[]{:S(2)}) collective-permute-start(bf16[128,768]{1,0:T(8,128)(2,1)S(1)} %add_convert_fusion.18), channel_id=1, source_target_pairs={{0,16},{1,17},{2,18},{3,19},{4,20},{5,21},{6,22},{7,23},{8,24},{9,... | collective-permute-start | bytes 589832 | tf_op jit(solution)/shard_map/ppermute | solution.py:1009
  256.1 15.4 %collective-permute-start.21 = (bf16[96,2432]{1,0:T(8,128)(2,1)}, bf16[96,2432]{1,0:T(8,128)(2,1)}, u32[]{:S(2)}, u32[]{:S(2)}) collective-permute-start(bf16[96,2432]{1,0:T(8,128)(2,1)} %get-tuple-element.206), channel_id=1, source_target_pairs={{0,2},{1,5},{2,0},{3,7},{4,6},{5,1},{6,4},{7,3},{8,10},{9,13},{10,... | collective-permute-start | bytes 1400840 | tf_op jit(solution)/shard_map/ppermute | solution.py:1009
  256.4 30.6 %all-to-all-start.2 = ((bf16[4,288,768]{2,1,0:T(8,128)(2,1)}), bf16[4,288,768]{2,1,0:T(8,128)(2,1)S(1)}, u32[]{:S(2)}, u32[]{:S(2)}) async-start(bf16[4,288,768]{2,1,0:T(8,128)(2,1)} %unsort.3), calls=%async_computation.2 | async-start | bytes 3538944 | tf_op jit(solution)/shard_map/all_to_all | solution.py:1089
  272.4 14.5 %collective-permute-start.26 = (bf16[256,768]{1,0:T(8,128)(2,1)S(1)}, bf16[256,768]{1,0:T(8,128)(2,1)}, u32[]{:S(2)}, u32[]{:S(2)}) collective-permute-start(bf16[256,768]{1,0:T(8,128)(2,1)S(1)} %pad_maximum_fusion.6), channel_id=1, source_target_pairs={{0,8},{1,9},{2,10},{3,11},{4,12},{5,13},{6,14},{7,15},{8,0},{9,1},... | collective-permute-start | bytes 1179656 | tf_op jit(solution)/shard_map/ppermute | solution.py:1009
  272.6 14.4 %collective-permute-start.25 = (bf16[96,1536]{1,0:T(8,128)(2,1)S(1)}, bf16[96,1536]{1,0:T(8,128)(2,1)S(1)}, u32[]{:S(2)}, u32[]{:S(2)}) collective-permute-start(bf16[96,1536]{1,0:T(8,128)(2,1)S(1)} %pad_maximum_fusion.7), channel_id=1, source_target_pairs={{0,2},{1,5},{2,0},{3,7},{4,6},{5,1},{6,4},{7,3},{8,10},{9,13},{10,... | collective-permute-start | bytes 884744 | tf_op jit(solution)/shard_map/ppermute | solution.py:1009
  289.1 18.4 %collective-permute-start.29 = (bf16[512,768]{1,0:T(8,128)(2,1)S(1)}, bf16[512,768]{1,0:T(8,128)(2,1)}, u32[]{:S(2)}, u32[]{:S(2)}) collective-permute-start(bf16[512,768]{1,0:T(8,128)(2,1)S(1)} %pad_maximum_fusion.3), channel_id=1, source_target_pairs={{0,2},{1,5},{2,0},{3,7},{4,6},{5,1},{6,4},{7,3},{8,10},{9,13},{10,... | collective-permute-start | bytes 2359304 | tf_op jit(solution)/shard_map/ppermute | solution.py:1009
  290.6 15.3 %collective-permute-start.28 = (bf16[192,1536]{1,0:T(8,128)(2,1)S(1)}, bf16[192,1536]{1,0:T(8,128)(2,1)}, u32[]{:S(2)}, u32[]{:S(2)}) collective-permute-start(bf16[192,1536]{1,0:T(8,128)(2,1)S(1)} %pad_maximum_fusion.4), channel_id=1, source_target_pairs={{0,4},{1,3},{2,6},{3,1},{4,0},{5,7},{6,2},{7,5},{8,12},{9,11},{10,... | collective-permute-start | bytes 1769480 | tf_op jit(solution)/shard_map/ppermute | solution.py:1009
  309.0 32.2 %collective-permute-start.32 = (bf16[1024,768]{1,0:T(8,128)(2,1)S(1)}, bf16[1024,768]{1,0:T(8,128)(2,1)}, u32[]{:S(2)}, u32[]{:S(2)}) collective-permute-start(bf16[1024,768]{1,0:T(8,128)(2,1)S(1)} %pad_maximum_fusion.refs_0_), channel_id=1, source_target_pairs={{0,4},{1,3},{2,6},{3,1},{4,0},{5,7},{6,2},{7,5},{8,12},{9,11},{10,... | collective-permute-start | bytes 4718600 | tf_op jit(solution)/shard_map/ppermute | solution.py:1009
  311.9 29.3 %collective-permute-start.31 = (bf16[384,1536]{1,0:T(8,128)(2,1)}, bf16[384,1536]{1,0:T(8,128)(2,1)}, u32[]{:S(2)}, u32[]{:S(2)}) collective-permute-start(bf16[384,1536]{1,0:T(8,128)(2,1)} %pad_maximum_fusion.1.refs_0_), channel_id=1, source_target_pairs={{0,8},{1,9},{2,10},{3,11},{4,12},{5,13},{6,14},{7,15},{8,0},{9,1},... | collective-permute-start | bytes 3538952 | tf_op jit(solution)/shard_map/ppermute | solution.py:1009
  312.8 26.1 %collective-permute-start.30 = (bf16[24,2432]{1,0:T(8,128)(2,1)S(1)}, bf16[24,2432]{1,0:T(8,128)(2,1)S(1)}, u32[]{:S(2)}, u32[]{:S(2)}) collective-permute-start(bf16[24,2432]{1,0:T(8,128)(2,1)S(1)} %add_convert_fusion.24), channel_id=1, source_target_pairs={{0,16},{1,17},{2,18},{3,19},{4,20},{5,21},{6,22},{7,23},{8,24},{9,... | collective-permute-start | bytes 350216 | tf_op jit(solution)/shard_map/ppermute | solution.py:1009
  316.3 29.8 %collective-permute-start.36 = (bf16[1024,768]{1,0:T(8,128)(2,1)S(1)}, bf16[1024,768]{1,0:T(8,128)(2,1)}, u32[]{:S(2)}, u32[]{:S(2)}) collective-permute-start(bf16[1024,768]{1,0:T(8,128)(2,1)S(1)} %pad_maximum_fusion.refs_0_), channel_id=1, source_target_pairs={{0,1},{1,0},{2,3},{3,2},{4,5},{5,4},{6,7},{7,6},{8,9},{9,8},{10,11... | collective-permute-start | bytes 4718600 | tf_op jit(solution)/shard_map/ppermute | solution.py:978
  341.2 11.8 %collective-permute-start.37 = (bf16[1024,768]{1,0:T(8,128)(2,1)}, bf16[1024,768]{1,0:T(8,128)(2,1)}, u32[]{:S(2)}, u32[]{:S(2)}) collective-permute-start(bf16[1024,768]{1,0:T(8,128)(2,1)} %collective-permute-done.32.refs_1_), channel_id=1, source_target_pairs={{0,1},{1,0},{2,3},{3,2},{4,5},{5,4},{6,7},{7,6},{8,9},{9,8},{10,11... | collective-permute-start | bytes 4718600 | tf_op jit(solution)/shard_map/ppermute | solution.py:978
  361.8 13.6 %collective-permute-start.39 = (bf16[192,2432]{1,0:T(8,128)(2,1)S(1)}, bf16[192,2432]{1,0:T(8,128)(2,1)S(1)}, u32[]{:S(2)}, u32[]{:S(2)}) collective-permute-start(bf16[192,2432]{1,0:T(8,128)(2,1)S(1)} %pad_maximum_fusion.2.refs_0_), channel_id=1, source_target_pairs={{0,4},{1,3},{2,6},{3,1},{4,0},{5,7},{6,2},{7,5},{8,12},{9,11},{10,... | collective-permute-start | bytes 2801672 | tf_op jit(solution)/shard_map/ppermute | solution.py:1009
  362.8 12.7 %collective-permute-start.40 = (bf16[192,2432]{1,0:T(8,128)(2,1)S(1)}, bf16[192,2432]{1,0:T(8,128)(2,1)}, u32[]{:S(2)}, u32[]{:S(2)}) collective-permute-start(bf16[192,2432]{1,0:T(8,128)(2,1)S(1)} %pad_maximum_fusion.2.refs_0_), channel_id=1, source_target_pairs={{0,1},{1,0},{2,3},{3,2},{4,5},{5,4},{6,7},{7,6},{8,9},{9,8},{10,11... | collective-permute-start | bytes 2801672 | tf_op jit(solution)/shard_map/ppermute | solution.py:978
  (53 other events, 341.1 us)

commit v3 on v2

--- a/solution.py
+++ b/solution.py
@@ -78,7 +78,7 @@
         qkv_out[j] = mixed * BF16(HEAD_DIM**-0.5) if j == 0 else mixed
 
 
-def qkv_call(rank, pieces, gain, shift, weight, bias, tile=288):
+def qkv_call(rank, pieces, gain, shift, weight, bias, tile=384):
     n = len(pieces)
     span, width = pieces[0].shape
     count = n * span

time: 395 us -> 394 us (level)
  transfers between devices with their start and end apart: 45 -> 45, of which waited for: 19 -> 17; matrix products, arithmetic and copies ran while one was open for 8% -> 8% of each run, Pallas kernels for 30% -> 30%
where the time goes in v3:
time: 394 us; the launch traced here: 387 us
  Pallas kernels  193 us (49%)
  waiting for transfers between devices  81.4 us (21%)
  starting transfers between devices  52.8 us (13%)
  other arithmetic  41.7 us (11%)
  local copies, waits for them, and re-layouts  17 us (4%)
    ppermute x24, waiting for transfers between devices, swap_two(): return lax.ppermute(value, ('rows', 'blk'), pairs)  67.4 us
    pallas_call x1, Pallas kernels, mlp_call(): pl.pallas_call(functools.partial(mlp_kernel, parts), grid_spec=pltpu.Pref...  58.8 us
    ppermute x24, starting transfers between devices, swap_two(): return lax.ppermute(value, ('rows', 'blk'), pairs)  33.3 us
    pallas_call x1, Pallas kernels, backward_call(): pl.pallas_call(backward_kernel, grid_spec=pltpu.PrefetchScalarGridSpec(nu...  32.3 us
    convert_element_type x15, other arithmetic, add_low(): return (a.astype(F32) + b.astype(F32)).astype(BF16)  29.7 us
    pallas_call x3, Pallas kernels, final_call(): pl.pallas_call(kernel, grid_spec=pltpu.PrefetchScalarGridSpec(num_scalar_...  23.7 us
    pallas_call x1, Pallas kernels, forward_call(): pl.pallas_call(forward_kernel, grid_spec=pltpu.PrefetchScalarGridSpec(num...  16.1 us
    ppermute x18, waiting for transfers between devices, swap(): lax.ppermute(value, axis, [(i, i ^ bit) for i in range(lax.axis_size(axis...  14 us
  transfers between devices with their start and end apart: 45, of which 17 were waited for; matrix products, arithmetic and copies ran while one was open for 8% of the time, Pallas kernels for 30%

profile of v3, /device:TPU:0, one launch (start us, length us, event | category | flops | bytes accessed | tf_op | source)
XLA Modules:
  0.0 387.4 jit_solution(2270663846593007445)
XLA Ops:
  22.2 4.3 %collective-permute-done.8.refs_4_ = bf16[288,768]{1,0:T(8,128)(2,1)S(1)} collective-permute-done((bf16[288,768]{1,0:T(8,128)(2,1)}, bf16[288,768]{1,0:T(8,128)(2,1)S(1)}, u32[]{:S(2)}, u32[]{:S(2)}) %collective-permute-start.8) | collective-permute-done | bytes 442400 | tf_op jit(solution)/shard_map/ppermute | solution.py:978
  27.3 12.7 %sort_qkv.1 = (bf16[1152,768]{1,0:T(8,128)(2,1)}, bf16[1152,768]{1,0:T(8,128)(2,1)}, bf16[3,1152,768]{2,1,0:T(8,128)(2,1)}) custom-call(s32[1,1152]{1,0:T(1,128)} %broadcast_in_dim.31.refs_0_.refs_1_, bf16[288,768]{1,0:T(8,128)(2,1)} %dynamic-slice_bitcast_fusion.refs_1_, bf16[288,768]{1,0:T(8,128)(2,1)} %copy-done.19, bf16[288,768]{1,0:T(8,128)(2,1)} %copy-done.20, ...), custom_call_target="tpu_custom_call" | custom-call | flops 1048576 | bytes 65536 | tf_op jit(solution)/shard_map/sort_qkv/pallas_call | solution.py:85
  40.0 16.1 %attention_forward.1 = (f32[1152,768]{1,0:T(8,128)}, f32[1152,768]{1,0:T(8,128)}, bf16[1152,768]{1,0:T(8,128)(2,1)}) custom-call(s32[6]{0:T(128)} %convert_reduce_fusion.1.starts, bf16[3,1152,768]{2,1,0:T(8,128)(2,1)} %get-tuple-element.105.qkv), custom_call_target="tpu_custom_call" | custom-call | flops 1048576 | bytes 65536 | tf_op jit(solution)/shard_map/attention_forward/pallas_call | solution.py:166
  56.1 9.7 %middle.1 = (bf16[1152,768]{1,0:T(8,128)(2,1)}, f32[1152,768]{1,0:T(8,128)}, bf16[1152,768]{1,0:T(8,128)(2,1)}, bf16[1152,768]{1,0:T(8,128)(2,1)}, f32[8,768]{1,0:T(8,128)}) custom-call(f32[2]{0:T(128)} %fusion.6.refs_0_.keep, s32[1,1152]{1,0:T(1,128)} %broadcast_in_dim.31.refs_0_.refs_1_, bf16[288,768]{1,0:T(8,128)(2,1)} %get-tuple-element.209.refs_2_, ...), custom_call_target="tpu_custom_call" | custom-call | flops 1048576 | bytes 65536 | tf_op jit(solution)/shard_map/middle/pallas_call | solution.py:319
  65.8 58.8 %mlp.1 = (bf16[768,1536]{1,0:T(8,128)(2,1)}, bf16[768,1536]{1,0:T(8,128)(2,1)}, bf16[2048,768]{1,0:T(8,128)(2,1)}, bf16[2048,768]{1,0:T(8,128)(2,1)}, f32[1,3072...) custom-call(s32[1]{0:T(128)} %bitcast.core.c, ...), custom_call_target="tpu_custom_call" | custom-call | flops 1048576 | bytes 65536 | tf_op jit(solution)/shard_map/mlp/pallas_call | solution.py:422
  127.1 6.0 %unsort.2 = bf16[4,288,768]{2,1,0:T(8,128)(2,1)} custom-call(s32[1]{0:T(128)} %bitcast.10.me, s32[1152,1]{1,0:T(8,128)} %broadcast_in_dim.37.rank, bf16[1152,768]{1,0:T(8,128)(2,1)} %get-tuple-element.120.source), custom_call_target="tpu_custom_call" | custom-call | flops 1048576 | bytes 65536 | tf_op jit(solution)/shard_map/unsort/pallas_call | solution.py:502
  135.0 5.3 %add_convert_fusion = (bf16[1024,768]{1,0:T(8,128)(2,1)}, bf16[1024,768]{1,0:T(8,128)(2,1)}) fusion(bf16[2048,768]{1,0:T(8,128)(2,1)} %collective-permute-done.10, s32[]{:T(128)S(6)} %select_n.384, bf16[2048,768]{1,0:T(8,128)(2,1)} %get-tuple-element.119, s32[]{:T(128)S(6)} %select_n.382), kind=kLoop, calls=%fused_computation.1 | loop fusion | flops 6291456 | bytes 9437192 | tf_op jit(solution)/shard_map/convert_element_type | solution.py:998
  141.9 3.6 all-to-all-start
  145.4 4.3 %add_convert_fusion.2 = (bf16[384,1536]{1,0:T(8,128)(2,1)}, bf16[384,1536]{1,0:T(8,128)(2,1)}) fusion(bf16[768,1536]{1,0:T(8,128)(2,1)} %collective-permute-done.9, s32[]{:T(128)S(6)} %select_n.383, bf16[768,1536]{1,0:T(8,128)(2,1)} %get-tuple-element.112, s32[]{:T(128)S(6)} %select_n.377), kind=kLoop, calls=%fused_computation.3 | loop fusion | flops 4718592 | bytes 7077896 | tf_op jit(solution)/shard_map/convert_element_type | solution.py:998
  151.5 32.3 %attention_backward.1 = (bf16[3,1152,768]{2,1,0:T(8,128)(2,1)}, f32[8,768]{1,0:T(8,128)}) custom-call(s32[6]{0:T(128)} %convert_reduce_fusion.1.starts, bf16[3,1152,768]{2,1,0:T(8,128)(2,1)} %get-tuple-element.105.qkv, bf16[1152,768]{1,0:T(8,128)(2,1)} %get-tuple-element.124.grad, f32[1152,768]{1,0:T(8,128)} %get-tuple-element.125.att, ...), custom_call_target="tpu_custom_call" | custom-call | flops 1048576 | bytes 65536 | tf_op jit(solution)/shard_map/attention_backward/pallas_call | solution.py:252
  183.8 4.0 %add_convert_fusion.6 = (bf16[512,768]{1,0:T(8,128)(2,1)}, bf16[512,768]{1,0:T(8,128)(2,1)}) fusion(bf16[1024,768]{1,0:T(8,128)(2,1)} %collective-permute-done.12, s32[]{:T(128)S(6)} %select_n.389, bf16[1024,768]{1,0:T(8,128)(2,1)} %get-tuple-element.195, s32[]{:T(128)S(6)} %select_n.388), kind=kLoop, calls=%fused_computation.8 | loop fusion | flops 3145728 | bytes 4718600 | tf_op jit(solution)/shard_map/convert_element_type | solution.py:998
  192.6 9.8 %input_weights.1 = (bf16[384,2432]{1,0:T(8,128)(2,1)}, bf16[384,2432]{1,0:T(8,128)(2,1)}) custom-call(s32[1]{0:T(128)} %bitcast.core.c, bf16[1152,768]{1,0:T(8,128)(2,1)} %get-tuple-element.132.normed, bf16[3,1152,768]{2,1,0:T(8,128)(2,1)} %get-tuple-element.127.grads, f32[8,768]{1,0:T(8,128)} %get-tuple-element.133.first, ...), custom_call_target="tpu_custom_call" | custom-call | flops 1048576 | bytes 65536 | tf_op jit(solution)/shard_map/input_weights/pallas_call | solution.py:543
  202.4 3.0 collective-permute-done.13
  211.0 10.6 %input_backward.1 = (bf16[1152,768]{1,0:T(8,128)(2,1)}, f32[8,768]{1,0:T(8,128)}) custom-call(bf16[3,1152,768]{2,1,0:T(8,128)(2,1)} %get-tuple-element.127.grads, bf16[768,2304]{1,0:T(8,128)(2,1)} %weight.1, bf16[1152,768]{1,0:T(8,128)(2,1)} %get-tuple-element.107.refs_7_.xs, f32[1152,768]{1,0:T(8,128)} %get-tuple-element.143.middle_grad, ...), custom_call_target="tpu_custom_call" | custom-call | flops 1048576 | bytes 65536 | tf_op jit(solution)/shard_map/input_backward/pallas_call | solution.py:475
  223.1 3.4 add_convert_fusion.5
  228.7 3.2 collective-permute-start.20
  237.9 6.0 %unsort.3 = bf16[4,288,768]{2,1,0:T(8,128)(2,1)} custom-call(s32[1]{0:T(128)} %bitcast.10.me, s32[1152,1]{1,0:T(8,128)} %broadcast_in_dim.37.rank, bf16[1152,768]{1,0:T(8,128)(2,1)} %get-tuple-element.150.source), custom_call_target="tpu_custom_call" | custom-call | flops 1048576 | bytes 65536 | tf_op jit(solution)/shard_map/unsort/pallas_call | solution.py:502
  243.9 8.1 %collective-permute-done.19 = bf16[48,1536]{1,0:T(8,128)(2,1)S(1)} collective-permute-done((bf16[48,1536]{1,0:T(8,128)(2,1)S(1)}, bf16[48,1536]{1,0:T(8,128)(2,1)S(1)}, u32[]{:S(2)}, u32[]{:S(2)}) %collective-permute-start.19) | collective-permute-done | bytes 147488 | tf_op jit(solution)/shard_map/ppermute | solution.py:1009
  256.2 3.6 all-to-all-start.2
  259.9 3.0 collective-permute-start.22
  263.5 7.8 %collective-permute-done.22 = bf16[48,1536]{1,0:T(8,128)(2,1)S(1)} collective-permute-done((bf16[48,1536]{1,0:T(8,128)(2,1)S(1)}, bf16[48,1536]{1,0:T(8,128)(2,1)S(1)}, u32[]{:S(2)}, u32[]{:S(2)}) %collective-permute-start.22) | collective-permute-done | bytes 147488 | tf_op jit(solution)/shard_map/ppermute | solution.py:1009
  276.5 11.8 %collective-permute-done.24 = bf16[48,2432]{1,0:T(8,128)(2,1)S(1)} collective-permute-done((bf16[48,2432]{1,0:T(8,128)(2,1)S(1)}, bf16[48,2432]{1,0:T(8,128)(2,1)S(1)}, u32[]{:S(2)}, u32[]{:S(2)}) %collective-permute-start.24) | collective-permute-done | bytes 233504 | tf_op jit(solution)/shard_map/ppermute | solution.py:1009
  292.4 3.3 collective-permute-start.27
  295.7 3.3 collective-permute-done.27
  299.0 8.2 %collective-permute-done.28 = bf16[192,1536]{1,0:T(8,128)(2,1)} collective-permute-done((bf16[192,1536]{1,0:T(8,128)(2,1)S(1)}, bf16[192,1536]{1,0:T(8,128)(2,1)}, u32[]{:S(2)}, u32[]{:S(2)}) %collective-permute-start.28) | collective-permute-done | bytes 589856 | tf_op jit(solution)/shard_map/ppermute | solution.py:1009
  316.0 3.6 copy.36
  319.7 3.6 copy.37
  323.3 16.4 %collective-permute-done.30 = bf16[24,2432]{1,0:T(8,128)(2,1)S(1)} collective-permute-done((bf16[24,2432]{1,0:T(8,128)(2,1)S(1)}, bf16[24,2432]{1,0:T(8,128)(2,1)S(1)}, u32[]{:S(2)}, u32[]{:S(2)}) %collective-permute-start.30) | collective-permute-done | bytes 116768 | tf_op jit(solution)/shard_map/ppermute | solution.py:1009
  346.9 3.8 collective-permute-done.33
  353.7 7.0 %up_final.1 = f32[768,3072]{1,0:T(8,128)} custom-call(s32[1]{0:T(128)} %bitcast.core.c, s32[2]{0:T(128)} %pad_add_fusion.1.t, bf16[384,1536]{1,0:T(8,128)(2,1)} %pad_maximum_fusion.1.refs_0_, bf16[384,1536]{1,0:T(8,128)(2,1)} %collective-permute-done.31.refs_1_, bf16[384,1536]{1,0:T(8,128)(2,1)} %copy-done.10, bf16[384,1536]{1,0:T(8,128)(2,1)} %copy-done.11), custom_call_target="tpu_custom_call" | custom-call | flops 1048576 | bytes 65536 | tf_op jit(solution)/shard_map/up_final/pallas_call | solution.py:592
  362.6 10.5 %down_final.1 = (f32[3072,768]{1,0:T(8,128)}, f32[768,768]{1,0:T(8,128)}) custom-call(s32[1]{0:T(128)} %bitcast.core.c, s32[2]{0:T(128)} %pad_add_fusion.t, bf16[1024,768]{1,0:T(8,128)(2,1)} %copy-done.2, bf16[1024,768]{1,0:T(8,128)(2,1)} %collective-permute-done.32.refs_1_, bf16[1024,768]{1,0:T(8,128)(2,1)} %collective-permute-done.36.refs_2_, ...), custom_call_target="tpu_custom_call" | custom-call | flops 1048576 | bytes 65536 | tf_op jit(solution)/shard_map/down_final/pallas_call | solution.py:592
  377.0 6.3 %input_final.1 = (f32[768,2304]{1,0:T(8,128)}, f32[128,768]{1,0:T(8,128)}) custom-call(s32[1]{0:T(128)} %bitcast.core.c, s32[2]{0:T(128)} %pad_add_fusion.t, bf16[192,2432]{1,0:T(8,128)(2,1)} %copy-done.4, bf16[192,2432]{1,0:T(8,128)(2,1)} %copy-done.14, bf16[192,2432]{1,0:T(8,128)(2,1)} %collective-permute-done.40.refs_2_, ...), custom_call_target="tpu_custom_call" | custom-call | flops 1048576 | bytes 65536 | tf_op jit(solution)/shard_map/input_final/pallas_call | solution.py:592
  (207 shorter events, 92.5 us)
Async XLA Ops:
  3.2 16.9 %collective-permute-start.6 = (bf16[288,768]{1,0:T(8,128)(2,1)}, bf16[288,768]{1,0:T(8,128)(2,1)S(1)}, u32[]{:S(2)}, u32[]{:S(2)}) collective-permute-start(bf16[288,768]{1,0:T(8,128)(2,1)} %get-tuple-element.213), channel_id=1, source_target_pairs={{0,1},{1,0},{2,3},{3,2},{4,5},{5,4},{6,7},{7,6},{8,9},{9,8},{10,11... | collective-permute-start | bytes 1327112 | tf_op jit(solution)/shard_map/ppermute | solution.py:978
  3.6 18.6 %collective-permute-start.7 = (bf16[288,768]{1,0:T(8,128)(2,1)}, bf16[288,768]{1,0:T(8,128)(2,1)S(1)}, u32[]{:S(2)}, u32[]{:S(2)}) collective-permute-start(bf16[288,768]{1,0:T(8,128)(2,1)} %get-tuple-element.212), channel_id=1, source_target_pairs={{0,2},{1,3},{2,0},{3,1},{4,6},{5,7},{6,4},{7,5},{8,10},{9,11},{10,... | collective-permute-start | bytes 1327112 | tf_op jit(solution)/shard_map/ppermute | solution.py:978
  14.4 12.1 %collective-permute-start.8 = (bf16[288,768]{1,0:T(8,128)(2,1)}, bf16[288,768]{1,0:T(8,128)(2,1)S(1)}, u32[]{:S(2)}, u32[]{:S(2)}) collective-permute-start(bf16[288,768]{1,0:T(8,128)(2,1)} %get-tuple-element.211), channel_id=1, source_target_pairs={{0,3},{1,2},{2,1},{3,0},{4,7},{5,6},{6,5},{7,4},{8,11},{9,10},{10,... | collective-permute-start | bytes 1327112 | tf_op jit(solution)/shard_map/ppermute | solution.py:978
  17.3 38.8 %collective-permute-start.5 = (bf16[288,768]{1,0:T(8,128)(2,1)}, bf16[288,768]{1,0:T(8,128)(2,1)}, u32[]{:S(2)}, u32[]{:S(2)}) collective-permute-start(bf16[288,768]{1,0:T(8,128)(2,1)} %get-tuple-element.103), channel_id=1, source_target_pairs={{0,3},{1,2},{2,1},{3,0},{4,7},{5,6},{6,5},{7,4},{8,11},{9,10},{10,... | collective-permute-start | bytes 1327112 | tf_op jit(solution)/shard_map/ppermute | solution.py:978
  18.3 37.8 %collective-permute-start.4 = (bf16[288,768]{1,0:T(8,128)(2,1)}, bf16[288,768]{1,0:T(8,128)(2,1)}, u32[]{:S(2)}, u32[]{:S(2)}) collective-permute-start(bf16[288,768]{1,0:T(8,128)(2,1)} %get-tuple-element.102), channel_id=1, source_target_pairs={{0,2},{1,3},{2,0},{3,1},{4,6},{5,7},{6,4},{7,5},{8,10},{9,11},{10,... | collective-permute-start | bytes 1327112 | tf_op jit(solution)/shard_map/ppermute | solution.py:978
  20.1 36.0 %collective-permute-start.3 = (bf16[288,768]{1,0:T(8,128)(2,1)S(1)}, bf16[288,768]{1,0:T(8,128)(2,1)}, u32[]{:S(2)}, u32[]{:S(2)}) collective-permute-start(bf16[288,768]{1,0:T(8,128)(2,1)S(1)} %get-tuple-element.101), channel_id=1, source_target_pairs={{0,1},{1,0},{2,3},{3,2},{4,5},{5,4},{6,7},{7,6},{8,9},{9,8},{10,11... | collective-permute-start | bytes 1327112 | tf_op jit(solution)/shard_map/ppermute | solution.py:978
  140.3 43.5 %collective-permute-start.12 = (bf16[1024,768]{1,0:T(8,128)(2,1)}, bf16[1024,768]{1,0:T(8,128)(2,1)}, u32[]{:S(2)}, u32[]{:S(2)}) collective-permute-start(bf16[1024,768]{1,0:T(8,128)(2,1)} %get-tuple-element.196), channel_id=1, source_target_pairs={{0,4},{1,3},{2,6},{3,1},{4,0},{5,7},{6,2},{7,5},{8,12},{9,11},{10,... | collective-permute-start | bytes 4718600 | tf_op jit(solution)/shard_map/ppermute | solution.py:1009
  141.9 41.9 %all-to-all-start = ((bf16[4,288,768]{2,1,0:T(8,128)(2,1)}), bf16[4,288,768]{2,1,0:T(8,128)(2,1)S(1)}, u32[]{:S(2)}, u32[]{:S(2)}) async-start(bf16[4,288,768]{2,1,0:T(8,128)(2,1)} %unsort.2), calls=%async_computation | async-start | bytes 3538944 | tf_op jit(solution)/shard_map/all_to_all | solution.py:1089
  149.8 34.0 %collective-permute-start.11 = (bf16[384,1536]{1,0:T(8,128)(2,1)}, bf16[384,1536]{1,0:T(8,128)(2,1)}, u32[]{:S(2)}, u32[]{:S(2)}) collective-permute-start(bf16[384,1536]{1,0:T(8,128)(2,1)} %get-tuple-element.198), channel_id=1, source_target_pairs={{0,8},{1,9},{2,10},{3,11},{4,12},{5,13},{6,14},{7,15},{8,0},{9,1},... | collective-permute-start | bytes 3538952 | tf_op jit(solution)/shard_map/ppermute | solution.py:1009
  187.9 18.7 %collective-permute-start.14 = (bf16[512,768]{1,0:T(8,128)(2,1)}, bf16[512,768]{1,0:T(8,128)(2,1)}, u32[]{:S(2)}, u32[]{:S(2)}) collective-permute-start(bf16[512,768]{1,0:T(8,128)(2,1)} %get-tuple-element.202), channel_id=1, source_target_pairs={{0,2},{1,5},{2,0},{3,7},{4,6},{5,1},{6,4},{7,3},{8,10},{9,13},{10,... | collective-permute-start | bytes 2359304 | tf_op jit(solution)/shard_map/ppermute | solution.py:1009
  192.3 13.2 %collective-permute-start.13 = (bf16[192,1536]{1,0:T(8,128)(2,1)}, bf16[192,1536]{1,0:T(8,128)(2,1)S(1)}, u32[]{:S(2)}, u32[]{:S(2)}) collective-permute-start(bf16[192,1536]{1,0:T(8,128)(2,1)} %get-tuple-element.204), channel_id=1, source_target_pairs={{0,4},{1,3},{2,6},{3,1},{4,0},{5,7},{6,2},{7,5},{8,12},{9,11},{10,... | collective-permute-start | bytes 1769480 | tf_op jit(solution)/shard_map/ppermute | solution.py:1009
  206.5 15.9 %collective-permute-start.15 = (bf16[384,2432]{1,0:T(8,128)(2,1)}, bf16[384,2432]{1,0:T(8,128)(2,1)}, u32[]{:S(2)}, u32[]{:S(2)}) collective-permute-start(bf16[384,2432]{1,0:T(8,128)(2,1)} %get-tuple-element.139), channel_id=1, source_target_pairs={{0,1},{1,0},{2,3},{3,2},{4,5},{5,4},{6,7},{7,6},{8,9},{9,8},{10,11... | collective-permute-start | bytes 5603336 | tf_op jit(solution)/shard_map/ppermute | solution.py:978
  208.7 13.7 %collective-permute-start.17 = (bf16[256,768]{1,0:T(8,128)(2,1)}, bf16[256,768]{1,0:T(8,128)(2,1)}, u32[]{:S(2)}, u32[]{:S(2)}) collective-permute-start(bf16[256,768]{1,0:T(8,128)(2,1)} %get-tuple-element.215), channel_id=1, source_target_pairs={{0,8},{1,9},{2,10},{3,11},{4,12},{5,13},{6,14},{7,15},{8,0},{9,1},... | collective-permute-start | bytes 1179656 | tf_op jit(solution)/shard_map/ppermute | solution.py:1009
  209.1 13.3 %collective-permute-start.16 = (bf16[96,1536]{1,0:T(8,128)(2,1)S(1)}, bf16[96,1536]{1,0:T(8,128)(2,1)S(1)}, u32[]{:S(2)}, u32[]{:S(2)}) collective-permute-start(bf16[96,1536]{1,0:T(8,128)(2,1)S(1)} %get-tuple-element.217), channel_id=1, source_target_pairs={{0,2},{1,5},{2,0},{3,7},{4,6},{5,1},{6,4},{7,3},{8,10},{9,13},{10,... | collective-permute-start | bytes 884744 | tf_op jit(solution)/shard_map/ppermute | solution.py:1009
  226.5 26.1 %collective-permute-start.18 = (bf16[192,2432]{1,0:T(8,128)(2,1)}, bf16[192,2432]{1,0:T(8,128)(2,1)}, u32[]{:S(2)}, u32[]{:S(2)}) collective-permute-start(bf16[192,2432]{1,0:T(8,128)(2,1)} %get-tuple-element.200), channel_id=1, source_target_pairs={{0,4},{1,3},{2,6},{3,1},{4,0},{5,7},{6,2},{7,5},{8,12},{9,11},{10,... | collective-permute-start | bytes 2801672 | tf_op jit(solution)/shard_map/ppermute | solution.py:1009
  228.7 23.3 %collective-permute-start.20 = (bf16[128,768]{1,0:T(8,128)(2,1)}, bf16[128,768]{1,0:T(8,128)(2,1)S(1)}, u32[]{:S(2)}, u32[]{:S(2)}) collective-permute-start(bf16[128,768]{1,0:T(8,128)(2,1)} %get-tuple-element.221), channel_id=1, source_target_pairs={{0,16},{1,17},{2,18},{3,19},{4,20},{5,21},{6,22},{7,23},{8,24},{9,... | collective-permute-start | bytes 589832 | tf_op jit(solution)/shard_map/ppermute | solution.py:1009
  231.9 20.0 %all-to-all-start.1 = ((f32[32,2,768]{2,1,0:T(2,128)}), f32[32,2,768]{2,1,0:T(2,128)S(1)}, u32[]{:S(2)}, u32[]{:S(2)}) async-start(f32[32,2,768]{2,1,0:T(2,128)} %broadcast_in_dim.36), calls=%async_computation.1 | async-start | bytes 393216 | tf_op jit(solution)/shard_map/all_to_all | solution.py:1077
  235.2 16.7 %collective-permute-start.19 = (bf16[48,1536]{1,0:T(8,128)(2,1)S(1)}, bf16[48,1536]{1,0:T(8,128)(2,1)S(1)}, u32[]{:S(2)}, u32[]{:S(2)}) collective-permute-start(bf16[48,1536]{1,0:T(8,128)(2,1)S(1)} %get-tuple-element.223), channel_id=1, source_target_pairs={{0,16},{1,17},{2,18},{3,19},{4,20},{5,21},{6,22},{7,23},{8,24},{9,... | collective-permute-start | bytes 442376 | tf_op jit(solution)/shard_map/ppermute | solution.py:1009
  253.6 17.6 %collective-permute-start.23 = (bf16[128,768]{1,0:T(8,128)(2,1)S(1)}, bf16[128,768]{1,0:T(8,128)(2,1)}, u32[]{:S(2)}, u32[]{:S(2)}) collective-permute-start(bf16[128,768]{1,0:T(8,128)(2,1)S(1)} %add_convert_fusion.18), channel_id=1, source_target_pairs={{0,16},{1,17},{2,18},{3,19},{4,20},{5,21},{6,22},{7,23},{8,24},{9,... | collective-permute-start | bytes 589832 | tf_op jit(solution)/shard_map/ppermute | solution.py:1009
  255.9 15.4 %collective-permute-start.21 = (bf16[96,2432]{1,0:T(8,128)(2,1)}, bf16[96,2432]{1,0:T(8,128)(2,1)}, u32[]{:S(2)}, u32[]{:S(2)}) collective-permute-start(bf16[96,2432]{1,0:T(8,128)(2,1)} %get-tuple-element.206), channel_id=1, source_target_pairs={{0,2},{1,5},{2,0},{3,7},{4,6},{5,1},{6,4},{7,3},{8,10},{9,13},{10,... | collective-permute-start | bytes 1400840 | tf_op jit(solution)/shard_map/ppermute | solution.py:1009
  256.2 32.1 %all-to-all-start.2 = ((bf16[4,288,768]{2,1,0:T(8,128)(2,1)}), bf16[4,288,768]{2,1,0:T(8,128)(2,1)S(1)}, u32[]{:S(2)}, u32[]{:S(2)}) async-start(bf16[4,288,768]{2,1,0:T(8,128)(2,1)} %unsort.3), calls=%async_computation.2 | async-start | bytes 3538944 | tf_op jit(solution)/shard_map/all_to_all | solution.py:1089
  272.3 16.1 %collective-permute-start.26 = (bf16[256,768]{1,0:T(8,128)(2,1)S(1)}, bf16[256,768]{1,0:T(8,128)(2,1)}, u32[]{:S(2)}, u32[]{:S(2)}) collective-permute-start(bf16[256,768]{1,0:T(8,128)(2,1)S(1)} %pad_maximum_fusion.6), channel_id=1, source_target_pairs={{0,8},{1,9},{2,10},{3,11},{4,12},{5,13},{6,14},{7,15},{8,0},{9,1},... | collective-permute-start | bytes 1179656 | tf_op jit(solution)/shard_map/ppermute | solution.py:1009
  272.4 16.0 %collective-permute-start.25 = (bf16[96,1536]{1,0:T(8,128)(2,1)S(1)}, bf16[96,1536]{1,0:T(8,128)(2,1)S(1)}, u32[]{:S(2)}, u32[]{:S(2)}) collective-permute-start(bf16[96,1536]{1,0:T(8,128)(2,1)S(1)} %pad_maximum_fusion.7), channel_id=1, source_target_pairs={{0,2},{1,5},{2,0},{3,7},{4,6},{5,1},{6,4},{7,3},{8,10},{9,13},{10,... | collective-permute-start | bytes 884744 | tf_op jit(solution)/shard_map/ppermute | solution.py:1009
  274.5 13.9 %collective-permute-start.24 = (bf16[48,2432]{1,0:T(8,128)(2,1)S(1)}, bf16[48,2432]{1,0:T(8,128)(2,1)S(1)}, u32[]{:S(2)}, u32[]{:S(2)}) collective-permute-start(bf16[48,2432]{1,0:T(8,128)(2,1)S(1)} %get-tuple-element.219), channel_id=1, source_target_pairs={{0,8},{1,9},{2,10},{3,11},{4,12},{5,13},{6,14},{7,15},{8,0},{9,1},... | collective-permute-start | bytes 700424 | tf_op jit(solution)/shard_map/ppermute | solution.py:1009
  290.6 17.1 %collective-permute-start.29 = (bf16[512,768]{1,0:T(8,128)(2,1)S(1)}, bf16[512,768]{1,0:T(8,128)(2,1)}, u32[]{:S(2)}, u32[]{:S(2)}) collective-permute-start(bf16[512,768]{1,0:T(8,128)(2,1)S(1)} %pad_maximum_fusion.3), channel_id=1, source_target_pairs={{0,2},{1,5},{2,0},{3,7},{4,6},{5,1},{6,4},{7,3},{8,10},{9,13},{10,... | collective-permute-start | bytes 2359304 | tf_op jit(solution)/shard_map/ppermute | solution.py:1009
  291.2 16.1 %collective-permute-start.28 = (bf16[192,1536]{1,0:T(8,128)(2,1)S(1)}, bf16[192,1536]{1,0:T(8,128)(2,1)}, u32[]{:S(2)}, u32[]{:S(2)}) collective-permute-start(bf16[192,1536]{1,0:T(8,128)(2,1)S(1)} %pad_maximum_fusion.4), channel_id=1, source_target_pairs={{0,4},{1,3},{2,6},{3,1},{4,0},{5,7},{6,2},{7,5},{8,12},{9,11},{10,... | collective-permute-start | bytes 1769480 | tf_op jit(solution)/shard_map/ppermute | solution.py:1009
  309.3 32.7 %collective-permute-start.32 = (bf16[1024,768]{1,0:T(8,128)(2,1)S(1)}, bf16[1024,768]{1,0:T(8,128)(2,1)}, u32[]{:S(2)}, u32[]{:S(2)}) collective-permute-start(bf16[1024,768]{1,0:T(8,128)(2,1)S(1)} %pad_maximum_fusion.refs_0_), channel_id=1, source_target_pairs={{0,4},{1,3},{2,6},{3,1},{4,0},{5,7},{6,2},{7,5},{8,12},{9,11},{10,... | collective-permute-start | bytes 4718600 | tf_op jit(solution)/shard_map/ppermute | solution.py:1009
  312.9 29.0 %collective-permute-start.31 = (bf16[384,1536]{1,0:T(8,128)(2,1)}, bf16[384,1536]{1,0:T(8,128)(2,1)}, u32[]{:S(2)}, u32[]{:S(2)}) collective-permute-start(bf16[384,1536]{1,0:T(8,128)(2,1)} %pad_maximum_fusion.1.refs_0_), channel_id=1, source_target_pairs={{0,8},{1,9},{2,10},{3,11},{4,12},{5,13},{6,14},{7,15},{8,0},{9,1},... | collective-permute-start | bytes 3538952 | tf_op jit(solution)/shard_map/ppermute | solution.py:1009
  313.6 26.1 %collective-permute-start.30 = (bf16[24,2432]{1,0:T(8,128)(2,1)S(1)}, bf16[24,2432]{1,0:T(8,128)(2,1)S(1)}, u32[]{:S(2)}, u32[]{:S(2)}) collective-permute-start(bf16[24,2432]{1,0:T(8,128)(2,1)S(1)} %add_convert_fusion.24), channel_id=1, source_target_pairs={{0,16},{1,17},{2,18},{3,19},{4,20},{5,21},{6,22},{7,23},{8,24},{9,... | collective-permute-start | bytes 350216 | tf_op jit(solution)/shard_map/ppermute | solution.py:1009
  316.0 30.9 %collective-permute-start.36 = (bf16[1024,768]{1,0:T(8,128)(2,1)S(1)}, bf16[1024,768]{1,0:T(8,128)(2,1)}, u32[]{:S(2)}, u32[]{:S(2)}) collective-permute-start(bf16[1024,768]{1,0:T(8,128)(2,1)S(1)} %pad_maximum_fusion.refs_0_), channel_id=1, source_target_pairs={{0,1},{1,0},{2,3},{3,2},{4,5},{5,4},{6,7},{7,6},{8,9},{9,8},{10,11... | collective-permute-start | bytes 4718600 | tf_op jit(solution)/shard_map/ppermute | solution.py:978
  360.7 13.6 %collective-permute-start.39 = (bf16[192,2432]{1,0:T(8,128)(2,1)S(1)}, bf16[192,2432]{1,0:T(8,128)(2,1)S(1)}, u32[]{:S(2)}, u32[]{:S(2)}) collective-permute-start(bf16[192,2432]{1,0:T(8,128)(2,1)S(1)} %pad_maximum_fusion.2.refs_0_), channel_id=1, source_target_pairs={{0,4},{1,3},{2,6},{3,1},{4,0},{5,7},{6,2},{7,5},{8,12},{9,11},{10,... | collective-permute-start | bytes 2801672 | tf_op jit(solution)/shard_map/ppermute | solution.py:1009
  362.6 11.7 %collective-permute-start.40 = (bf16[192,2432]{1,0:T(8,128)(2,1)S(1)}, bf16[192,2432]{1,0:T(8,128)(2,1)}, u32[]{:S(2)}, u32[]{:S(2)}) collective-permute-start(bf16[192,2432]{1,0:T(8,128)(2,1)S(1)} %pad_maximum_fusion.2.refs_0_), channel_id=1, source_target_pairs={{0,1},{1,0},{2,3},{3,2},{4,5},{5,4},{6,7},{7,6},{8,9},{9,8},{10,11... | collective-permute-start | bytes 2801672 | tf_op jit(solution)/shard_map/ppermute | solution.py:978
  (53 other events, 331.7 us)
